TPU v7x, 512 devices: a whole 4x4x16 slice. The times are simulated.
512 devices in a mesh: dp: 32 (over z_lo, x, core), fsdp: 16 (over z_hi, y).
Axes of the slice: x: 4, y: 4, z: 16 (z_hi: 4, z_lo: 4; z = z_hi * 4 + z_lo), core: 2. Of those that a mesh axis runs over, the one named last changes fastest.
Arguments:
- grad_partials: bfloat16 [32, 16, 2, 64, 5120], P('dp', 'fsdp'), may hold values from -5 to 5
- momentum: float32 [32, 2, 64, 5120], P('dp', None, 'fsdp'), may hold values from -6 to 6
- params: float32 [2, 64, 5120], P(None, 'fsdp'), may hold values from -6 to 6
- kept: int32 [8], replicated, may hold values from 0 to 63, as said below
Outputs:
- new_params: float32 [2, 64, 5120], P(None, 'fsdp')
- new_momentum: float32 [32, 2, 64, 5120], P('dp', None, 'fsdp')
Inputs may be any that keep to these rules, and one draw needn't show every extreme that they name: `kept`: 8 distinct coefficient indices.
All inputs are finite; a program needn't handle non-finite values.
Results may differ from a plain program's by a relative error of at most 0.0003.
Values sent between devices are 32-bit elements; how exact they have to be, the bound alone decides.
No kernel may reach another device: no remote copies, remote signals or barrier semaphores. Data moves between devices by JAX's collectives and lax.ppermute only.
A program may use at most 64 MiB of HBM per device.

v0:
```python
import jax
import jax.numpy as jnp
from jax import lax
from jax.sharding import PartitionSpec as P

SPAN = 64
KEEP = 8
ROW_VALS = 5120


def dct_table():
    k = lax.broadcasted_iota(jnp.float32, (SPAN, SPAN), 0)
    n = lax.broadcasted_iota(jnp.float32, (SPAN, SPAN), 1)
    scale = jnp.where(k == 0, jnp.sqrt(1.0 / SPAN), jnp.sqrt(2.0 / SPAN))
    return scale * jnp.cos(jnp.pi * (2.0 * n + 1.0) * k / (2.0 * SPAN))


def shards(grad_partials, momentum, params, kept):
    blocks = ROW_VALS // SPAN
    table = dct_table()
    onehot = (kept[:, None] == jnp.arange(SPAN, dtype=jnp.int32)[None, :]).astype(jnp.float32)
    picked = jnp.dot(onehot, table, precision=lax.Precision.HIGHEST)
    terms = grad_partials[0, 0].astype(jnp.float32)
    grad = lax.psum_scatter(terms, "fsdp", scatter_dimension=1, tiled=True)
    moment = 0.9 * momentum[0] + grad
    layer_count = moment.shape[0]
    row_count = moment.shape[1]
    spans = moment.reshape(layer_count, row_count, blocks, SPAN)
    spectra = jnp.einsum("lrcn,kn->lrck", spans, table, precision=lax.Precision.HIGHEST)
    coeffs = jnp.take(spectra, kept, axis=3)
    local = jnp.einsum("lrcj,jn->lrcn", coeffs, picked, precision=lax.Precision.HIGHEST)
    new_momentum = (moment - local.reshape(moment.shape))[None]
    flat_coeffs = coeffs.reshape(layer_count, row_count, blocks * KEEP)
    replicas = lax.axis_size("dp")
    total = jnp.sum(lax.all_gather(flat_coeffs[None], "dp", axis=0, tiled=True), axis=0)
    shared = (total / replicas).reshape(layer_count, row_count, blocks, KEEP)
    update = jnp.einsum("lrcj,jn->lrcn", shared, picked, precision=lax.Precision.HIGHEST)
    new_params = params - update.reshape(params.shape)
    return (new_params, new_momentum)


def solution(mesh):
    placed = (
        P("dp", "fsdp", None, None, None),
        P("dp", None, "fsdp", None),
        P(None, "fsdp", None),
        P(),
    )
    return jax.shard_map(
        shards,
        mesh=mesh,
        in_specs=placed,
        out_specs=(P(None, "fsdp", None), P("dp", None, "fsdp", None)),
        check_vma=False,
    )
```

profile of v0, /device:TPU:25, one launch (start us, length us, event | category | flops | bytes accessed | tf_op | source)
XLA Modules:
  0.0 365.6 jit_solution(8465279014468407105)
XLA Ops:
  7.2 0.0 all-reduce.3.cloned.1.call-start
  7.2 3.1 bitcast_convert_fusion
  10.4 0.0 all-reduce.3.cloned.1.call-update
  10.4 0.1 broadcast_in_dim.34
  10.5 1.3 dynamic-slice
  12.5 0.3 convolution_bitcast_fusion
  12.8 290.6 %all-reduce.3.cloned.1.call-done = f32[2,64,5120]{2,1,0:T(8,128)} async-done(((f32[2,64,5120]{2,1,0:T(8,128)}), f32[2,64,5120]{2,1,0:T(8,128)}) %all-reduce.3.cloned.1.call-update) | async-done | bytes 2621456
  303.4 1.0 dynamic-slice_add_fusion
  304.4 0.2 reshape.38
  304.6 1.0 fusion
  305.7 0.2 copy.15
  305.8 0.6 gather_fusion
  306.4 0.1 broadcast_select_fusion
  306.5 0.1 copy.16
  306.7 0.2 gather.7
  306.9 48.7 %all_gather.3 = f32[32,2,4,640]{3,2,1,0:T(4,128)S(1)} all-gather(f32[1,2,4,640]{3,2,1,0:T(4,128)S(1)} %broadcast_select_fusion.1), channel_id=1, replica_groups=mesh['dp'=32,'fsdp'=16] {'dp'}, dimensions={0}, use_global_device_ids=true | all-gather | bytes 675840 | tf_op jit(solution)/shard_map/all_gather | solution.py:35
  355.5 0.1 reduce_sum.9
  355.7 0.2 div.20
  355.9 0.4 fusion.15
  356.3 0.2 reshape.39
  356.5 0.7 fusion.2
  357.2 0.2 reshape.40
  357.3 0.7 subtract_bitcast_fusion
  358.1 0.7 sub.6
  (14 shorter events, 0.1 us)
Async XLA Ops:
  7.2 3.2 copy-start.2
  7.2 296.2 %copy-start = (f32[1,2,4,5120]{3,2,1,0:T(4,128)S(1)}, f32[1,2,4,5120]{3,2,1,0:T(4,128)}, u32[]{:S(2)}) copy-start(f32[1,2,4,5120]{3,2,1,0:T(4,128)} %param.5) | copy-start | bytes 491524
  7.2 296.2 %all-reduce.3.cloned.1.call-start = ((), (), s32[]{:S(2)}) async-start(), calls=%async_computation | async-start | bytes 5242880
  306.4 51.6 %copy-start.1 = (f32[2,4,5120]{2,1,0:T(4,128)S(1)}, f32[2,4,5120]{2,1,0:T(4,128)}, u32[]{:S(2)}) copy-start(f32[2,4,5120]{2,1,0:T(4,128)} %param.6) | copy-start | bytes 491524
Sparse Core Ops, SparseCore 0:
  11.0 292.3 all-reduce.2
where the time goes:
time: 366 us
  waiting for transfers between devices  291 us (80%)
  blocking collectives  48.7 us (13%)
  between operations  14.8 us (4%)
  other arithmetic  5.84 us (2%)
    unnamed x2, waiting for transfers between devices  291 us
    all_gather x1, blocking collectives, shards(): lax.all_gather(flat_coeffs[None], 'dp', axis=0, tiled=True)  48.7 us
  transfers between devices with their start and end apart: 1, of which 1 were waited for; matrix products, arithmetic and copies ran while one was open for 0% of the time, Pallas kernels for 0%

commit v1 on v0

v1 whole, which is shorter than its diff:
```python
import functools

import jax
import jax.numpy as jnp
import numpy as np
from jax import lax
from jax.experimental import pallas as pl
from jax.experimental.pallas import tpu as pltpu
from jax.sharding import PartitionSpec as P

SPAN = 64
KEEP = 8
ROW_VALS = 5120
LAYERS = 2
GROUP = 128 // KEEP
WIDE = GROUP * SPAN
CHUNKS = ROW_VALS // WIDE
COEFFS = ROW_VALS // SPAN * KEEP
OWN = 8
HIGHEST = lax.Precision.HIGHEST
BOTH = ("dp", "fsdp")
N_DP = 32
N_FSDP = 16


def dct_table_t():
    n = np.arange(SPAN)[:, None]
    k = np.arange(SPAN)[None, :]
    turn = ((2 * n + 1) * k) % (4 * SPAN)
    scale = np.where(k == 0, np.sqrt(1.0 / SPAN), np.sqrt(2.0 / SPAN))
    return scale * np.cos(np.pi * turn / (2 * SPAN))


def spread(table, kept_ref, dtype):
    lane = lax.broadcasted_iota(jnp.int32, (SPAN, 128), 1)
    k = lax.broadcasted_iota(jnp.int32, (SPAN, 128), 0)
    which = jnp.zeros((SPAN, 128), jnp.int32)
    for j in range(KEEP):
        which = jnp.where(lane % KEEP == j, kept_ref[j], which)
    onehot = (which == k).astype(jnp.float32)
    if dtype == jnp.bfloat16:
        picked = jnp.dot(table, onehot.astype(dtype), preferred_element_type=jnp.float32)
    else:
        picked = jnp.dot(table, onehot, precision=HIGHEST, preferred_element_type=jnp.float32)
    tall = jnp.concatenate([picked] * GROUP, axis=0)
    row = lax.broadcasted_iota(jnp.int32, (WIDE, 128), 0)
    col = lax.broadcasted_iota(jnp.int32, (WIDE, 128), 1)
    return jnp.where(row // SPAN == col // KEEP, tall, 0.0).astype(dtype)


def prep_kernel(first, place_ref, kept_ref, hi_ref, lo_ref, grad_ref, main_ref, coef_ref):
    y, z, near, far = place_ref[0], place_ref[1], place_ref[2], place_ref[3]
    shape = (2 * 4 * OWN, 2 * 64)
    r = lax.broadcasted_iota(jnp.int32, shape, 0)
    col = lax.broadcasted_iota(jnp.int32, shape, 1)

    def partner(slot):
        return jnp.where(slot == 0, 0, jnp.where(slot == 1, far, jnp.where(slot == 2, near, 2)))

    to_y = y ^ partner(first + r // (4 * OWN))
    to_z = z ^ partner((r // OWN) % 4)
    source = ((r // 4) % 2) * 64 + to_z * 16 + to_y * 4 + r % 4
    order = (source == col).astype(jnp.float32).astype(jnp.bfloat16)
    wide_hi = spread(hi_ref[...], kept_ref, jnp.bfloat16)
    wide_lo = spread(lo_ref[...], kept_ref, jnp.bfloat16)
    for c in range(CHUNKS):
        values = grad_ref[:, :, c * WIDE:(c + 1) * WIDE].reshape(128, WIDE)
        rows = jnp.dot(order, values, preferred_element_type=jnp.float32)
        main_ref[:, :, :, c * WIDE:(c + 1) * WIDE] = rows.reshape(2, 4, OWN, WIDE)
        exact = rows.astype(jnp.bfloat16)
        coef = jnp.dot(exact, wide_hi, preferred_element_type=jnp.float32)
        coef = coef + jnp.dot(exact, wide_lo, preferred_element_type=jnp.float32)
        coef_ref[:, :, :, c * 128:(c + 1) * 128] = coef.reshape(2, 4, OWN, 128)


def prep(first, place, kept, hi, lo, grad):
    smem = pl.BlockSpec(memory_space=pltpu.SMEM)
    vmem = pl.BlockSpec(memory_space=pltpu.VMEM)
    return pl.pallas_call(
        functools.partial(prep_kernel, first),
        out_shape=(
            jax.ShapeDtypeStruct((2, 4, OWN, ROW_VALS), jnp.float32),
            jax.ShapeDtypeStruct((2, 4, OWN, COEFFS), jnp.float32),
        ),
        in_specs=[smem, smem, vmem, vmem, vmem],
        out_specs=(vmem, vmem),
        compiler_params=pltpu.CompilerParams(vmem_limit_bytes=32 * 2**20),
        cost_estimate=pl.CostEstimate(flops=400_000_000, bytes_accessed=3_000_000, transcendentals=0),
        name="prep",
    )(place, kept, hi, lo, grad)


def tall(x):
    return jnp.concatenate([x[:, c * 128:(c + 1) * 128] for c in range(x.shape[1] // 128)], axis=0)


def state_kernel(kept_ref, table_ref, momentum_ref, coef_ref, reject_ref, expand_ref):
    wide = spread(table_ref[...], kept_ref, jnp.float32)
    pair = wide[:128, :]
    row = lax.broadcasted_iota(jnp.int32, (128, 128), 0)
    col = lax.broadcasted_iota(jnp.int32, (128, 128), 1)
    onto = lax.dot_general(pair, pair, (((1,), (1,)), ((), ())), precision=HIGHEST, preferred_element_type=jnp.float32)
    reject_ref[...] = jnp.where(row == col, 1.0, 0.0) - onto
    expand_ref[...] = wide
    state = 0.9 * jnp.concatenate([momentum_ref[0, 0], momentum_ref[0, 1]], axis=0)
    deep = jnp.concatenate([state[:, c * WIDE:(c + 1) * WIDE] for c in range(CHUNKS)], axis=0)
    coef = jnp.dot(deep, wide, precision=HIGHEST, preferred_element_type=jnp.float32)
    for c in range(CHUNKS):
        coef_ref[:, c * 128:(c + 1) * 128] = coef[c * OWN:(c + 1) * OWN]


def state_of(kept, table, momentum):
    smem = pl.BlockSpec(memory_space=pltpu.SMEM)
    vmem = pl.BlockSpec(memory_space=pltpu.VMEM)
    return pl.pallas_call(
        state_kernel,
        out_shape=(
            jax.ShapeDtypeStruct((OWN, COEFFS), jnp.float32),
            jax.ShapeDtypeStruct((128, 128), jnp.float32),
            jax.ShapeDtypeStruct((WIDE, 128), jnp.float32),
        ),
        in_specs=[smem, vmem, vmem],
        out_specs=(vmem, vmem, vmem),
        compiler_params=pltpu.CompilerParams(vmem_limit_bytes=32 * 2**20),
        cost_estimate=pl.CostEstimate(flops=100_000_000, bytes_accessed=1_000_000, transcendentals=0),
        name="state",
    )(kept, table, momentum)


def momentum_kernel(own_ref, got_ref, momentum_ref, reject_ref, out_ref):
    state = jnp.concatenate([momentum_ref[0, 0], momentum_ref[0, 1]], axis=0)
    moment = 0.9 * state + (own_ref[...] + got_ref[...])
    new = jnp.dot(tall(moment), reject_ref[...], precision=HIGHEST, preferred_element_type=jnp.float32)
    for c in range(ROW_VALS // 128):
        part = new[c * OWN:(c + 1) * OWN]
        out_ref[0, 0, :, c * 128:(c + 1) * 128] = part[:4]
        out_ref[0, 1, :, c * 128:(c + 1) * 128] = part[4:]


def new_momentum_of(own, got, momentum, reject):
    vmem = pl.BlockSpec(memory_space=pltpu.VMEM)
    return pl.pallas_call(
        momentum_kernel,
        out_shape=jax.ShapeDtypeStruct(momentum.shape, jnp.float32),
        in_specs=[vmem] * 4,
        out_specs=vmem,
        compiler_params=pltpu.CompilerParams(vmem_limit_bytes=32 * 2**20),
        cost_estimate=pl.CostEstimate(flops=60_000_000, bytes_accessed=700_000, transcendentals=0),
        name="momentum",
    )(own, got, momentum, reject)


def params_kernel(own_ref, got_ref, params_ref, expand_ref, out_ref):
    shared = (own_ref[...] + got_ref[...]) * (1.0 / N_DP)
    deep = tall(shared)
    update = lax.dot_general(
        deep, expand_ref[...], (((1,), (1,)), ((), ())), precision=HIGHEST, preferred_element_type=jnp.float32
    )
    for c in range(CHUNKS):
        lanes = slice(c * WIDE, (c + 1) * WIDE)
        part = update[c * OWN:(c + 1) * OWN]
        out_ref[0, :, lanes] = params_ref[0, :, lanes] - part[:4]
        out_ref[1, :, lanes] = params_ref[1, :, lanes] - part[4:]


def new_params_of(own, got, params, expand):
    vmem = pl.BlockSpec(memory_space=pltpu.VMEM)
    return pl.pallas_call(
        params_kernel,
        out_shape=jax.ShapeDtypeStruct(params.shape, jnp.float32),
        in_specs=[vmem] * 4,
        out_specs=vmem,
        compiler_params=pltpu.CompilerParams(vmem_limit_bytes=32 * 2**20),
        cost_estimate=pl.CostEstimate(flops=60_000_000, bytes_accessed=700_000, transcendentals=0),
        name="params",
    )(own, got, params, expand)


def sum_pairs(step, axis):
    pairs = []
    for d in range(N_DP):
        flip = (1, 3)[(d % 2) ^ step]
        for f in range(N_FSDP):
            to = f ^ (flip if axis == "y" else 4 * flip)
            pairs.append((d * N_FSDP + f, d * N_FSDP + to))
    return pairs


def halve(x, first, step, axis):
    return lax.ppermute(x, BOTH, sum_pairs(step, axis))


def dp_swap(x, flip):
    return lax.ppermute(x, "dp", [(d, d ^ flip) for d in range(N_DP)])


def scatter_z(x):
    got = lax.ppermute(x[2:], BOTH, sum_pairs(0, "z"))
    last = lax.ppermute(x[1] + got[1], BOTH, sum_pairs(1, "z"))
    return x[0] + got[0], last


def scatter_y(sent, kept):
    got = lax.ppermute(sent, BOTH, sum_pairs(0, "y"))
    last = lax.ppermute(kept[1] + got[1], BOTH, sum_pairs(1, "y"))
    return kept[0] + got[0] + last


def shards(grad_partials, momentum, params, kept):
    place = lax.axis_index("fsdp")
    core = lax.axis_index("dp") % 2
    near = 1 + 2 * core
    place = jnp.stack([place % 4, place // 4, near, 4 - near]).astype(jnp.int32)
    exact = dct_table_t()
    table = jnp.asarray(exact.astype(np.float32))
    hi = np.asarray(exact, jnp.bfloat16)
    lo = np.asarray(exact - hi.astype(np.float64), jnp.bfloat16)
    grad = grad_partials[0, 0]

    main_out, coef_out = prep(2, place, kept, hi, lo, grad)
    main_own, coef_own = prep(0, place, kept, hi, lo, grad)
    state_coef, reject, expand = state_of(kept, table, momentum)

    coef = scatter_y(coef_out, coef_own)
    own, got = scatter_z(coef)
    coef = own + got + state_coef
    for flip in (1, 2, 6, 8):
        coef = coef + dp_swap(coef, flip)
    other = dp_swap(coef, 16)
    new_params = new_params_of(coef, other, params, expand)

    main = scatter_y(main_out, main_own)
    own, got = scatter_z(main)
    new_momentum = new_momentum_of(own, got, momentum, reject)
    return (new_params, new_momentum)


def solution(mesh):
    placed = (
        P("dp", "fsdp", None, None, None),
        P("dp", None, "fsdp", None),
        P(None, "fsdp", None),
        P(),
    )
    return jax.shard_map(
        shards,
        mesh=mesh,
        in_specs=placed,
        out_specs=(P(None, "fsdp", None), P("dp", None, "fsdp", None)),
        check_vma=False,
    )
```

time: 366 us -> 112 us (0.31)
  the two profiles are of different devices: /device:TPU:25 before, /device:TPU:6 now
where the time goes in v1:
time: 112 us; the launch traced here: 111 us
  starting transfers between devices  51.6 us (46%)
  waiting for transfers between devices  47.9 us (43%)
  Pallas kernels  7 us (6%)
  local copies, waits for them, and re-layouts  3.45 us (3%)
    ppermute x2, waiting for transfers between devices, scatter_y(): got = lax.ppermute(sent, BOTH, sum_pairs(0, 'y'))  20.5 us
    ppermute x5, waiting for transfers between devices, dp_swap(): return lax.ppermute(x, 'dp', [(d, d ^ flip) for d in range(N_DP)])  15.9 us
    ppermute x2, starting transfers between devices, scatter_z(): got = lax.ppermute(x[2:], BOTH, sum_pairs(0, 'z'))  13.6 us
    ppermute x2, starting transfers between devices, scatter_z(): last = lax.ppermute(x[1] + got[1], BOTH, sum_pairs(1, 'z'))  12.7 us
    ppermute x5, starting transfers between devices, dp_swap(): return lax.ppermute(x, 'dp', [(d, d ^ flip) for d in range(N_DP)])  11.9 us
    ppermute x2, waiting for transfers between devices, scatter_z(): got = lax.ppermute(x[2:], BOTH, sum_pairs(0, 'z'))  11.5 us
    ppermute x2, starting transfers between devices, scatter_y(): last = lax.ppermute(kept[1] + got[1], BOTH, sum_pairs(1, 'y'))  7.92 us
    ppermute x2, starting transfers between devices, scatter_y(): got = lax.ppermute(sent, BOTH, sum_pairs(0, 'y'))  5.53 us
  transfers between devices with their start and end apart: 13, of which 8 were waited for; matrix products, arithmetic and copies ran while one was open for 0% of the time, Pallas kernels for 4%

profile of v1, /device:TPU:6, one launch (start us, length us, event | category | flops | bytes accessed | tf_op | source)
XLA Modules:
  0.0 111.2 jit_solution(17020991662096720467)
XLA Ops:
  0.7 1.3 %copy-done.2 = bf16[1,1,2,64,5120]{4,3,2,1,0:T(8,128)(2,1)S(1)} copy-done((bf16[1,1,2,64,5120]{4,3,2,1,0:T(8,128)(2,1)S(1)}, bf16[1,1,2,64,5120]{4,3,2,1,0:T(8,128)(2,1)}, u32[]{:S(2)}) %copy-start.2) | copy-done | bytes 1310744
  4.1 1.8 %prep.3 = (f32[2,4,8,5120]{3,2,1,0:T(8,128)S(1)}, f32[2,4,8,640]{3,2,1,0:T(8,128)S(1)}) custom-call(s32[4]{0:T(128)S(1)} %pad_add_fusion.place_ref, s32[8]{0:T(128)S(1)} %copy-done.3, bf16[64,64]{1,0:T(8,128)(2,1)S(1)} %copy-done.6, bf16[64,64]{1,0:T(8,128)(2,1)S(1)} %copy-done.5, bf16[2,64,5120]{2,1,0:T(8,128)(2,1)S(1)} %bitcast.29), custom_call_target="tpu_custom_call" | custom-call | flops 400000000 | bytes 3000000 | tf_op jit(solution)/shard_map/prep/pallas_call | solution.py:79
  5.9 3.5 %collective-permute-start.9 = (f32[2,4,8,5120]{3,2,1,0:T(8,128)S(1)}, f32[2,4,8,5120]{3,2,1,0:T(8,128)S(1)}, u32[]{:S(2)}, u32[]{:S(2)}) collective-permute-start(f32[2,4,8,5120]{3,2,1,0:T(8,128)S(1)} %get-tuple-element.14), channel_id=1, source_target_pairs={{0,1},{1,0},{2,3},{3,2},{4,5},{5,4},{6,7},{7,6},{8,9},{9,8},{10,11... | collective-permute-start | bytes 3932168 | tf_op jit(solution)/shard_map/ppermute | solution.py:204
  9.4 1.8 %prep.2 = (f32[2,4,8,5120]{3,2,1,0:T(8,128)S(1)}, f32[2,4,8,640]{3,2,1,0:T(8,128)S(1)}) custom-call(s32[4]{0:T(128)S(1)} %pad_add_fusion.place_ref, s32[8]{0:T(128)S(1)} %copy-done.3, bf16[64,64]{1,0:T(8,128)(2,1)S(1)} %copy-done.6, bf16[64,64]{1,0:T(8,128)(2,1)S(1)} %copy-done.5, bf16[2,64,5120]{2,1,0:T(8,128)(2,1)S(1)} %bitcast.30), custom_call_target="tpu_custom_call" | custom-call | flops 400000000 | bytes 3000000 | tf_op jit(solution)/shard_map/prep/pallas_call | solution.py:79
  11.2 14.2 %collective-permute-done.9 = f32[2,4,8,5120]{3,2,1,0:T(8,128)S(1)} collective-permute-done((f32[2,4,8,5120]{3,2,1,0:T(8,128)S(1)}, f32[2,4,8,5120]{3,2,1,0:T(8,128)S(1)}, u32[]{:S(2)}, u32[]{:S(2)}) %collective-permute-start.9) | collective-permute-done | bytes 1310752 | tf_op jit(solution)/shard_map/ppermute | solution.py:204
  25.5 4.9 %collective-permute-start.10 = (f32[4,8,5120]{2,1,0:T(8,128)S(1)}, f32[4,8,5120]{2,1,0:T(8,128)S(1)}, u32[]{:S(2)}, u32[]{:S(2)}) collective-permute-start(f32[4,8,5120]{2,1,0:T(8,128)S(1)} %fusion), channel_id=1, source_target_pairs={{0,3},{1,2},{2,1},{3,0},{4,7},{5,6},{6,5},{7,4},{8,11},{9,10},{10,... | collective-permute-start | bytes 1966088 | tf_op jit(solution)/shard_map/ppermute | solution.py:205
  30.5 2.0 %collective-permute-start = (f32[2,4,8,640]{3,2,1,0:T(8,128)S(1)}, f32[2,4,8,640]{3,2,1,0:T(8,128)S(1)}, u32[]{:S(2)}, u32[]{:S(2)}) collective-permute-start(f32[2,4,8,640]{3,2,1,0:T(8,128)S(1)} %get-tuple-element.10), channel_id=1, source_target_pairs={{0,1},{1,0},{2,3},{3,2},{4,5},{5,4},{6,7},{7,6},{8,9},{9,8},{10,11... | collective-permute-start | bytes 491528 | tf_op jit(solution)/shard_map/ppermute | solution.py:204
  32.5 6.2 %collective-permute-done = f32[2,4,8,640]{3,2,1,0:T(8,128)S(1)} collective-permute-done((f32[2,4,8,640]{3,2,1,0:T(8,128)S(1)}, f32[2,4,8,640]{3,2,1,0:T(8,128)S(1)}, u32[]{:S(2)}, u32[]{:S(2)}) %collective-permute-start) | collective-permute-done | bytes 163872 | tf_op jit(solution)/shard_map/ppermute | solution.py:204
  38.8 3.0 %collective-permute-start.1 = (f32[4,8,640]{2,1,0:T(8,128)S(1)}, f32[4,8,640]{2,1,0:T(8,128)S(1)}, u32[]{:S(2)}, u32[]{:S(2)}) collective-permute-start(f32[4,8,640]{2,1,0:T(8,128)S(1)} %fusion.5), channel_id=1, source_target_pairs={{0,3},{1,2},{2,1},{3,0},{4,7},{5,6},{6,5},{7,4},{8,11},{9,10},{10,... | collective-permute-start | bytes 245768 | tf_op jit(solution)/shard_map/ppermute | solution.py:205
  42.0 9.2 %collective-permute-start.11 = (f32[2,8,5120]{2,1,0:T(8,128)S(1)}, f32[2,8,5120]{2,1,0:T(8,128)S(1)}, u32[]{:S(2)}, u32[]{:S(2)}) collective-permute-start(f32[2,8,5120]{2,1,0:T(8,128)S(1)} %slice.82), channel_id=1, source_target_pairs={{0,4},{1,5},{2,6},{3,7},{4,0},{5,1},{6,2},{7,3},{8,12},{9,13},{10,... | collective-permute-start | bytes 983048 | tf_op jit(solution)/shard_map/ppermute | solution.py:198
  51.3 4.3 %collective-permute-start.2 = (f32[2,8,640]{2,1,0:T(8,128)S(1)}, f32[2,8,640]{2,1,0:T(8,128)S(1)}, u32[]{:S(2)}, u32[]{:S(2)}) collective-permute-start(f32[2,8,640]{2,1,0:T(8,128)S(1)} %slice.75), channel_id=1, source_target_pairs={{0,4},{1,5},{2,6},{3,7},{4,0},{5,1},{6,2},{7,3},{8,12},{9,13},{10,... | collective-permute-start | bytes 122888 | tf_op jit(solution)/shard_map/ppermute | solution.py:198
  56.9 11.5 %collective-permute-done.2 = f32[2,8,640]{2,1,0:T(8,128)S(1)} collective-permute-done((f32[2,8,640]{2,1,0:T(8,128)S(1)}, f32[2,8,640]{2,1,0:T(8,128)S(1)}, u32[]{:S(2)}, u32[]{:S(2)}) %collective-permute-start.2) | collective-permute-done | bytes 40992 | tf_op jit(solution)/shard_map/ppermute | solution.py:198
  68.3 10.8 %collective-permute-start.3 = (f32[8,640]{1,0:T(8,128)S(1)}, f32[8,640]{1,0:T(8,128)S(1)}, u32[]{:S(2)}, u32[]{:S(2)}) collective-permute-start(f32[8,640]{1,0:T(8,128)S(1)} %fusion.8), channel_id=1, source_target_pairs={{0,12},{1,13},{2,14},{3,15},{4,8},{5,9},{6,10},{7,11},{8,4},{9,5},... | collective-permute-start | bytes 61448 | tf_op jit(solution)/shard_map/ppermute | solution.py:199
  79.2 1.9 %collective-permute-start.12 = (f32[8,5120]{1,0:T(8,128)S(1)}, f32[8,5120]{1,0:T(8,128)S(1)}, u32[]{:S(2)}, u32[]{:S(2)}) collective-permute-start(f32[8,5120]{1,0:T(8,128)S(1)} %get-tuple-element.16), channel_id=1, source_target_pairs={{0,12},{1,13},{2,14},{3,15},{4,8},{5,9},{6,10},{7,11},{8,4},{9,5},... | collective-permute-start | bytes 491528 | tf_op jit(solution)/shard_map/ppermute | solution.py:199
  81.1 1.9 %collective-permute-start.4 = (f32[8,640]{1,0:T(8,128)S(1)}, f32[8,640]{1,0:T(8,128)S(1)}, u32[]{:S(2)}, u32[]{:S(2)}) collective-permute-start(f32[8,640]{1,0:T(8,128)S(1)} %fusion.11), channel_id=1, source_target_pairs={{0,16},{16,0},{32,48},{48,32},{64,80},{80,64},{96,112},{112,96},{1... | collective-permute-start | bytes 61448 | tf_op jit(solution)/shard_map/ppermute | solution.py:194
  84.2 2.7 %collective-permute-start.5 = (f32[8,640]{1,0:T(8,128)S(1)}, f32[8,640]{1,0:T(8,128)S(1)}, u32[]{:S(2)}, u32[]{:S(2)}) collective-permute-start(f32[8,640]{1,0:T(8,128)S(1)} %add.92), channel_id=1, source_target_pairs={{0,32},{16,48},{32,0},{48,16},{64,96},{80,112},{96,64},{112,80},{1... | collective-permute-start | bytes 61448 | tf_op jit(solution)/shard_map/ppermute | solution.py:194
  86.9 2.9 %collective-permute-done.5 = f32[8,640]{1,0:T(8,128)S(1)} collective-permute-done((f32[8,640]{1,0:T(8,128)S(1)}, f32[8,640]{1,0:T(8,128)S(1)}, u32[]{:S(2)}, u32[]{:S(2)}) %collective-permute-start.5) | collective-permute-done | bytes 20512 | tf_op jit(solution)/shard_map/ppermute | solution.py:194
  89.9 2.4 %collective-permute-start.6 = (f32[8,640]{1,0:T(8,128)S(1)}, f32[8,640]{1,0:T(8,128)S(1)}, u32[]{:S(2)}, u32[]{:S(2)}) collective-permute-start(f32[8,640]{1,0:T(8,128)S(1)} %add.93), channel_id=1, source_target_pairs={{0,96},{16,112},{32,64},{48,80},{64,32},{80,48},{96,0},{112,16},{1... | collective-permute-start | bytes 61448 | tf_op jit(solution)/shard_map/ppermute | solution.py:194
  92.3 4.5 %collective-permute-done.6 = f32[8,640]{1,0:T(8,128)S(1)} collective-permute-done((f32[8,640]{1,0:T(8,128)S(1)}, f32[8,640]{1,0:T(8,128)S(1)}, u32[]{:S(2)}, u32[]{:S(2)}) %collective-permute-start.6) | collective-permute-done | bytes 20512 | tf_op jit(solution)/shard_map/ppermute | solution.py:194
  96.8 1.9 %collective-permute-start.7 = (f32[8,640]{1,0:T(8,128)S(1)}, f32[8,640]{1,0:T(8,128)S(1)}, u32[]{:S(2)}, u32[]{:S(2)}) collective-permute-start(f32[8,640]{1,0:T(8,128)S(1)} %add.94), channel_id=1, source_target_pairs={{0,128},{16,144},{32,160},{48,176},{64,192},{80,208},{96,224},{112... | collective-permute-start | bytes 61448 | tf_op jit(solution)/shard_map/ppermute | solution.py:194
  98.7 3.7 %collective-permute-done.7 = f32[8,640]{1,0:T(8,128)S(1)} collective-permute-done((f32[8,640]{1,0:T(8,128)S(1)}, f32[8,640]{1,0:T(8,128)S(1)}, u32[]{:S(2)}, u32[]{:S(2)}) %collective-permute-start.7) | collective-permute-done | bytes 20512 | tf_op jit(solution)/shard_map/ppermute | solution.py:194
  102.4 3.0 %collective-permute-start.8 = (f32[8,640]{1,0:T(8,128)S(1)}, f32[8,640]{1,0:T(8,128)S(1)}, u32[]{:S(2)}, u32[]{:S(2)}) collective-permute-start(f32[8,640]{1,0:T(8,128)S(1)} %add.95.own_ref), channel_id=1, source_target_pairs={{0,256},{16,272},{32,288},{48,304},{64,320},{80,336},{96,352},{112... | collective-permute-start | bytes 61448 | tf_op jit(solution)/shard_map/ppermute | solution.py:194
  105.4 3.6 %collective-permute-done.8.got_ref = f32[8,640]{1,0:T(8,128)S(1)} collective-permute-done((f32[8,640]{1,0:T(8,128)S(1)}, f32[8,640]{1,0:T(8,128)S(1)}, u32[]{:S(2)}, u32[]{:S(2)}) %collective-permute-start.8) | collective-permute-done | bytes 20512 | tf_op jit(solution)/shard_map/ppermute | solution.py:194
  109.0 1.3 %params.1 = f32[2,4,5120]{2,1,0:T(4,128)} custom-call(f32[8,640]{1,0:T(8,128)S(1)} %add.95.own_ref, f32[8,640]{1,0:T(8,128)S(1)} %collective-permute-done.8.got_ref, f32[2,4,5120]{2,1,0:T(4,128)S(1)} %copy-done, f32[1024,128]{1,0:T(8,128)S(1)} %get-tuple-element.12.expand_ref), custom_call_target="tpu_custom_call" | custom-call | flops 60000000 | bytes 700000 | tf_op jit(solution)/shard_map/params/pallas_call | solution.py:168
  (35 shorter events, 5.9 us)
Async XLA Ops:
  0.7 1.3 %copy-start.2 = (bf16[1,1,2,64,5120]{4,3,2,1,0:T(8,128)(2,1)S(1)}, bf16[1,1,2,64,5120]{4,3,2,1,0:T(8,128)(2,1)}, u32[]{:S(2)}) copy-start(bf16[1,1,2,64,5120]{4,3,2,1,0:T(8,128)(2,1)} %param.7) | copy-start | bytes 3932164
  2.1 0.7 copy-start.3
  2.7 0.7 copy-start.5
  3.4 0.7 copy-start.6
  5.9 19.5 %collective-permute-start.9 = (f32[2,4,8,5120]{3,2,1,0:T(8,128)S(1)}, f32[2,4,8,5120]{3,2,1,0:T(8,128)S(1)}, u32[]{:S(2)}, u32[]{:S(2)}) collective-permute-start(f32[2,4,8,5120]{3,2,1,0:T(8,128)S(1)} %get-tuple-element.14), channel_id=1, source_target_pairs={{0,1},{1,0},{2,3},{3,2},{4,5},{5,4},{6,7},{7,6},{8,9},{9,8},{10,11... | collective-permute-start | bytes 3932168 | tf_op jit(solution)/shard_map/ppermute | solution.py:204
  25.5 16.3 %collective-permute-start.10 = (f32[4,8,5120]{2,1,0:T(8,128)S(1)}, f32[4,8,5120]{2,1,0:T(8,128)S(1)}, u32[]{:S(2)}, u32[]{:S(2)}) collective-permute-start(f32[4,8,5120]{2,1,0:T(8,128)S(1)} %fusion), channel_id=1, source_target_pairs={{0,3},{1,2},{2,1},{3,0},{4,7},{5,6},{6,5},{7,4},{8,11},{9,10},{10,... | collective-permute-start | bytes 1966088 | tf_op jit(solution)/shard_map/ppermute | solution.py:205
  30.5 8.3 %collective-permute-start = (f32[2,4,8,640]{3,2,1,0:T(8,128)S(1)}, f32[2,4,8,640]{3,2,1,0:T(8,128)S(1)}, u32[]{:S(2)}, u32[]{:S(2)}) collective-permute-start(f32[2,4,8,640]{3,2,1,0:T(8,128)S(1)} %get-tuple-element.10), channel_id=1, source_target_pairs={{0,1},{1,0},{2,3},{3,2},{4,5},{5,4},{6,7},{7,6},{8,9},{9,8},{10,11... | collective-permute-start | bytes 491528 | tf_op jit(solution)/shard_map/ppermute | solution.py:204
  38.8 16.8 %copy-start.1 = (f32[1,2,4,5120]{3,2,1,0:T(4,128)S(1)}, f32[1,2,4,5120]{3,2,1,0:T(4,128)}, u32[]{:S(2)}) copy-start(f32[1,2,4,5120]{3,2,1,0:T(4,128)} %momentum_ref.3) | copy-start | bytes 491524
  38.8 16.8 %copy-start.4 = (f32[64,64]{1,0:T(8,128)S(1)}, f32[64,64]{1,0:T(8,128)}, u32[]{:S(2)}) copy-start(f32[64,64]{1,0:T(8,128)} %constant.50.clone.table_ref) | copy-start | bytes 49156
  38.8 12.4 %collective-permute-start.1 = (f32[4,8,640]{2,1,0:T(8,128)S(1)}, f32[4,8,640]{2,1,0:T(8,128)S(1)}, u32[]{:S(2)}, u32[]{:S(2)}) collective-permute-start(f32[4,8,640]{2,1,0:T(8,128)S(1)} %fusion.5), channel_id=1, source_target_pairs={{0,3},{1,2},{2,1},{3,0},{4,7},{5,6},{6,5},{7,4},{8,11},{9,10},{10,... | collective-permute-start | bytes 245768 | tf_op jit(solution)/shard_map/ppermute | solution.py:205
  42.0 67.0 %copy-start = (f32[2,4,5120]{2,1,0:T(4,128)S(1)}, f32[2,4,5120]{2,1,0:T(4,128)}, u32[]{:S(2)}) copy-start(f32[2,4,5120]{2,1,0:T(4,128)} %params_ref.1) | copy-start | bytes 491524
  42.0 37.1 %collective-permute-start.11 = (f32[2,8,5120]{2,1,0:T(8,128)S(1)}, f32[2,8,5120]{2,1,0:T(8,128)S(1)}, u32[]{:S(2)}, u32[]{:S(2)}) collective-permute-start(f32[2,8,5120]{2,1,0:T(8,128)S(1)} %slice.82), channel_id=1, source_target_pairs={{0,4},{1,5},{2,6},{3,7},{4,0},{5,1},{6,2},{7,3},{8,12},{9,13},{10,... | collective-permute-start | bytes 983048 | tf_op jit(solution)/shard_map/ppermute | solution.py:198
  51.3 17.0 %collective-permute-start.2 = (f32[2,8,640]{2,1,0:T(8,128)S(1)}, f32[2,8,640]{2,1,0:T(8,128)S(1)}, u32[]{:S(2)}, u32[]{:S(2)}) collective-permute-start(f32[2,8,640]{2,1,0:T(8,128)S(1)} %slice.75), channel_id=1, source_target_pairs={{0,4},{1,5},{2,6},{3,7},{4,0},{5,1},{6,2},{7,3},{8,12},{9,13},{10,... | collective-permute-start | bytes 122888 | tf_op jit(solution)/shard_map/ppermute | solution.py:198
  68.3 12.8 %collective-permute-start.3 = (f32[8,640]{1,0:T(8,128)S(1)}, f32[8,640]{1,0:T(8,128)S(1)}, u32[]{:S(2)}, u32[]{:S(2)}) collective-permute-start(f32[8,640]{1,0:T(8,128)S(1)} %fusion.8), channel_id=1, source_target_pairs={{0,12},{1,13},{2,14},{3,15},{4,8},{5,9},{6,10},{7,11},{8,4},{9,5},... | collective-permute-start | bytes 61448 | tf_op jit(solution)/shard_map/ppermute | solution.py:199
  79.2 31.1 %collective-permute-start.12 = (f32[8,5120]{1,0:T(8,128)S(1)}, f32[8,5120]{1,0:T(8,128)S(1)}, u32[]{:S(2)}, u32[]{:S(2)}) collective-permute-start(f32[8,5120]{1,0:T(8,128)S(1)} %get-tuple-element.16), channel_id=1, source_target_pairs={{0,12},{1,13},{2,14},{3,15},{4,8},{5,9},{6,10},{7,11},{8,4},{9,5},... | collective-permute-start | bytes 491528 | tf_op jit(solution)/shard_map/ppermute | solution.py:199
  81.1 3.1 %collective-permute-start.4 = (f32[8,640]{1,0:T(8,128)S(1)}, f32[8,640]{1,0:T(8,128)S(1)}, u32[]{:S(2)}, u32[]{:S(2)}) collective-permute-start(f32[8,640]{1,0:T(8,128)S(1)} %fusion.11), channel_id=1, source_target_pairs={{0,16},{16,0},{32,48},{48,32},{64,80},{80,64},{96,112},{112,96},{1... | collective-permute-start | bytes 61448 | tf_op jit(solution)/shard_map/ppermute | solution.py:194
  84.2 5.7 %collective-permute-start.5 = (f32[8,640]{1,0:T(8,128)S(1)}, f32[8,640]{1,0:T(8,128)S(1)}, u32[]{:S(2)}, u32[]{:S(2)}) collective-permute-start(f32[8,640]{1,0:T(8,128)S(1)} %add.92), channel_id=1, source_target_pairs={{0,32},{16,48},{32,0},{48,16},{64,96},{80,112},{96,64},{112,80},{1... | collective-permute-start | bytes 61448 | tf_op jit(solution)/shard_map/ppermute | solution.py:194
  89.9 6.9 %collective-permute-start.6 = (f32[8,640]{1,0:T(8,128)S(1)}, f32[8,640]{1,0:T(8,128)S(1)}, u32[]{:S(2)}, u32[]{:S(2)}) collective-permute-start(f32[8,640]{1,0:T(8,128)S(1)} %add.93), channel_id=1, source_target_pairs={{0,96},{16,112},{32,64},{48,80},{64,32},{80,48},{96,0},{112,16},{1... | collective-permute-start | bytes 61448 | tf_op jit(solution)/shard_map/ppermute | solution.py:194
  96.8 5.7 %collective-permute-start.7 = (f32[8,640]{1,0:T(8,128)S(1)}, f32[8,640]{1,0:T(8,128)S(1)}, u32[]{:S(2)}, u32[]{:S(2)}) collective-permute-start(f32[8,640]{1,0:T(8,128)S(1)} %add.94), channel_id=1, source_target_pairs={{0,128},{16,144},{32,160},{48,176},{64,192},{80,208},{96,224},{112... | collective-permute-start | bytes 61448 | tf_op jit(solution)/shard_map/ppermute | solution.py:194
  102.4 6.6 %collective-permute-start.8 = (f32[8,640]{1,0:T(8,128)S(1)}, f32[8,640]{1,0:T(8,128)S(1)}, u32[]{:S(2)}, u32[]{:S(2)}) collective-permute-start(f32[8,640]{1,0:T(8,128)S(1)} %add.95.own_ref), channel_id=1, source_target_pairs={{0,256},{16,272},{32,288},{48,304},{64,320},{80,336},{96,352},{112... | collective-permute-start | bytes 61448 | tf_op jit(solution)/shard_map/ppermute | solution.py:194

commit v2 on v1

v2 whole, which is shorter than its diff:
```python
import math

import jax
import jax.numpy as jnp
import numpy as np
from jax import lax
from jax.experimental import pallas as pl
from jax.experimental.pallas import tpu as pltpu
from jax.sharding import PartitionSpec as P

SPAN = 64
KEEP = 8
ROW_VALS = 5120
LAYERS = 2
GROUP = 128 // KEEP
WIDE = GROUP * SPAN
CHUNKS = ROW_VALS // WIDE
COEFFS = ROW_VALS // SPAN * KEEP
OWN = 8
HIGHEST = lax.Precision.HIGHEST
BOTH = ("dp", "fsdp")
N_DP = 32
N_FSDP = 16


def picked_t(kept_ref):
    lane = lax.broadcasted_iota(jnp.int32, (SPAN, 128), 1) % KEEP
    n = lax.broadcasted_iota(jnp.int32, (SPAN, 128), 0)
    k = jnp.zeros((SPAN, 128), jnp.int32)
    for j in range(KEEP):
        k = jnp.where(lane == j, kept_ref[j], k)
    turn = ((2 * n + 1) * k) & (4 * SPAN - 1)
    turn = jnp.minimum(turn, 4 * SPAN - turn)
    flip = turn > SPAN
    angle = jnp.where(flip, 2 * SPAN - turn, turn).astype(jnp.float32) * np.float32(np.pi / (2 * SPAN))
    square = angle * angle
    value = jnp.full((SPAN, 128), (-1.0) ** 8 / math.factorial(16), jnp.float32)
    for term in range(7, -1, -1):
        value = value * square + (-1.0) ** term / math.factorial(2 * term)
    value = jnp.where(flip, -value, value)
    return value * jnp.where(k == 0, np.float32(np.sqrt(1.0 / SPAN)), np.float32(np.sqrt(2.0 / SPAN)))


def spread(picked):
    tall = jnp.concatenate([picked] * GROUP, axis=0)
    row = lax.broadcasted_iota(jnp.int32, (WIDE, 128), 0)
    col = lax.broadcasted_iota(jnp.int32, (WIDE, 128), 1)
    return jnp.where(row // SPAN == col // KEEP, tall, 0.0)


def slot_order():
    y, z = lax.axis_index("fsdp") % 4, lax.axis_index("fsdp") // 4
    near = 1 + 2 * (lax.axis_index("dp") % 2)
    far = 4 - near
    r = lax.broadcasted_iota(jnp.int32, (128, 128), 0)
    col = lax.broadcasted_iota(jnp.int32, (128, 128), 1)

    def partner(slot):
        return jnp.where(slot == 0, 0, jnp.where(slot == 1, far, jnp.where(slot == 2, near, 2)))

    to_y = y ^ partner(r // (4 * OWN))
    to_z = z ^ partner((r // OWN) % 4)
    source = ((r // 4) % 2) * 64 + to_z * 16 + to_y * 4 + r % 4
    return (source == col).astype(jnp.float32).astype(jnp.bfloat16)


def coef_kernel(indices_ref, grad_ref, kept_out_ref, sent_ref, kept_ref, held, sems):
    indices = pltpu.make_async_copy(indices_ref, kept_ref, sems.at[CHUNKS])
    indices.start()

    def chunk(c):
        lanes = pl.ds(c * WIDE, WIDE)
        return pltpu.make_async_copy(grad_ref.at[:, :, lanes], held.at[:, :, lanes], sems.at[c])

    for c in range(CHUNKS):
        chunk(c).start()
    order = slot_order()
    indices.wait()
    picked = picked_t(kept_ref)
    high = picked.astype(jnp.bfloat16).astype(jnp.float32)
    wide_hi = spread(high).astype(jnp.bfloat16)
    wide_lo = spread(picked - high).astype(jnp.bfloat16)
    for c in range(CHUNKS):
        chunk(c).wait()
        values = held[:, :, c * WIDE:(c + 1) * WIDE].reshape(128, WIDE)
        exact = jnp.dot(order, values, preferred_element_type=jnp.float32).astype(jnp.bfloat16)
        coef = jnp.dot(exact, wide_hi, preferred_element_type=jnp.float32)
        coef = coef + jnp.dot(exact, wide_lo, preferred_element_type=jnp.float32)
        kept_out_ref[:, :, :, c * 128:(c + 1) * 128] = coef[:64].reshape(2, 4, OWN, 128)
        sent_ref[:, :, :, c * 128:(c + 1) * 128] = coef[64:].reshape(2, 4, OWN, 128)


def coef_of(kept, grad):
    hbm = pl.BlockSpec(memory_space=pltpu.HBM)
    vmem = pl.BlockSpec(memory_space=pltpu.VMEM)
    half = jax.ShapeDtypeStruct((2, 4, OWN, COEFFS), jnp.float32)
    return pl.pallas_call(
        coef_kernel,
        out_shape=(half, half),
        in_specs=[hbm, hbm],
        out_specs=(vmem, vmem),
        scratch_shapes=[
            pltpu.SMEM(kept.shape, kept.dtype),
            pltpu.VMEM(grad.shape, grad.dtype),
            pltpu.SemaphoreType.DMA((CHUNKS + 1,)),
        ],
        compiler_params=pltpu.CompilerParams(vmem_limit_bytes=32 * 2**20),
        cost_estimate=pl.CostEstimate(flops=500_000_000, bytes_accessed=2_000_000, transcendentals=0),
        name="coef",
    )(kept, grad)


def main_kernel(grad_ref, kept_ref, sent_ref):
    order = slot_order()
    for c in range(CHUNKS):
        lanes = slice(c * WIDE, (c + 1) * WIDE)
        values = grad_ref[:, :, lanes].reshape(128, WIDE)
        rows = jnp.dot(order, values, preferred_element_type=jnp.float32)
        kept_ref[:, :, :, lanes] = rows[:64].reshape(2, 4, OWN, WIDE)
        sent_ref[:, :, :, lanes] = rows[64:].reshape(2, 4, OWN, WIDE)


def main_of(grad):
    vmem = pl.BlockSpec(memory_space=pltpu.VMEM)
    half = jax.ShapeDtypeStruct((2, 4, OWN, ROW_VALS), jnp.float32)
    return pl.pallas_call(
        main_kernel,
        out_shape=(half, half),
        in_specs=[vmem],
        out_specs=(vmem, vmem),
        compiler_params=pltpu.CompilerParams(vmem_limit_bytes=32 * 2**20),
        cost_estimate=pl.CostEstimate(flops=200_000_000, bytes_accessed=4_000_000, transcendentals=0),
        name="main",
    )(grad)


def tall(x):
    return jnp.concatenate([x[:, c * 128:(c + 1) * 128] for c in range(x.shape[1] // 128)], axis=0)


def state_kernel(kept_ref, momentum_ref, coef_ref, reject_ref, expand_ref):
    wide = spread(picked_t(kept_ref))
    pair = wide[:128, :]
    row = lax.broadcasted_iota(jnp.int32, (128, 128), 0)
    col = lax.broadcasted_iota(jnp.int32, (128, 128), 1)
    onto = lax.dot_general(pair, pair, (((1,), (1,)), ((), ())), precision=HIGHEST, preferred_element_type=jnp.float32)
    reject_ref[...] = jnp.where(row == col, 1.0, 0.0) - onto
    expand_ref[...] = wide
    state = 0.9 * jnp.concatenate([momentum_ref[0, 0], momentum_ref[0, 1]], axis=0)
    deep = jnp.concatenate([state[:, c * WIDE:(c + 1) * WIDE] for c in range(CHUNKS)], axis=0)
    coef = jnp.dot(deep, wide, precision=HIGHEST, preferred_element_type=jnp.float32)
    for c in range(CHUNKS):
        coef_ref[:, c * 128:(c + 1) * 128] = coef[c * OWN:(c + 1) * OWN]


def state_of(kept, momentum):
    smem = pl.BlockSpec(memory_space=pltpu.SMEM)
    vmem = pl.BlockSpec(memory_space=pltpu.VMEM)
    return pl.pallas_call(
        state_kernel,
        out_shape=(
            jax.ShapeDtypeStruct((OWN, COEFFS), jnp.float32),
            jax.ShapeDtypeStruct((128, 128), jnp.float32),
            jax.ShapeDtypeStruct((WIDE, 128), jnp.float32),
        ),
        in_specs=[smem, vmem],
        out_specs=(vmem, vmem, vmem),
        compiler_params=pltpu.CompilerParams(vmem_limit_bytes=32 * 2**20),
        cost_estimate=pl.CostEstimate(flops=100_000_000, bytes_accessed=1_000_000, transcendentals=0),
        name="state",
    )(kept, momentum)


def momentum_kernel(own_ref, got_ref, momentum_ref, reject_ref, out_ref):
    state = jnp.concatenate([momentum_ref[0, 0], momentum_ref[0, 1]], axis=0)
    moment = 0.9 * state + (own_ref[...] + got_ref[...])
    new = jnp.dot(tall(moment), reject_ref[...], precision=HIGHEST, preferred_element_type=jnp.float32)
    for c in range(ROW_VALS // 128):
        part = new[c * OWN:(c + 1) * OWN]
        out_ref[0, 0, :, c * 128:(c + 1) * 128] = part[:4]
        out_ref[0, 1, :, c * 128:(c + 1) * 128] = part[4:]


def new_momentum_of(own, got, momentum, reject):
    vmem = pl.BlockSpec(memory_space=pltpu.VMEM)
    return pl.pallas_call(
        momentum_kernel,
        out_shape=jax.ShapeDtypeStruct(momentum.shape, jnp.float32),
        in_specs=[vmem] * 4,
        out_specs=vmem,
        compiler_params=pltpu.CompilerParams(vmem_limit_bytes=32 * 2**20),
        cost_estimate=pl.CostEstimate(flops=60_000_000, bytes_accessed=700_000, transcendentals=0),
        name="momentum",
    )(own, got, momentum, reject)


def params_kernel(own_ref, got_ref, params_ref, expand_ref, out_ref):
    shared = (own_ref[...] + got_ref[...]) * (1.0 / N_DP)
    deep = tall(shared)
    update = lax.dot_general(
        deep, expand_ref[...], (((1,), (1,)), ((), ())), precision=HIGHEST, preferred_element_type=jnp.float32
    )
    for c in range(CHUNKS):
        lanes = slice(c * WIDE, (c + 1) * WIDE)
        part = update[c * OWN:(c + 1) * OWN]
        out_ref[0, :, lanes] = params_ref[0, :, lanes] - part[:4]
        out_ref[1, :, lanes] = params_ref[1, :, lanes] - part[4:]


def new_params_of(own, got, params, expand):
    vmem = pl.BlockSpec(memory_space=pltpu.VMEM)
    return pl.pallas_call(
        params_kernel,
        out_shape=jax.ShapeDtypeStruct(params.shape, jnp.float32),
        in_specs=[vmem] * 4,
        out_specs=vmem,
        compiler_params=pltpu.CompilerParams(vmem_limit_bytes=32 * 2**20),
        cost_estimate=pl.CostEstimate(flops=60_000_000, bytes_accessed=700_000, transcendentals=0),
        name="params",
    )(own, got, params, expand)


def sum_pairs(step, axis):
    pairs = []
    for d in range(N_DP):
        flip = (1, 3)[(d % 2) ^ step]
        for f in range(N_FSDP):
            to = f ^ (flip if axis == "y" else 4 * flip)
            pairs.append((d * N_FSDP + f, d * N_FSDP + to))
    return pairs


def halve(x, step, axis):
    return lax.ppermute(x, BOTH, sum_pairs(step, axis))


def dp_swap(x, flip):
    return lax.ppermute(x, "dp", [(d, d ^ flip) for d in range(N_DP)])


def after(x, earlier):
    return lax.optimization_barrier((x, earlier))


def shards(grad_partials, momentum, params, kept):
    grad = grad_partials[0, 0]
    coef, coef_sent = coef_of(kept, grad)
    main, main_sent = main_of(grad)
    state_coef, reject, expand = state_of(kept, momentum)

    coef_got = halve(coef_sent, 0, "y")
    main_sent, coef_got = after(main_sent, coef_got)
    main_got = halve(main_sent, 0, "y")
    coef_last = halve(coef[1] + coef_got[1], 1, "y")
    coef = coef[0] + coef_got[0] + coef_last
    coef_got = halve(coef[2:], 0, "z")
    main_got, coef_got = after(main_got, coef_got)

    main_last = halve(main[1] + main_got[1], 1, "y")
    coef_last = halve(coef[1] + coef_got[1], 1, "z")
    coef = coef[0] + coef_got[0] + coef_last + state_coef
    coef = coef + dp_swap(coef, 1)
    main_last, coef = after(main_last, coef)

    main = main[0] + main_got[0] + main_last
    main_got = halve(main[2:], 0, "z")
    for flip in (2, 6, 8):
        coef = coef + dp_swap(coef, flip)
    main_got, coef = after(main_got, coef)

    main_last = halve(main[1] + main_got[1], 1, "z")
    other = dp_swap(coef, 16)
    new_params = new_params_of(coef, other, params, expand)
    main_last, new_params = after(main_last, new_params)
    new_momentum = new_momentum_of(main[0] + main_got[0], main_last, momentum, reject)
    return (new_params, new_momentum)


def solution(mesh):
    placed = (
        P("dp", "fsdp", None, None, None),
        P("dp", None, "fsdp", None),
        P(None, "fsdp", None),
        P(),
    )
    return jax.shard_map(
        shards,
        mesh=mesh,
        in_specs=placed,
        out_specs=(P(None, "fsdp", None), P("dp", None, "fsdp", None)),
        check_vma=False,
    )
```

time: 112 us -> 101 us (0.902)
  waiting for transfers between devices: 47.9 us -> 29.2 us
  starting transfers between devices: 51.6 us -> 61.5 us
  local copies, waits for them, and re-layouts: 3.45 us -> 2.01 us
    ppermute x8, waiting for transfers between devices: 32 us -> 11.1 us  [halve(): return lax.ppermute(x, BOTH, sum_pairs(step, axis))]
    ppermute x8, starting transfers between devices: 39.7 us -> 48.1 us  [halve(): return lax.ppermute(x, BOTH, sum_pairs(step, axis))]
    ppermute x5, waiting for transfers between devices: 15.9 us -> 18.1 us  [dp_swap(): return lax.ppermute(x, 'dp', [(d, d ^ flip) for d in range(N_DP)])]
    ppermute x5, starting transfers between devices: 11.9 us -> 13.3 us  [dp_swap(): return lax.ppermute(x, 'dp', [(d, d ^ flip) for d in range(N_DP)])]
    unnamed x14 -> x10, local copies, waits for them, and re-layouts: 3.43 us -> 1.98 us
  transfers between devices with their start and end apart: 13 -> 13, of which waited for: 8 -> 9; matrix products, arithmetic and copies ran while one was open for 0% -> 0% of each run, Pallas kernels for 4% -> 3%
where the time goes in v2:
time: 101 us; the launch traced here: 100 us
  starting transfers between devices  61.5 us (61%)
  waiting for transfers between devices  29.2 us (29%)
  Pallas kernels  6.61 us (7%)
  local copies, waits for them, and re-layouts  2.01 us (2%)
    ppermute x8, starting transfers between devices, halve(): return lax.ppermute(x, BOTH, sum_pairs(step, axis))  48.1 us
    ppermute x5, waiting for transfers between devices, dp_swap(): return lax.ppermute(x, 'dp', [(d, d ^ flip) for d in range(N_DP)])  18.1 us
    ppermute x5, starting transfers between devices, dp_swap(): return lax.ppermute(x, 'dp', [(d, d ^ flip) for d in range(N_DP)])  13.3 us
    ppermute x8, waiting for transfers between devices, halve(): return lax.ppermute(x, BOTH, sum_pairs(step, axis))  11.1 us
    pallas_call x1, Pallas kernels, coef_of(): pl.pallas_call(coef_kernel, out_shape=(half, half), in_specs=[hbm, hbm],...  2.8 us
  transfers between devices with their start and end apart: 13, of which 9 were waited for; matrix products, arithmetic and copies ran while one was open for 0% of the time, Pallas kernels for 3%

profile of v2, /device:TPU:6, one launch (start us, length us, event | category | flops | bytes accessed | tf_op | source)
XLA Modules:
  0.0 100.4 jit_solution(5340574201307628865)
XLA Ops:
  0.6 1.3 %copy-done = bf16[1,1,2,64,5120]{4,3,2,1,0:T(8,128)(2,1)S(1)} copy-done((bf16[1,1,2,64,5120]{4,3,2,1,0:T(8,128)(2,1)S(1)}, bf16[1,1,2,64,5120]{4,3,2,1,0:T(8,128)(2,1)}, u32[]{:S(2)}) %copy-start) | copy-done | bytes 1310744
  2.6 2.8 %coef.1 = (f32[2,4,8,640]{3,2,1,0:T(8,128)S(1)}, f32[2,4,8,640]{3,2,1,0:T(8,128)S(1)}) custom-call(s32[8]{0:T(128)S(1)} %copy-done.4, bf16[2,64,5120]{2,1,0:T(8,128)(2,1)S(1)} %bitcast.21), custom_call_target="tpu_custom_call" | custom-call | flops 500000000 | bytes 2000000 | tf_op jit(solution)/shard_map/coef/pallas_call | solution.py:97
  5.4 3.5 %collective-permute-start = (f32[2,4,8,640]{3,2,1,0:T(8,128)S(1)}, f32[2,4,8,640]{3,2,1,0:T(8,128)S(1)}, u32[]{:S(2)}, u32[]{:S(2)}) collective-permute-start(f32[2,4,8,640]{3,2,1,0:T(8,128)S(1)} %get-tuple-element.21), channel_id=1, source_target_pairs={{0,1},{1,0},{2,3},{3,2},{4,5},{5,4},{6,7},{7,6},{8,9},{9,8},{10,11... | collective-permute-start | bytes 491528 | tf_op jit(solution)/shard_map/ppermute | solution.py:234
  9.4 3.2 %collective-permute-done = f32[2,4,8,640]{3,2,1,0:T(8,128)S(1)} collective-permute-done((f32[2,4,8,640]{3,2,1,0:T(8,128)S(1)}, f32[2,4,8,640]{3,2,1,0:T(8,128)S(1)}, u32[]{:S(2)}, u32[]{:S(2)}) %collective-permute-start) | collective-permute-done | bytes 163872 | tf_op jit(solution)/shard_map/ppermute | solution.py:234
  12.6 3.5 %collective-permute-start.1 = (f32[2,4,8,5120]{3,2,1,0:T(8,128)S(1)}, f32[2,4,8,5120]{3,2,1,0:T(8,128)S(1)}, u32[]{:S(2)}, u32[]{:S(2)}) collective-permute-start(f32[2,4,8,5120]{3,2,1,0:T(8,128)S(1)} %get-tuple-element.22), channel_id=1, source_target_pairs={{0,1},{1,0},{2,3},{3,2},{4,5},{5,4},{6,7},{7,6},{8,9},{9,8},{10,11... | collective-permute-start | bytes 3932168 | tf_op jit(solution)/shard_map/ppermute | solution.py:234
  16.1 4.2 %collective-permute-start.2 = (f32[4,8,640]{2,1,0:T(8,128)S(1)}, f32[4,8,640]{2,1,0:T(8,128)S(1)}, u32[]{:S(2)}, u32[]{:S(2)}) collective-permute-start(f32[4,8,640]{2,1,0:T(8,128)S(1)} %add_bitcast_fusion.1), channel_id=1, source_target_pairs={{0,3},{1,2},{2,1},{3,0},{4,7},{5,6},{6,5},{7,4},{8,11},{9,10},{10,... | collective-permute-start | bytes 245768 | tf_op jit(solution)/shard_map/ppermute | solution.py:234
  20.4 4.4 %collective-permute-done.2 = f32[4,8,640]{2,1,0:T(8,128)S(1)} collective-permute-done((f32[4,8,640]{2,1,0:T(8,128)S(1)}, f32[4,8,640]{2,1,0:T(8,128)S(1)}, u32[]{:S(2)}, u32[]{:S(2)}) %collective-permute-start.2) | collective-permute-done | bytes 81952 | tf_op jit(solution)/shard_map/ppermute | solution.py:234
  24.8 9.1 %collective-permute-start.3 = (f32[2,8,640]{2,1,0:T(8,128)S(1)}, f32[2,8,640]{2,1,0:T(8,128)S(1)}, u32[]{:S(2)}, u32[]{:S(2)}) collective-permute-start(f32[2,8,640]{2,1,0:T(8,128)S(1)} %slice.72), channel_id=1, source_target_pairs={{0,4},{1,5},{2,6},{3,7},{4,0},{5,1},{6,2},{7,3},{8,12},{9,13},{10,... | collective-permute-start | bytes 122888 | tf_op jit(solution)/shard_map/ppermute | solution.py:234
  33.9 2.8 %collective-permute-done.3 = f32[2,8,640]{2,1,0:T(8,128)S(1)} collective-permute-done((f32[2,8,640]{2,1,0:T(8,128)S(1)}, f32[2,8,640]{2,1,0:T(8,128)S(1)}, u32[]{:S(2)}, u32[]{:S(2)}) %collective-permute-start.3) | collective-permute-done | bytes 40992 | tf_op jit(solution)/shard_map/ppermute | solution.py:234
  36.8 3.2 %collective-permute-start.4 = (f32[4,8,5120]{2,1,0:T(8,128)S(1)}, f32[4,8,5120]{2,1,0:T(8,128)S(1)}, u32[]{:S(2)}, u32[]{:S(2)}) collective-permute-start(f32[4,8,5120]{2,1,0:T(8,128)S(1)} %add_bitcast_fusion), channel_id=1, source_target_pairs={{0,3},{1,2},{2,1},{3,0},{4,7},{5,6},{6,5},{7,4},{8,11},{9,10},{10,... | collective-permute-start | bytes 1966088 | tf_op jit(solution)/shard_map/ppermute | solution.py:234
  40.0 11.5 %collective-permute-start.5 = (f32[8,640]{1,0:T(8,128)S(1)}, f32[8,640]{1,0:T(8,128)S(1)}, u32[]{:S(2)}, u32[]{:S(2)}) collective-permute-start(f32[8,640]{1,0:T(8,128)S(1)} %fusion.2), channel_id=1, source_target_pairs={{0,12},{1,13},{2,14},{3,15},{4,8},{5,9},{6,10},{7,11},{8,4},{9,5},... | collective-permute-start | bytes 61448 | tf_op jit(solution)/shard_map/ppermute | solution.py:234
  53.3 1.9 %collective-permute-start.6 = (f32[8,640]{1,0:T(8,128)S(1)}, f32[8,640]{1,0:T(8,128)S(1)}, u32[]{:S(2)}, u32[]{:S(2)}) collective-permute-start(f32[8,640]{1,0:T(8,128)S(1)} %fusion.5), channel_id=1, source_target_pairs={{0,16},{16,0},{32,48},{48,32},{64,80},{80,64},{96,112},{112,96},{1... | collective-permute-start | bytes 61448 | tf_op jit(solution)/shard_map/ppermute | solution.py:238
  55.2 1.2 %collective-permute-done.6 = f32[8,640]{1,0:T(8,128)S(1)} collective-permute-done((f32[8,640]{1,0:T(8,128)S(1)}, f32[8,640]{1,0:T(8,128)S(1)}, u32[]{:S(2)}, u32[]{:S(2)}) %collective-permute-start.6) | collective-permute-done | bytes 20512 | tf_op jit(solution)/shard_map/ppermute | solution.py:238
  56.5 5.6 %collective-permute-start.7 = (f32[2,8,5120]{2,1,0:T(8,128)S(1)}, f32[2,8,5120]{2,1,0:T(8,128)S(1)}, u32[]{:S(2)}, u32[]{:S(2)}) collective-permute-start(f32[2,8,5120]{2,1,0:T(8,128)S(1)} %slice.76), channel_id=1, source_target_pairs={{0,4},{1,5},{2,6},{3,7},{4,0},{5,1},{6,2},{7,3},{8,12},{9,13},{10,... | collective-permute-start | bytes 983048 | tf_op jit(solution)/shard_map/ppermute | solution.py:234
  62.1 2.7 %collective-permute-start.8 = (f32[8,640]{1,0:T(8,128)S(1)}, f32[8,640]{1,0:T(8,128)S(1)}, u32[]{:S(2)}, u32[]{:S(2)}) collective-permute-start(f32[8,640]{1,0:T(8,128)S(1)} %add.86), channel_id=1, source_target_pairs={{0,32},{16,48},{32,0},{48,16},{64,96},{80,112},{96,64},{112,80},{1... | collective-permute-start | bytes 61448 | tf_op jit(solution)/shard_map/ppermute | solution.py:238
  64.9 2.9 %collective-permute-done.8 = f32[8,640]{1,0:T(8,128)S(1)} collective-permute-done((f32[8,640]{1,0:T(8,128)S(1)}, f32[8,640]{1,0:T(8,128)S(1)}, u32[]{:S(2)}, u32[]{:S(2)}) %collective-permute-start.8) | collective-permute-done | bytes 20512 | tf_op jit(solution)/shard_map/ppermute | solution.py:238
  67.8 2.4 %collective-permute-start.9 = (f32[8,640]{1,0:T(8,128)S(1)}, f32[8,640]{1,0:T(8,128)S(1)}, u32[]{:S(2)}, u32[]{:S(2)}) collective-permute-start(f32[8,640]{1,0:T(8,128)S(1)} %add.88), channel_id=1, source_target_pairs={{0,96},{16,112},{32,64},{48,80},{64,32},{80,48},{96,0},{112,16},{1... | collective-permute-start | bytes 61448 | tf_op jit(solution)/shard_map/ppermute | solution.py:238
  70.2 4.5 %collective-permute-done.9 = f32[8,640]{1,0:T(8,128)S(1)} collective-permute-done((f32[8,640]{1,0:T(8,128)S(1)}, f32[8,640]{1,0:T(8,128)S(1)}, u32[]{:S(2)}, u32[]{:S(2)}) %collective-permute-start.9) | collective-permute-done | bytes 20512 | tf_op jit(solution)/shard_map/ppermute | solution.py:238
  74.7 2.9 %collective-permute-start.10 = (f32[8,640]{1,0:T(8,128)S(1)}, f32[8,640]{1,0:T(8,128)S(1)}, u32[]{:S(2)}, u32[]{:S(2)}) collective-permute-start(f32[8,640]{1,0:T(8,128)S(1)} %add.89), channel_id=1, source_target_pairs={{0,128},{16,144},{32,160},{48,176},{64,192},{80,208},{96,224},{112... | collective-permute-start | bytes 61448 | tf_op jit(solution)/shard_map/ppermute | solution.py:238
  77.6 2.9 %collective-permute-done.10 = f32[8,640]{1,0:T(8,128)S(1)} collective-permute-done((f32[8,640]{1,0:T(8,128)S(1)}, f32[8,640]{1,0:T(8,128)S(1)}, u32[]{:S(2)}, u32[]{:S(2)}) %collective-permute-start.10) | collective-permute-done | bytes 20512 | tf_op jit(solution)/shard_map/ppermute | solution.py:238
  80.6 7.6 %collective-permute-start.11 = (f32[8,5120]{1,0:T(8,128)S(1)}, f32[8,5120]{1,0:T(8,128)S(1)}, u32[]{:S(2)}, u32[]{:S(2)}) collective-permute-start(f32[8,5120]{1,0:T(8,128)S(1)} %get-tuple-element.37), channel_id=1, source_target_pairs={{0,12},{1,13},{2,14},{3,15},{4,8},{5,9},{6,10},{7,11},{8,4},{9,5},... | collective-permute-start | bytes 491528 | tf_op jit(solution)/shard_map/ppermute | solution.py:234
  88.2 3.4 %collective-permute-start.12 = (f32[8,640]{1,0:T(8,128)S(1)}, f32[8,640]{1,0:T(8,128)S(1)}, u32[]{:S(2)}, u32[]{:S(2)}) collective-permute-start(f32[8,640]{1,0:T(8,128)S(1)} %add.90.own_ref), channel_id=1, source_target_pairs={{0,256},{16,272},{32,288},{48,304},{64,320},{80,336},{96,352},{112... | collective-permute-start | bytes 61448 | tf_op jit(solution)/shard_map/ppermute | solution.py:238
  91.6 6.6 %collective-permute-done.12.got_ref = f32[8,640]{1,0:T(8,128)S(1)} collective-permute-done((f32[8,640]{1,0:T(8,128)S(1)}, f32[8,640]{1,0:T(8,128)S(1)}, u32[]{:S(2)}, u32[]{:S(2)}) %collective-permute-start.12) | collective-permute-done | bytes 20512 | tf_op jit(solution)/shard_map/ppermute | solution.py:238
  98.2 1.3 %params.1 = f32[2,4,5120]{2,1,0:T(4,128)} custom-call(f32[8,640]{1,0:T(8,128)S(1)} %add.90.own_ref, f32[8,640]{1,0:T(8,128)S(1)} %collective-permute-done.12.got_ref, f32[2,4,5120]{2,1,0:T(4,128)S(1)} %copy-done.2, f32[1024,128]{1,0:T(8,128)S(1)} %get-tuple-element.32.expand_ref), custom_call_target="tpu_custom_call" | custom-call | flops 60000000 | bytes 700000 | tf_op jit(solution)/shard_map/params/pallas_call | solution.py:212
  (30 shorter events, 4.2 us)
Async XLA Ops:
  0.6 1.3 %copy-start = (bf16[1,1,2,64,5120]{4,3,2,1,0:T(8,128)(2,1)S(1)}, bf16[1,1,2,64,5120]{4,3,2,1,0:T(8,128)(2,1)}, u32[]{:S(2)}) copy-start(bf16[1,1,2,64,5120]{4,3,2,1,0:T(8,128)(2,1)} %param.4) | copy-start | bytes 3932164
  1.9 0.7 copy-start.4
  2.6 6.3 %copy-start.1 = (bf16[1,1,2,64,5120]{4,3,2,1,0:T(8,128)(2,1)S(1)}, bf16[1,1,2,64,5120]{4,3,2,1,0:T(8,128)(2,1)}, u32[]{:S(2)}) copy-start(bf16[1,1,2,64,5120]{4,3,2,1,0:T(8,128)(2,1)} %param.4) | copy-start | bytes 3932164
  5.4 7.2 %collective-permute-start = (f32[2,4,8,640]{3,2,1,0:T(8,128)S(1)}, f32[2,4,8,640]{3,2,1,0:T(8,128)S(1)}, u32[]{:S(2)}, u32[]{:S(2)}) collective-permute-start(f32[2,4,8,640]{3,2,1,0:T(8,128)S(1)} %get-tuple-element.21), channel_id=1, source_target_pairs={{0,1},{1,0},{2,3},{3,2},{4,5},{5,4},{6,7},{7,6},{8,9},{9,8},{10,11... | collective-permute-start | bytes 491528 | tf_op jit(solution)/shard_map/ppermute | solution.py:234
  12.6 24.1 %collective-permute-start.1 = (f32[2,4,8,5120]{3,2,1,0:T(8,128)S(1)}, f32[2,4,8,5120]{3,2,1,0:T(8,128)S(1)}, u32[]{:S(2)}, u32[]{:S(2)}) collective-permute-start(f32[2,4,8,5120]{3,2,1,0:T(8,128)S(1)} %get-tuple-element.22), channel_id=1, source_target_pairs={{0,1},{1,0},{2,3},{3,2},{4,5},{5,4},{6,7},{7,6},{8,9},{9,8},{10,11... | collective-permute-start | bytes 3932168 | tf_op jit(solution)/shard_map/ppermute | solution.py:234
  16.1 35.4 %copy-start.3 = (f32[1,2,4,5120]{3,2,1,0:T(4,128)S(1)}, f32[1,2,4,5120]{3,2,1,0:T(4,128)}, u32[]{:S(2)}) copy-start(f32[1,2,4,5120]{3,2,1,0:T(4,128)} %momentum_ref.3) | copy-start | bytes 491524
  16.1 8.6 %collective-permute-start.2 = (f32[4,8,640]{2,1,0:T(8,128)S(1)}, f32[4,8,640]{2,1,0:T(8,128)S(1)}, u32[]{:S(2)}, u32[]{:S(2)}) collective-permute-start(f32[4,8,640]{2,1,0:T(8,128)S(1)} %add_bitcast_fusion.1), channel_id=1, source_target_pairs={{0,3},{1,2},{2,1},{3,0},{4,7},{5,6},{6,5},{7,4},{8,11},{9,10},{10,... | collective-permute-start | bytes 245768 | tf_op jit(solution)/shard_map/ppermute | solution.py:234
  24.8 12.0 %collective-permute-start.3 = (f32[2,8,640]{2,1,0:T(8,128)S(1)}, f32[2,8,640]{2,1,0:T(8,128)S(1)}, u32[]{:S(2)}, u32[]{:S(2)}) collective-permute-start(f32[2,8,640]{2,1,0:T(8,128)S(1)} %slice.72), channel_id=1, source_target_pairs={{0,4},{1,5},{2,6},{3,7},{4,0},{5,1},{6,2},{7,3},{8,12},{9,13},{10,... | collective-permute-start | bytes 122888 | tf_op jit(solution)/shard_map/ppermute | solution.py:234
  36.8 19.6 %collective-permute-start.4 = (f32[4,8,5120]{2,1,0:T(8,128)S(1)}, f32[4,8,5120]{2,1,0:T(8,128)S(1)}, u32[]{:S(2)}, u32[]{:S(2)}) collective-permute-start(f32[4,8,5120]{2,1,0:T(8,128)S(1)} %add_bitcast_fusion), channel_id=1, source_target_pairs={{0,3},{1,2},{2,1},{3,0},{4,7},{5,6},{6,5},{7,4},{8,11},{9,10},{10,... | collective-permute-start | bytes 1966088 | tf_op jit(solution)/shard_map/ppermute | solution.py:234
  40.0 13.2 %collective-permute-start.5 = (f32[8,640]{1,0:T(8,128)S(1)}, f32[8,640]{1,0:T(8,128)S(1)}, u32[]{:S(2)}, u32[]{:S(2)}) collective-permute-start(f32[8,640]{1,0:T(8,128)S(1)} %fusion.2), channel_id=1, source_target_pairs={{0,12},{1,13},{2,14},{3,15},{4,8},{5,9},{6,10},{7,11},{8,4},{9,5},... | collective-permute-start | bytes 61448 | tf_op jit(solution)/shard_map/ppermute | solution.py:234
  53.3 3.1 %collective-permute-start.6 = (f32[8,640]{1,0:T(8,128)S(1)}, f32[8,640]{1,0:T(8,128)S(1)}, u32[]{:S(2)}, u32[]{:S(2)}) collective-permute-start(f32[8,640]{1,0:T(8,128)S(1)} %fusion.5), channel_id=1, source_target_pairs={{0,16},{16,0},{32,48},{48,32},{64,80},{80,64},{96,112},{112,96},{1... | collective-permute-start | bytes 61448 | tf_op jit(solution)/shard_map/ppermute | solution.py:238
  56.5 41.7 %copy-start.2 = (f32[2,4,5120]{2,1,0:T(4,128)S(1)}, f32[2,4,5120]{2,1,0:T(4,128)}, u32[]{:S(2)}) copy-start(f32[2,4,5120]{2,1,0:T(4,128)} %params_ref.1) | copy-start | bytes 491524
  56.5 24.0 %collective-permute-start.7 = (f32[2,8,5120]{2,1,0:T(8,128)S(1)}, f32[2,8,5120]{2,1,0:T(8,128)S(1)}, u32[]{:S(2)}, u32[]{:S(2)}) collective-permute-start(f32[2,8,5120]{2,1,0:T(8,128)S(1)} %slice.76), channel_id=1, source_target_pairs={{0,4},{1,5},{2,6},{3,7},{4,0},{5,1},{6,2},{7,3},{8,12},{9,13},{10,... | collective-permute-start | bytes 983048 | tf_op jit(solution)/shard_map/ppermute | solution.py:234
  62.1 5.7 %collective-permute-start.8 = (f32[8,640]{1,0:T(8,128)S(1)}, f32[8,640]{1,0:T(8,128)S(1)}, u32[]{:S(2)}, u32[]{:S(2)}) collective-permute-start(f32[8,640]{1,0:T(8,128)S(1)} %add.86), channel_id=1, source_target_pairs={{0,32},{16,48},{32,0},{48,16},{64,96},{80,112},{96,64},{112,80},{1... | collective-permute-start | bytes 61448 | tf_op jit(solution)/shard_map/ppermute | solution.py:238
  67.8 6.9 %collective-permute-start.9 = (f32[8,640]{1,0:T(8,128)S(1)}, f32[8,640]{1,0:T(8,128)S(1)}, u32[]{:S(2)}, u32[]{:S(2)}) collective-permute-start(f32[8,640]{1,0:T(8,128)S(1)} %add.88), channel_id=1, source_target_pairs={{0,96},{16,112},{32,64},{48,80},{64,32},{80,48},{96,0},{112,16},{1... | collective-permute-start | bytes 61448 | tf_op jit(solution)/shard_map/ppermute | solution.py:238
  74.7 5.9 %collective-permute-start.10 = (f32[8,640]{1,0:T(8,128)S(1)}, f32[8,640]{1,0:T(8,128)S(1)}, u32[]{:S(2)}, u32[]{:S(2)}) collective-permute-start(f32[8,640]{1,0:T(8,128)S(1)} %add.89), channel_id=1, source_target_pairs={{0,128},{16,144},{32,160},{48,176},{64,192},{80,208},{96,224},{112... | collective-permute-start | bytes 61448 | tf_op jit(solution)/shard_map/ppermute | solution.py:238
  80.6 18.9 %collective-permute-start.11 = (f32[8,5120]{1,0:T(8,128)S(1)}, f32[8,5120]{1,0:T(8,128)S(1)}, u32[]{:S(2)}, u32[]{:S(2)}) collective-permute-start(f32[8,5120]{1,0:T(8,128)S(1)} %get-tuple-element.37), channel_id=1, source_target_pairs={{0,12},{1,13},{2,14},{3,15},{4,8},{5,9},{6,10},{7,11},{8,4},{9,5},... | collective-permute-start | bytes 491528 | tf_op jit(solution)/shard_map/ppermute | solution.py:234
  88.2 9.9 %collective-permute-start.12 = (f32[8,640]{1,0:T(8,128)S(1)}, f32[8,640]{1,0:T(8,128)S(1)}, u32[]{:S(2)}, u32[]{:S(2)}) collective-permute-start(f32[8,640]{1,0:T(8,128)S(1)} %add.90.own_ref), channel_id=1, source_target_pairs={{0,256},{16,272},{32,288},{48,304},{64,320},{80,336},{96,352},{112... | collective-permute-start | bytes 61448 | tf_op jit(solution)/shard_map/ppermute | solution.py:238

commit v3 on v2

--- a/solution.py
+++ b/solution.py
@@ -48,6 +48,13 @@
     return jnp.where(row // SPAN == col // KEEP, tall, 0.0)
 
 
+def row_order():
+    r = lax.broadcasted_iota(jnp.int32, (128, 128), 0)
+    col = lax.broadcasted_iota(jnp.int32, (128, 128), 1)
+    source = ((r // 4) % 2) * 64 + ((r // OWN) % 4) * 16 + (r // (4 * OWN)) * 4 + r % 4
+    return (source == col).astype(jnp.float32).astype(jnp.bfloat16)
+
+
 def slot_order():
     y, z = lax.axis_index("fsdp") % 4, lax.axis_index("fsdp") // 4
     near = 1 + 2 * (lax.axis_index("dp") % 2)
@@ -64,7 +71,7 @@
     return (source == col).astype(jnp.float32).astype(jnp.bfloat16)
 
 
-def coef_kernel(indices_ref, grad_ref, kept_out_ref, sent_ref, kept_ref, held, sems):
+def coef_kernel(indices_ref, grad_ref, coef_ref, kept_ref, held, sems):
     indices = pltpu.make_async_copy(indices_ref, kept_ref, sems.at[CHUNKS])
     indices.start()
 
@@ -74,7 +81,7 @@
 
     for c in range(CHUNKS):
         chunk(c).start()
-    order = slot_order()
+    order = row_order()
     indices.wait()
     picked = picked_t(kept_ref)
     high = picked.astype(jnp.bfloat16).astype(jnp.float32)
@@ -86,19 +93,17 @@
         exact = jnp.dot(order, values, preferred_element_type=jnp.float32).astype(jnp.bfloat16)
         coef = jnp.dot(exact, wide_hi, preferred_element_type=jnp.float32)
         coef = coef + jnp.dot(exact, wide_lo, preferred_element_type=jnp.float32)
-        kept_out_ref[:, :, :, c * 128:(c + 1) * 128] = coef[:64].reshape(2, 4, OWN, 128)
-        sent_ref[:, :, :, c * 128:(c + 1) * 128] = coef[64:].reshape(2, 4, OWN, 128)
+        coef_ref[:, :, :, c * 128:(c + 1) * 128] = coef.reshape(4, 4, OWN, 128)
 
 
 def coef_of(kept, grad):
     hbm = pl.BlockSpec(memory_space=pltpu.HBM)
     vmem = pl.BlockSpec(memory_space=pltpu.VMEM)
-    half = jax.ShapeDtypeStruct((2, 4, OWN, COEFFS), jnp.float32)
     return pl.pallas_call(
         coef_kernel,
-        out_shape=(half, half),
+        out_shape=jax.ShapeDtypeStruct((4, 4, OWN, COEFFS), jnp.float32),
         in_specs=[hbm, hbm],
-        out_specs=(vmem, vmem),
+        out_specs=vmem,
         scratch_shapes=[
             pltpu.SMEM(kept.shape, kept.dtype),
             pltpu.VMEM(grad.shape, grad.dtype),
@@ -194,8 +199,8 @@
     )(own, got, momentum, reject)
 
 
-def params_kernel(own_ref, got_ref, params_ref, expand_ref, out_ref):
-    shared = (own_ref[...] + got_ref[...]) * (1.0 / N_DP)
+def params_kernel(total_ref, params_ref, expand_ref, out_ref):
+    shared = total_ref[...] * (1.0 / N_DP)
     deep = tall(shared)
     update = lax.dot_general(
         deep, expand_ref[...], (((1,), (1,)), ((), ())), precision=HIGHEST, preferred_element_type=jnp.float32
@@ -207,17 +212,17 @@
         out_ref[1, :, lanes] = params_ref[1, :, lanes] - part[4:]
 
 
-def new_params_of(own, got, params, expand):
+def new_params_of(total, params, expand):
     vmem = pl.BlockSpec(memory_space=pltpu.VMEM)
     return pl.pallas_call(
         params_kernel,
         out_shape=jax.ShapeDtypeStruct(params.shape, jnp.float32),
-        in_specs=[vmem] * 4,
+        in_specs=[vmem] * 3,
         out_specs=vmem,
         compiler_params=pltpu.CompilerParams(vmem_limit_bytes=32 * 2**20),
         cost_estimate=pl.CostEstimate(flops=60_000_000, bytes_accessed=700_000, transcendentals=0),
         name="params",
-    )(own, got, params, expand)
+    )(total, params, expand)
 
 
 def sum_pairs(step, axis):
@@ -234,8 +239,18 @@
     return lax.ppermute(x, BOTH, sum_pairs(step, axis))
 
 
-def dp_swap(x, flip):
-    return lax.ppermute(x, "dp", [(d, d ^ flip) for d in range(N_DP)])
+def sum_over(x, axis, groups):
+    return jnp.sum(lax.all_to_all(x, axis, 0, 0, tiled=True, axis_index_groups=groups), axis=0)
+
+
+def share(x, groups):
+    return sum_over(jnp.broadcast_to(x, (len(groups[0]), *x.shape)), "dp", groups)
+
+
+Y_GROUPS = [[z * 4 + y for y in range(4)] for z in range(4)]
+Z_GROUPS = [[z * 4 + y for z in range(4)] for y in range(4)]
+PLANE_GROUPS = [[z * 8 + i for i in range(8)] for z in range(4)]
+COLUMN_GROUPS = [[z * 8 + i for z in range(4)] for i in range(8)]
 
 
 def after(x, earlier):
@@ -244,33 +259,25 @@
 
 def shards(grad_partials, momentum, params, kept):
     grad = grad_partials[0, 0]
-    coef, coef_sent = coef_of(kept, grad)
     main, main_sent = main_of(grad)
+    main_got = halve(main_sent, 0, "y")
+    coef = coef_of(kept, grad)
     state_coef, reject, expand = state_of(kept, momentum)
-
-    coef_got = halve(coef_sent, 0, "y")
-    main_sent, coef_got = after(main_sent, coef_got)
-    main_got = halve(main_sent, 0, "y")
-    coef_last = halve(coef[1] + coef_got[1], 1, "y")
-    coef = coef[0] + coef_got[0] + coef_last
-    coef_got = halve(coef[2:], 0, "z")
-    main_got, coef_got = after(main_got, coef_got)
+    coef = sum_over(coef, "fsdp", Y_GROUPS)
+    main_got, coef = after(main_got, coef)
 
     main_last = halve(main[1] + main_got[1], 1, "y")
-    coef_last = halve(coef[1] + coef_got[1], 1, "z")
-    coef = coef[0] + coef_got[0] + coef_last + state_coef
-    coef = coef + dp_swap(coef, 1)
+    coef = sum_over(coef, "fsdp", Z_GROUPS) + state_coef
     main_last, coef = after(main_last, coef)
 
     main = main[0] + main_got[0] + main_last
     main_got = halve(main[2:], 0, "z")
-    for flip in (2, 6, 8):
-        coef = coef + dp_swap(coef, flip)
+    coef = share(coef, PLANE_GROUPS)
     main_got, coef = after(main_got, coef)
 
     main_last = halve(main[1] + main_got[1], 1, "z")
-    other = dp_swap(coef, 16)
-    new_params = new_params_of(coef, other, params, expand)
+    coef = share(coef, COLUMN_GROUPS)
+    new_params = new_params_of(coef, params, expand)
     main_last, new_params = after(main_last, new_params)
     new_momentum = new_momentum_of(main[0] + main_got[0], main_last, momentum, reject)
     return (new_params, new_momentum)

time: 101 us -> 106 us (1.050)
  the two profiles are of different devices: /device:TPU:6 before, /device:TPU:102 now
where the time goes in v3:
time: 106 us
  waiting for transfers between devices  32.7 us (31%)
  starting transfers between devices  32.1 us (30%)
  blocking collectives  28.1 us (27%)
  Pallas kernels  6.6 us (6%)
  other arithmetic  3.26 us (3%)
  local copies, waits for them, and re-layouts  2.01 us (2%)
    all_to_all x2, blocking collectives, sum_over(): lax.all_to_all(x, axis, 0, 0, tiled=True, axis_index_groups=groups)  28.1 us
    all_to_all x2, starting transfers between devices, sum_over(): lax.all_to_all(x, axis, 0, 0, tiled=True, axis_index_groups=groups)  21 us
    ppermute x4, waiting for transfers between devices, halve(): return lax.ppermute(x, BOTH, sum_pairs(step, axis))  20.5 us
    all_to_all x2, waiting for transfers between devices, sum_over(): lax.all_to_all(x, axis, 0, 0, tiled=True, axis_index_groups=groups)  12.3 us
    ppermute x4, starting transfers between devices, halve(): return lax.ppermute(x, BOTH, sum_pairs(step, axis))  11.2 us
    pallas_call x1, Pallas kernels, coef_of(): pl.pallas_call(coef_kernel, out_shape=jax.ShapeDtypeStruct((4, 4, OWN, CO...  2.8 us
  transfers between devices with their start and end apart: 6, of which 4 were waited for; matrix products, arithmetic and copies ran while one was open for 1% of the time, Pallas kernels for 5%

profile of v3, /device:TPU:102, one launch (start us, length us, event | category | flops | bytes accessed | tf_op | source)
XLA Modules:
  0.0 105.7 jit_solution(4096472028467357921)
XLA Ops:
  0.6 1.3 %copy-done = bf16[1,1,2,64,5120]{4,3,2,1,0:T(8,128)(2,1)S(1)} copy-done((bf16[1,1,2,64,5120]{4,3,2,1,0:T(8,128)(2,1)S(1)}, bf16[1,1,2,64,5120]{4,3,2,1,0:T(8,128)(2,1)}, u32[]{:S(2)}) %copy-start) | copy-done | bytes 1310744
  2.0 0.5 main.1
  2.5 3.5 %collective-permute-start = (f32[2,4,8,5120]{3,2,1,0:T(8,128)S(1)}, f32[2,4,8,5120]{3,2,1,0:T(8,128)}, u32[]{:S(2)}, u32[]{:S(2)}) collective-permute-start(f32[2,4,8,5120]{3,2,1,0:T(8,128)S(1)} %get-tuple-element.16), channel_id=1, source_target_pairs={{0,1},{1,0},{2,3},{3,2},{4,5},{5,4},{6,7},{7,6},{8,9},{9,8},{10,11... | collective-permute-start | bytes 3932168 | tf_op jit(solution)/shard_map/ppermute | solution.py:239
  6.0 2.8 %coef.1 = f32[4,4,8,640]{3,2,1,0:T(8,128)S(1)} custom-call(s32[8]{0:T(128)S(1)} %copy-done.4, bf16[2,64,5120]{2,1,0:T(8,128)(2,1)S(1)} %bitcast.10), custom_call_target="tpu_custom_call" | custom-call | flops 500000000 | bytes 2000000 | tf_op jit(solution)/shard_map/coef/pallas_call | solution.py:102
  8.8 19.1 %all_to_all.20 = f32[4,4,8,640]{3,2,1,0:T(8,128)S(1)} all-to-all(f32[4,4,8,640]{3,2,1,0:T(8,128)S(1)} %coef.1), channel_id=1, replica_groups={{0,1,2,3},{4,5,6,7},{8,9,10,11},{12,13,14,15},{16,17,18,19},{20,21,22,2..., dimensions={0} | all-to-all | bytes 655360 | tf_op jit(solution)/shard_map/all_to_all | solution.py:243
  27.9 0.7 reduce_sum.36
  28.6 0.0 collective-permute-done
  28.6 1.2 %add_bitcast_fusion = f32[4,8,5120]{2,1,0:T(8,128)S(1)} fusion(f32[2,4,8,5120]{3,2,1,0:T(8,128)} %collective-permute-done, f32[2,4,8,5120]{3,2,1,0:T(8,128)S(1)} %get-tuple-element.15), kind=kLoop, calls=%fused_computation.1 | loop fusion | flops 163840 | bytes 1966080 | tf_op jit(solution)/shard_map/add | solution.py:269
  29.7 2.3 %collective-permute-start.1 = (f32[4,8,5120]{2,1,0:T(8,128)S(1)}, f32[4,8,5120]{2,1,0:T(8,128)}, u32[]{:S(2)}, u32[]{:S(2)}) collective-permute-start(f32[4,8,5120]{2,1,0:T(8,128)S(1)} %add_bitcast_fusion), channel_id=1, source_target_pairs={{0,3},{1,2},{2,1},{3,0},{4,7},{5,6},{6,5},{7,4},{8,11},{9,10},{10,... | collective-permute-start | bytes 1966088 | tf_op jit(solution)/shard_map/ppermute | solution.py:239
  32.0 12.4 %all-to-all-start.1 = ((f32[4,8,640]{2,1,0:T(8,128)}), f32[4,8,640]{2,1,0:T(8,128)S(1)}, u32[]{:S(2)}, u32[]{:S(2)}) async-start(f32[4,8,640]{2,1,0:T(8,128)} %reduce_sum.36), calls=%async_computation.1 | async-start | bytes 163840 | tf_op jit(solution)/shard_map/all_to_all | solution.py:243
  44.5 1.1 %state.1 = (f32[8,640]{1,0:T(8,128)S(1)}, f32[128,128]{1,0:T(8,128)S(1)}, f32[1024,128]{1,0:T(8,128)S(1)}) custom-call(s32[8]{0:T(128)S(1)} %copy-done.4, f32[1,2,4,5120]{3,2,1,0:T(4,128)S(1)} %copy-done.3), custom_call_target="tpu_custom_call" | custom-call | flops 100000000 | bytes 1000000 | tf_op jit(solution)/shard_map/state/pallas_call | solution.py:164
  45.5 12.0 %all-to-all-done.1 = f32[4,8,640]{2,1,0:T(8,128)S(1)} async-done(((f32[4,8,640]{2,1,0:T(8,128)}), f32[4,8,640]{2,1,0:T(8,128)S(1)}, u32[]{:S(2)}, u32[]{:S(2)}) %all-to-all-start.1) | async-done | bytes 81952 | tf_op jit(solution)/shard_map/all_to_all | solution.py:243
  57.5 1.4 %bitcast_add_fusion = f32[4,8,5120]{2,1,0:T(8,128)S(1)} fusion(f32[4,8,5120]{2,1,0:T(8,128)} %collective-permute-done.1, f32[2,4,8,5120]{3,2,1,0:T(8,128)} %collective-permute-done, f32[2,4,8,5120]{3,2,1,0:T(8,128)S(1)} %get-tuple-element.15), kind=kLoop, calls=%fused_computation | loop fusion | flops 327680 | bytes 2621440 | tf_op jit(solution)/shard_map/add | solution.py:273
  58.9 0.0 copy-start.2
  59.0 2.7 %collective-permute-start.2 = (f32[2,8,5120]{2,1,0:T(8,128)S(1)}, f32[2,8,5120]{2,1,0:T(8,128)S(1)}, u32[]{:S(2)}, u32[]{:S(2)}) collective-permute-start(f32[2,8,5120]{2,1,0:T(8,128)S(1)} %slice.37), channel_id=1, source_target_pairs={{0,4},{1,5},{2,6},{3,7},{4,0},{5,1},{6,2},{7,3},{8,12},{9,13},{10,... | collective-permute-start | bytes 983048 | tf_op jit(solution)/shard_map/ppermute | solution.py:239
  61.7 9.0 %all_to_all.21 = f32[8,8,640]{2,1,0:T(8,128)S(1)} all-to-all(f32[8,8,640]{2,1,0:T(8,128)S(1)} %broadcast_in_dim.6), channel_id=1, replica_groups={{0,16,32,48,64,80,96,112},{128,144,160,176,192,208,224,240},{256,272,28..., dimensions={0} | all-to-all | bytes 327680 | tf_op jit(solution)/shard_map/all_to_all | solution.py:243
  70.7 8.4 %collective-permute-done.2 = f32[2,8,5120]{2,1,0:T(8,128)S(1)} collective-permute-done((f32[2,8,5120]{2,1,0:T(8,128)S(1)}, f32[2,8,5120]{2,1,0:T(8,128)S(1)}, u32[]{:S(2)}, u32[]{:S(2)}) %collective-permute-start.2) | collective-permute-done | bytes 327712 | tf_op jit(solution)/shard_map/ppermute | solution.py:239
  79.1 0.6 broadcast_in_dim.7
  79.8 8.6 %all-to-all-start.3 = ((f32[4,8,640]{2,1,0:T(8,128)}), f32[4,8,640]{2,1,0:T(8,128)S(1)}, u32[]{:S(2)}, u32[]{:S(2)}) async-start(f32[4,8,640]{2,1,0:T(8,128)} %broadcast_in_dim.7), calls=%async_computation.3 | async-start | bytes 163840 | tf_op jit(solution)/shard_map/all_to_all | solution.py:243
  88.4 2.7 %collective-permute-start.3 = (f32[8,5120]{1,0:T(8,128)S(1)}, f32[8,5120]{1,0:T(8,128)S(1)}, u32[]{:S(2)}, u32[]{:S(2)}) collective-permute-start(f32[8,5120]{1,0:T(8,128)S(1)} %get-tuple-element.29), channel_id=1, source_target_pairs={{0,12},{1,13},{2,14},{3,15},{4,8},{5,9},{6,10},{7,11},{8,4},{9,5},... | collective-permute-start | bytes 491528 | tf_op jit(solution)/shard_map/ppermute | solution.py:239
  91.1 0.3 all-to-all-done.3
  91.4 1.3 %params.1 = f32[2,4,5120]{2,1,0:T(4,128)} custom-call(f32[8,640]{1,0:T(8,128)S(1)} %reduce_sum.39.total_ref, f32[2,4,5120]{2,1,0:T(4,128)S(1)} %copy-done.2, f32[1024,128]{1,0:T(8,128)S(1)} %get-tuple-element.24.expand_ref), custom_call_target="tpu_custom_call" | custom-call | flops 60000000 | bytes 700000 | tf_op jit(solution)/shard_map/params/pallas_call | solution.py:217
  92.7 12.0 %collective-permute-done.3.got_ref = f32[8,5120]{1,0:T(8,128)S(1)} collective-permute-done((f32[8,5120]{1,0:T(8,128)S(1)}, f32[8,5120]{1,0:T(8,128)S(1)}, u32[]{:S(2)}, u32[]{:S(2)}) %collective-permute-start.3) | collective-permute-done | bytes 163872 | tf_op jit(solution)/shard_map/ppermute | solution.py:239
  104.7 1.0 momentum.1
  (16 shorter events, 0.1 us)
Async XLA Ops:
  0.6 5.3 %copy-start.4 = (s32[8]{0:T(128)S(1)}, s32[8]{0:T(128)}, u32[]{:S(2)}) copy-start(s32[8]{0:T(128)} %kept_ref.1) | copy-start | bytes 100
  0.6 1.3 %copy-start = (bf16[1,1,2,64,5120]{4,3,2,1,0:T(8,128)(2,1)S(1)}, bf16[1,1,2,64,5120]{4,3,2,1,0:T(8,128)(2,1)}, u32[]{:S(2)}) copy-start(bf16[1,1,2,64,5120]{4,3,2,1,0:T(8,128)(2,1)} %param.4) | copy-start | bytes 3932164
  2.0 4.0 %copy-start.1 = (bf16[1,1,2,64,5120]{4,3,2,1,0:T(8,128)(2,1)S(1)}, bf16[1,1,2,64,5120]{4,3,2,1,0:T(8,128)(2,1)}, u32[]{:S(2)}) copy-start(bf16[1,1,2,64,5120]{4,3,2,1,0:T(8,128)(2,1)} %param.4) | copy-start | bytes 3932164
  2.5 26.1 %collective-permute-start = (f32[2,4,8,5120]{3,2,1,0:T(8,128)S(1)}, f32[2,4,8,5120]{3,2,1,0:T(8,128)}, u32[]{:S(2)}, u32[]{:S(2)}) collective-permute-start(f32[2,4,8,5120]{3,2,1,0:T(8,128)S(1)} %get-tuple-element.16), channel_id=1, source_target_pairs={{0,1},{1,0},{2,3},{3,2},{4,5},{5,4},{6,7},{7,6},{8,9},{9,8},{10,11... | collective-permute-start | bytes 3932168 | tf_op jit(solution)/shard_map/ppermute | solution.py:239
  27.9 16.5 %copy-start.3 = (f32[1,2,4,5120]{3,2,1,0:T(4,128)S(1)}, f32[1,2,4,5120]{3,2,1,0:T(4,128)}, u32[]{:S(2)}) copy-start(f32[1,2,4,5120]{3,2,1,0:T(4,128)} %momentum_ref.3) | copy-start | bytes 491524
  29.7 27.8 %collective-permute-start.1 = (f32[4,8,5120]{2,1,0:T(8,128)S(1)}, f32[4,8,5120]{2,1,0:T(8,128)}, u32[]{:S(2)}, u32[]{:S(2)}) collective-permute-start(f32[4,8,5120]{2,1,0:T(8,128)S(1)} %add_bitcast_fusion), channel_id=1, source_target_pairs={{0,3},{1,2},{2,1},{3,0},{4,7},{5,6},{6,5},{7,4},{8,11},{9,10},{10,... | collective-permute-start | bytes 1966088 | tf_op jit(solution)/shard_map/ppermute | solution.py:239
  32.0 25.4 %all-to-all-start.1 = ((f32[4,8,640]{2,1,0:T(8,128)}), f32[4,8,640]{2,1,0:T(8,128)S(1)}, u32[]{:S(2)}, u32[]{:S(2)}) async-start(f32[4,8,640]{2,1,0:T(8,128)} %reduce_sum.36), calls=%async_computation.1 | async-start | bytes 163840 | tf_op jit(solution)/shard_map/all_to_all | solution.py:243
  58.9 32.5 %copy-start.2 = (f32[2,4,5120]{2,1,0:T(4,128)S(1)}, f32[2,4,5120]{2,1,0:T(4,128)}, u32[]{:S(2)}) copy-start(f32[2,4,5120]{2,1,0:T(4,128)} %params_ref.1) | copy-start | bytes 491524
  59.0 20.2 %collective-permute-start.2 = (f32[2,8,5120]{2,1,0:T(8,128)S(1)}, f32[2,8,5120]{2,1,0:T(8,128)S(1)}, u32[]{:S(2)}, u32[]{:S(2)}) collective-permute-start(f32[2,8,5120]{2,1,0:T(8,128)S(1)} %slice.37), channel_id=1, source_target_pairs={{0,4},{1,5},{2,6},{3,7},{4,0},{5,1},{6,2},{7,3},{8,12},{9,13},{10,... | collective-permute-start | bytes 983048 | tf_op jit(solution)/shard_map/ppermute | solution.py:239
  79.8 11.6 %all-to-all-start.3 = ((f32[4,8,640]{2,1,0:T(8,128)}), f32[4,8,640]{2,1,0:T(8,128)S(1)}, u32[]{:S(2)}, u32[]{:S(2)}) async-start(f32[4,8,640]{2,1,0:T(8,128)} %broadcast_in_dim.7), calls=%async_computation.3 | async-start | bytes 163840 | tf_op jit(solution)/shard_map/all_to_all | solution.py:243
  88.4 16.3 %collective-permute-start.3 = (f32[8,5120]{1,0:T(8,128)S(1)}, f32[8,5120]{1,0:T(8,128)S(1)}, u32[]{:S(2)}, u32[]{:S(2)}) collective-permute-start(f32[8,5120]{1,0:T(8,128)S(1)} %get-tuple-element.29), channel_id=1, source_target_pairs={{0,12},{1,13},{2,14},{3,15},{4,8},{5,9},{6,10},{7,11},{8,4},{9,5},... | collective-permute-start | bytes 491528 | tf_op jit(solution)/shard_map/ppermute | solution.py:239

commit v4 on v3

--- a/solution.py
+++ b/solution.py
@@ -16,6 +16,7 @@
 WIDE = GROUP * SPAN
 CHUNKS = ROW_VALS // WIDE
 COEFFS = ROW_VALS // SPAN * KEEP
+HEAD = 1280
 OWN = 8
 HIGHEST = lax.Precision.HIGHEST
 BOTH = ("dp", "fsdp")
@@ -48,13 +49,6 @@
     return jnp.where(row // SPAN == col // KEEP, tall, 0.0)
 
 
-def row_order():
-    r = lax.broadcasted_iota(jnp.int32, (128, 128), 0)
-    col = lax.broadcasted_iota(jnp.int32, (128, 128), 1)
-    source = ((r // 4) % 2) * 64 + ((r // OWN) % 4) * 16 + (r // (4 * OWN)) * 4 + r % 4
-    return (source == col).astype(jnp.float32).astype(jnp.bfloat16)
-
-
 def slot_order():
     y, z = lax.axis_index("fsdp") % 4, lax.axis_index("fsdp") // 4
     near = 1 + 2 * (lax.axis_index("dp") % 2)
@@ -71,71 +65,79 @@
     return (source == col).astype(jnp.float32).astype(jnp.bfloat16)
 
 
-def coef_kernel(indices_ref, grad_ref, coef_ref, kept_ref, held, sems):
-    indices = pltpu.make_async_copy(indices_ref, kept_ref, sems.at[CHUNKS])
-    indices.start()
-
+def first_kernel(indices_ref, grad_ref, rest_ref, sent_ref, kept_ref, held, sems):
     def chunk(c):
         lanes = pl.ds(c * WIDE, WIDE)
         return pltpu.make_async_copy(grad_ref.at[:, :, lanes], held.at[:, :, lanes], sems.at[c])
 
+    indices = pltpu.make_async_copy(indices_ref, kept_ref, sems.at[CHUNKS])
+    indices.start()
     for c in range(CHUNKS):
         chunk(c).start()
-    order = row_order()
+    order = slot_order()
     indices.wait()
     picked = picked_t(kept_ref)
     high = picked.astype(jnp.bfloat16).astype(jnp.float32)
-    wide_hi = spread(high).astype(jnp.bfloat16)
-    wide_lo = spread(picked - high).astype(jnp.bfloat16)
+    wide = jnp.concatenate([spread(high), spread(picked - high)], axis=1).astype(jnp.bfloat16)
+
+    def put(lanes, rows):
+        rest_ref[:, :, :, lanes] = rows[:64].reshape(2, 4, OWN, rows.shape[1])
+        sent_ref[:, :, :, lanes] = rows[64:].reshape(2, 4, OWN, rows.shape[1])
+
     for c in range(CHUNKS):
         chunk(c).wait()
         values = held[:, :, c * WIDE:(c + 1) * WIDE].reshape(128, WIDE)
-        exact = jnp.dot(order, values, preferred_element_type=jnp.float32).astype(jnp.bfloat16)
-        coef = jnp.dot(exact, wide_hi, preferred_element_type=jnp.float32)
-        coef = coef + jnp.dot(exact, wide_lo, preferred_element_type=jnp.float32)
-        coef_ref[:, :, :, c * 128:(c + 1) * 128] = coef.reshape(4, 4, OWN, 128)
-
-
-def coef_of(kept, grad):
+        rows = jnp.dot(order, values, preferred_element_type=jnp.float32)
+        coef = jnp.dot(rows.astype(jnp.bfloat16), wide, preferred_element_type=jnp.float32)
+        put(slice(c * 128, (c + 1) * 128), coef[:, :128] + coef[:, 128:])
+        head = min(HEAD - c * WIDE, WIDE)
+        if head > 0:
+            put(slice(COEFFS + c * WIDE, COEFFS + c * WIDE + head), rows[:, :head])
+
+
+def first_of(kept, grad):
     hbm = pl.BlockSpec(memory_space=pltpu.HBM)
     vmem = pl.BlockSpec(memory_space=pltpu.VMEM)
-    return pl.pallas_call(
-        coef_kernel,
-        out_shape=jax.ShapeDtypeStruct((4, 4, OWN, COEFFS), jnp.float32),
+    half = jax.ShapeDtypeStruct((2, 4, OWN, COEFFS + HEAD), jnp.float32)
+    return pl.pallas_call(
+        first_kernel,
+        out_shape=(half, half),
         in_specs=[hbm, hbm],
-        out_specs=vmem,
+        out_specs=(vmem, vmem),
         scratch_shapes=[
             pltpu.SMEM(kept.shape, kept.dtype),
             pltpu.VMEM(grad.shape, grad.dtype),
             pltpu.SemaphoreType.DMA((CHUNKS + 1,)),
         ],
         compiler_params=pltpu.CompilerParams(vmem_limit_bytes=32 * 2**20),
-        cost_estimate=pl.CostEstimate(flops=500_000_000, bytes_accessed=2_000_000, transcendentals=0),
-        name="coef",
+        cost_estimate=pl.CostEstimate(flops=500_000_000, bytes_accessed=3_000_000, transcendentals=0),
+        name="first",
     )(kept, grad)
 
 
-def main_kernel(grad_ref, kept_ref, sent_ref):
+def second_kernel(grad_ref, rest_ref, sent_ref):
     order = slot_order()
-    for c in range(CHUNKS):
-        lanes = slice(c * WIDE, (c + 1) * WIDE)
-        values = grad_ref[:, :, lanes].reshape(128, WIDE)
+    for start in range(HEAD, ROW_VALS, WIDE):
+        lanes = slice(start, min(start + WIDE, ROW_VALS))
+        width = lanes.stop - lanes.start
+        values = grad_ref[:, :, lanes].reshape(128, width)
         rows = jnp.dot(order, values, preferred_element_type=jnp.float32)
-        kept_ref[:, :, :, lanes] = rows[:64].reshape(2, 4, OWN, WIDE)
-        sent_ref[:, :, :, lanes] = rows[64:].reshape(2, 4, OWN, WIDE)
-
-
-def main_of(grad):
-    vmem = pl.BlockSpec(memory_space=pltpu.VMEM)
-    half = jax.ShapeDtypeStruct((2, 4, OWN, ROW_VALS), jnp.float32)
-    return pl.pallas_call(
-        main_kernel,
+        at = slice(start - HEAD, start - HEAD + width)
+        rest_ref[:, :, :, at] = rows[:64].reshape(2, 4, OWN, width)
+        sent_ref[:, :, :, at] = rows[64:].reshape(2, 4, OWN, width)
+
+
+def second_of(grad):
+    vmem = pl.BlockSpec(memory_space=pltpu.VMEM)
+    half = jax.ShapeDtypeStruct((2, 4, OWN, ROW_VALS - HEAD), jnp.float32)
+    return pl.pallas_call(
+        second_kernel,
         out_shape=(half, half),
         in_specs=[vmem],
         out_specs=(vmem, vmem),
         compiler_params=pltpu.CompilerParams(vmem_limit_bytes=32 * 2**20),
         cost_estimate=pl.CostEstimate(flops=200_000_000, bytes_accessed=4_000_000, transcendentals=0),
-        name="main",
+        name="second",
     )(grad)
 
 
@@ -176,9 +178,11 @@
     )(kept, momentum)
 
 
-def momentum_kernel(own_ref, got_ref, momentum_ref, reject_ref, out_ref):
+def momentum_kernel(own1_ref, got1_ref, own2_ref, got2_ref, momentum_ref, reject_ref, out_ref):
     state = jnp.concatenate([momentum_ref[0, 0], momentum_ref[0, 1]], axis=0)
-    moment = 0.9 * state + (own_ref[...] + got_ref[...])
+    head = own1_ref[:, COEFFS:] + got1_ref[:, COEFFS:]
+    grad = jnp.concatenate([head, own2_ref[...] + got2_ref[...]], axis=1)
+    moment = 0.9 * state + grad
     new = jnp.dot(tall(moment), reject_ref[...], precision=HIGHEST, preferred_element_type=jnp.float32)
     for c in range(ROW_VALS // 128):
         part = new[c * OWN:(c + 1) * OWN]
@@ -186,17 +190,17 @@
         out_ref[0, 1, :, c * 128:(c + 1) * 128] = part[4:]
 
 
-def new_momentum_of(own, got, momentum, reject):
+def new_momentum_of(first, second, momentum, reject):
     vmem = pl.BlockSpec(memory_space=pltpu.VMEM)
     return pl.pallas_call(
         momentum_kernel,
         out_shape=jax.ShapeDtypeStruct(momentum.shape, jnp.float32),
-        in_specs=[vmem] * 4,
+        in_specs=[vmem] * 6,
         out_specs=vmem,
         compiler_params=pltpu.CompilerParams(vmem_limit_bytes=32 * 2**20),
         cost_estimate=pl.CostEstimate(flops=60_000_000, bytes_accessed=700_000, transcendentals=0),
         name="momentum",
-    )(own, got, momentum, reject)
+    )(*first, *second, momentum, reject)
 
 
 def params_kernel(total_ref, params_ref, expand_ref, out_ref):
@@ -247,8 +251,6 @@
     return sum_over(jnp.broadcast_to(x, (len(groups[0]), *x.shape)), "dp", groups)
 
 
-Y_GROUPS = [[z * 4 + y for y in range(4)] for z in range(4)]
-Z_GROUPS = [[z * 4 + y for z in range(4)] for y in range(4)]
 PLANE_GROUPS = [[z * 8 + i for i in range(8)] for z in range(4)]
 COLUMN_GROUPS = [[z * 8 + i for z in range(4)] for i in range(8)]
 
@@ -259,27 +261,35 @@
 
 def shards(grad_partials, momentum, params, kept):
     grad = grad_partials[0, 0]
-    main, main_sent = main_of(grad)
-    main_got = halve(main_sent, 0, "y")
-    coef = coef_of(kept, grad)
+    rest1, sent1 = first_of(kept, grad)
+    rest2, sent2 = second_of(grad)
     state_coef, reject, expand = state_of(kept, momentum)
-    coef = sum_over(coef, "fsdp", Y_GROUPS)
-    main_got, coef = after(main_got, coef)
-
-    main_last = halve(main[1] + main_got[1], 1, "y")
-    coef = sum_over(coef, "fsdp", Z_GROUPS) + state_coef
-    main_last, coef = after(main_last, coef)
-
-    main = main[0] + main_got[0] + main_last
-    main_got = halve(main[2:], 0, "z")
+
+    got1 = halve(sent1, 0, "y")
+    got2 = halve(sent2, 0, "y")
+    next1 = rest1[1] + got1[1]
+    last1 = halve(next1, 1, "y")
+    got2, _ = after(got2, next1)
+    last2 = halve(rest2[1] + got2[1], 1, "y")
+
+    sum1 = rest1[0] + got1[0] + last1
+    got1 = halve(sum1[2:], 0, "z")
+    last2, _ = after(last2, sum1)
+    sum2 = rest2[0] + got2[0] + last2
+    got2 = halve(sum2[2:], 0, "z")
+    next1 = sum1[1] + got1[1]
+    last1 = halve(next1, 1, "z")
+    own1 = sum1[0] + got1[0]
+
+    coef = own1[:, :COEFFS] + last1[:, :COEFFS] + state_coef
     coef = share(coef, PLANE_GROUPS)
-    main_got, coef = after(main_got, coef)
-
-    main_last = halve(main[1] + main_got[1], 1, "z")
+    got2, coef = after(got2, coef)
+    last2 = halve(sum2[1] + got2[1], 1, "z")
+    own2 = sum2[0] + got2[0]
     coef = share(coef, COLUMN_GROUPS)
     new_params = new_params_of(coef, params, expand)
-    main_last, new_params = after(main_last, new_params)
-    new_momentum = new_momentum_of(main[0] + main_got[0], main_last, momentum, reject)
+    last2, new_params = after(last2, new_params)
+    new_momentum = new_momentum_of((own1, last1), (own2, last2), momentum, reject)
     return (new_params, new_momentum)
 
 

time: 106 us -> 97.6 us (0.921)
  the two profiles are of different devices: /device:TPU:102 before, /device:TPU:6 now
where the time goes in v4:
time: 97.6 us; the launch traced here: 95.6 us
  starting transfers between devices  53.8 us (55%)
  waiting for transfers between devices  22.7 us (23%)
  blocking collectives  8.99 us (9%)
  Pallas kernels  6.37 us (7%)
  local copies, waits for them, and re-layouts  2.66 us (3%)
    ppermute x8, starting transfers between devices, halve(): return lax.ppermute(x, BOTH, sum_pairs(step, axis))  44.9 us
    ppermute x8, waiting for transfers between devices, halve(): return lax.ppermute(x, BOTH, sum_pairs(step, axis))  19.2 us
    all_to_all x1, blocking collectives, sum_over(): lax.all_to_all(x, axis, 0, 0, tiled=True, axis_index_groups=groups)  8.99 us
    all_to_all x1, starting transfers between devices, sum_over(): lax.all_to_all(x, axis, 0, 0, tiled=True, axis_index_groups=groups)  8.88 us
    all_to_all x1, waiting for transfers between devices, sum_over(): lax.all_to_all(x, axis, 0, 0, tiled=True, axis_index_groups=groups)  3.53 us
    pallas_call x1, Pallas kernels, first_of(): pl.pallas_call(first_kernel, out_shape=(half, half), in_specs=[hbm, hbm],...  2.64 us
    unnamed x10, local copies, waits for them, and re-layouts  1.98 us
  transfers between devices with their start and end apart: 9, of which 5 were waited for; matrix products, arithmetic and copies ran while one was open for 0% of the time, Pallas kernels for 3%

profile of v4, /device:TPU:6, one launch (start us, length us, event | category | flops | bytes accessed | tf_op | source)
XLA Modules:
  0.0 95.6 jit_solution(5316508136341125268)
XLA Ops:
  0.6 1.3 %copy-done = bf16[1,1,2,64,5120]{4,3,2,1,0:T(8,128)(2,1)S(1)} copy-done((bf16[1,1,2,64,5120]{4,3,2,1,0:T(8,128)(2,1)S(1)}, bf16[1,1,2,64,5120]{4,3,2,1,0:T(8,128)(2,1)}, u32[]{:S(2)}) %copy-start) | copy-done | bytes 1310744
  1.9 0.7 copy-done.4
  2.6 2.6 %first.1 = (f32[2,4,8,1920]{3,2,1,0:T(8,128)S(1)}, f32[2,4,8,1920]{3,2,1,0:T(8,128)S(1)}) custom-call(s32[8]{0:T(128)S(1)} %copy-done.4, bf16[2,64,5120]{2,1,0:T(8,128)(2,1)S(1)} %bitcast.19), custom_call_target="tpu_custom_call" | custom-call | flops 500000000 | bytes 3000000 | tf_op jit(solution)/shard_map/first/pallas_call | solution.py:102
  5.3 3.5 %collective-permute-start.1 = (f32[2,4,8,1920]{3,2,1,0:T(8,128)S(1)}, f32[2,4,8,1920]{3,2,1,0:T(8,128)S(1)}, u32[]{:S(2)}, u32[]{:S(2)}) collective-permute-start(f32[2,4,8,1920]{3,2,1,0:T(8,128)S(1)} %get-tuple-element.18), channel_id=1, source_target_pairs={{0,1},{1,0},{2,3},{3,2},{4,5},{5,4},{6,7},{7,6},{8,9},{9,8},{10,11... | collective-permute-start | bytes 1474568 | tf_op jit(solution)/shard_map/ppermute | solution.py:243
  8.8 0.4 second.1
  9.2 2.4 %collective-permute-start = (f32[2,4,8,3840]{3,2,1,0:T(8,128)S(1)}, f32[2,4,8,3840]{3,2,1,0:T(8,128)S(1)}, u32[]{:S(2)}, u32[]{:S(2)}) collective-permute-start(f32[2,4,8,3840]{3,2,1,0:T(8,128)S(1)} %get-tuple-element.16), channel_id=1, source_target_pairs={{0,1},{1,0},{2,3},{3,2},{4,5},{5,4},{6,7},{7,6},{8,9},{9,8},{10,11... | collective-permute-start | bytes 2949128 | tf_op jit(solution)/shard_map/ppermute | solution.py:243
  11.5 4.4 %collective-permute-done.1 = f32[2,4,8,1920]{3,2,1,0:T(8,128)S(1)} collective-permute-done((f32[2,4,8,1920]{3,2,1,0:T(8,128)S(1)}, f32[2,4,8,1920]{3,2,1,0:T(8,128)S(1)}, u32[]{:S(2)}, u32[]{:S(2)}) %collective-permute-start.1) | collective-permute-done | bytes 491552 | tf_op jit(solution)/shard_map/ppermute | solution.py:243
  16.0 5.1 %collective-permute-start.3 = (f32[4,8,1920]{2,1,0:T(8,128)S(1)}, f32[4,8,1920]{2,1,0:T(8,128)S(1)}, u32[]{:S(2)}, u32[]{:S(2)}) collective-permute-start(f32[4,8,1920]{2,1,0:T(8,128)S(1)} %fusion.2), channel_id=1, source_target_pairs={{0,3},{1,2},{2,1},{3,0},{4,7},{5,6},{6,5},{7,4},{8,11},{9,10},{10,... | collective-permute-start | bytes 737288 | tf_op jit(solution)/shard_map/ppermute | solution.py:243
  21.1 7.1 %collective-permute-done.3 = f32[4,8,1920]{2,1,0:T(8,128)S(1)} collective-permute-done((f32[4,8,1920]{2,1,0:T(8,128)S(1)}, f32[4,8,1920]{2,1,0:T(8,128)S(1)}, u32[]{:S(2)}, u32[]{:S(2)}) %collective-permute-start.3) | collective-permute-done | bytes 245792 | tf_op jit(solution)/shard_map/ppermute | solution.py:243
  28.2 9.1 %collective-permute-start.5 = (f32[2,8,1920]{2,1,0:T(8,128)S(1)}, f32[2,8,1920]{2,1,0:T(8,128)S(1)}, u32[]{:S(2)}, u32[]{:S(2)}) collective-permute-start(f32[2,8,1920]{2,1,0:T(8,128)S(1)} %slice.85), channel_id=1, source_target_pairs={{0,4},{1,5},{2,6},{3,7},{4,0},{5,1},{6,2},{7,3},{8,12},{9,13},{10,... | collective-permute-start | bytes 368648 | tf_op jit(solution)/shard_map/ppermute | solution.py:243
  37.4 4.9 %collective-permute-start.2 = (f32[4,8,3840]{2,1,0:T(8,128)S(1)}, f32[4,8,3840]{2,1,0:T(8,128)S(1)}, u32[]{:S(2)}, u32[]{:S(2)}) collective-permute-start(f32[4,8,3840]{2,1,0:T(8,128)S(1)} %add_bitcast_fusion), channel_id=1, source_target_pairs={{0,3},{1,2},{2,1},{3,0},{4,7},{5,6},{6,5},{7,4},{8,11},{9,10},{10,... | collective-permute-start | bytes 1474568 | tf_op jit(solution)/shard_map/ppermute | solution.py:243
  42.3 1.1 %state.1 = (f32[8,640]{1,0:T(8,128)S(1)}, f32[128,128]{1,0:T(8,128)S(1)}, f32[1024,128]{1,0:T(8,128)S(1)}) custom-call(s32[8]{0:T(128)S(1)} %copy-done.4, f32[1,2,4,5120]{3,2,1,0:T(4,128)S(1)} %copy-done.3), custom_call_target="tpu_custom_call" | custom-call | flops 100000000 | bytes 1000000 | tf_op jit(solution)/shard_map/state/pallas_call | solution.py:166
  43.4 9.1 %collective-permute-start.6 = (f32[8,1920]{1,0:T(8,128)S(1)}, f32[8,1920]{1,0:T(8,128)S(1)}, u32[]{:S(2)}, u32[]{:S(2)}) collective-permute-start(f32[8,1920]{1,0:T(8,128)S(1)} %get-tuple-element.31), channel_id=1, source_target_pairs={{0,12},{1,13},{2,14},{3,15},{4,8},{5,9},{6,10},{7,11},{8,4},{9,5},... | collective-permute-start | bytes 184328 | tf_op jit(solution)/shard_map/ppermute | solution.py:243
  52.6 0.1 bitcast_add_fusion
  52.7 8.7 %collective-permute-start.4 = (f32[2,8,3840]{2,1,0:T(8,128)S(1)}, f32[2,8,3840]{2,1,0:T(8,128)S(1)}, u32[]{:S(2)}, u32[]{:S(2)}) collective-permute-start(f32[2,8,3840]{2,1,0:T(8,128)S(1)} %slice.83), channel_id=1, source_target_pairs={{0,4},{1,5},{2,6},{3,7},{4,0},{5,1},{6,2},{7,3},{8,12},{9,13},{10,... | collective-permute-start | bytes 737288 | tf_op jit(solution)/shard_map/ppermute | solution.py:243
  61.4 9.0 %all_to_all.10 = f32[8,8,640]{2,1,0:T(8,128)S(1)} all-to-all(f32[8,8,640]{2,1,0:T(8,128)S(1)} %broadcast_in_dim.6), channel_id=1, replica_groups={{0,16,32,48,64,80,96,112},{128,144,160,176,192,208,224,240},{256,272,28..., dimensions={0} | all-to-all | bytes 327680 | tf_op jit(solution)/shard_map/all_to_all | solution.py:247
  70.4 0.4 collective-permute-done.4
  70.8 0.6 broadcast_in_dim.7
  71.5 8.9 %all-to-all-start.1 = ((f32[4,8,640]{2,1,0:T(8,128)}), f32[4,8,640]{2,1,0:T(8,128)S(1)}, u32[]{:S(2)}, u32[]{:S(2)}) async-start(f32[4,8,640]{2,1,0:T(8,128)} %broadcast_in_dim.7), calls=%async_computation.1 | async-start | bytes 163840 | tf_op jit(solution)/shard_map/all_to_all | solution.py:247
  80.4 2.2 %collective-permute-start.7 = (f32[8,3840]{1,0:T(8,128)S(1)}, f32[8,3840]{1,0:T(8,128)S(1)}, u32[]{:S(2)}, u32[]{:S(2)}) collective-permute-start(f32[8,3840]{1,0:T(8,128)S(1)} %get-tuple-element.29), channel_id=1, source_target_pairs={{0,12},{1,13},{2,14},{3,15},{4,8},{5,9},{6,10},{7,11},{8,4},{9,5},... | collective-permute-start | bytes 368648 | tf_op jit(solution)/shard_map/ppermute | solution.py:243
  82.6 3.5 %all-to-all-done.1 = f32[4,8,640]{2,1,0:T(8,128)S(1)} async-done(((f32[4,8,640]{2,1,0:T(8,128)}), f32[4,8,640]{2,1,0:T(8,128)S(1)}, u32[]{:S(2)}, u32[]{:S(2)}) %all-to-all-start.1) | async-done | bytes 81952 | tf_op jit(solution)/shard_map/all_to_all | solution.py:247
  86.1 1.3 %params.1 = f32[2,4,5120]{2,1,0:T(4,128)} custom-call(f32[8,640]{1,0:T(8,128)S(1)} %reduce_sum.19.total_ref, f32[2,4,5120]{2,1,0:T(4,128)S(1)} %copy-done.2, f32[1024,128]{1,0:T(8,128)S(1)} %get-tuple-element.24.expand_ref), custom_call_target="tpu_custom_call" | custom-call | flops 60000000 | bytes 700000 | tf_op jit(solution)/shard_map/params/pallas_call | solution.py:221
  87.4 7.2 %collective-permute-done.7.got2_ref = f32[8,3840]{1,0:T(8,128)S(1)} collective-permute-done((f32[8,3840]{1,0:T(8,128)S(1)}, f32[8,3840]{1,0:T(8,128)S(1)}, u32[]{:S(2)}, u32[]{:S(2)}) %collective-permute-start.7) | collective-permute-done | bytes 122912 | tf_op jit(solution)/shard_map/ppermute | solution.py:243
  94.7 1.0 %momentum.1 = f32[1,2,4,5120]{3,2,1,0:T(4,128)} custom-call(f32[8,1920]{1,0:T(8,128)S(1)} %get-tuple-element.30.own1_ref, f32[8,1920]{1,0:T(8,128)S(1)} %collective-permute-done.6.got1_ref, f32[8,3840]{1,0:T(8,128)S(1)} %get-tuple-element.28.own2_ref, f32[8,3840]{1,0:T(8,128)S(1)} %collective-permute-done.7.got2_ref, f32[1,2,4,5120]{3,2,1,0:T(4,128)S(1)} %copy-done.3, ...), custom_call_target="tpu_custom_call" | custom-call | flops 60000000 | bytes 700000 | tf_op jit(solution)/shard_map/momentum/pallas_call | solution.py:195
  (23 shorter events, 0.3 us)
Async XLA Ops:
  0.6 1.3 %copy-start = (bf16[1,1,2,64,5120]{4,3,2,1,0:T(8,128)(2,1)S(1)}, bf16[1,1,2,64,5120]{4,3,2,1,0:T(8,128)(2,1)}, u32[]{:S(2)}) copy-start(bf16[1,1,2,64,5120]{4,3,2,1,0:T(8,128)(2,1)} %param.4) | copy-start | bytes 3932164
  1.9 0.7 copy-start.4
  2.6 6.1 %copy-start.1 = (bf16[1,1,2,64,5120]{4,3,2,1,0:T(8,128)(2,1)S(1)}, bf16[1,1,2,64,5120]{4,3,2,1,0:T(8,128)(2,1)}, u32[]{:S(2)}) copy-start(bf16[1,1,2,64,5120]{4,3,2,1,0:T(8,128)(2,1)} %param.4) | copy-start | bytes 3932164
  5.3 10.7 %collective-permute-start.1 = (f32[2,4,8,1920]{3,2,1,0:T(8,128)S(1)}, f32[2,4,8,1920]{3,2,1,0:T(8,128)S(1)}, u32[]{:S(2)}, u32[]{:S(2)}) collective-permute-start(f32[2,4,8,1920]{3,2,1,0:T(8,128)S(1)} %get-tuple-element.18), channel_id=1, source_target_pairs={{0,1},{1,0},{2,3},{3,2},{4,5},{5,4},{6,7},{7,6},{8,9},{9,8},{10,11... | collective-permute-start | bytes 1474568 | tf_op jit(solution)/shard_map/ppermute | solution.py:243
  9.2 28.2 %collective-permute-start = (f32[2,4,8,3840]{3,2,1,0:T(8,128)S(1)}, f32[2,4,8,3840]{3,2,1,0:T(8,128)S(1)}, u32[]{:S(2)}, u32[]{:S(2)}) collective-permute-start(f32[2,4,8,3840]{3,2,1,0:T(8,128)S(1)} %get-tuple-element.16), channel_id=1, source_target_pairs={{0,1},{1,0},{2,3},{3,2},{4,5},{5,4},{6,7},{7,6},{8,9},{9,8},{10,11... | collective-permute-start | bytes 2949128 | tf_op jit(solution)/shard_map/ppermute | solution.py:243
  16.0 26.3 %copy-start.3 = (f32[1,2,4,5120]{3,2,1,0:T(4,128)S(1)}, f32[1,2,4,5120]{3,2,1,0:T(4,128)}, u32[]{:S(2)}) copy-start(f32[1,2,4,5120]{3,2,1,0:T(4,128)} %momentum_ref.3) | copy-start | bytes 491524
  16.0 12.1 %collective-permute-start.3 = (f32[4,8,1920]{2,1,0:T(8,128)S(1)}, f32[4,8,1920]{2,1,0:T(8,128)S(1)}, u32[]{:S(2)}, u32[]{:S(2)}) collective-permute-start(f32[4,8,1920]{2,1,0:T(8,128)S(1)} %fusion.2), channel_id=1, source_target_pairs={{0,3},{1,2},{2,1},{3,0},{4,7},{5,6},{6,5},{7,4},{8,11},{9,10},{10,... | collective-permute-start | bytes 737288 | tf_op jit(solution)/shard_map/ppermute | solution.py:243
  28.2 15.2 %collective-permute-start.5 = (f32[2,8,1920]{2,1,0:T(8,128)S(1)}, f32[2,8,1920]{2,1,0:T(8,128)S(1)}, u32[]{:S(2)}, u32[]{:S(2)}) collective-permute-start(f32[2,8,1920]{2,1,0:T(8,128)S(1)} %slice.85), channel_id=1, source_target_pairs={{0,4},{1,5},{2,6},{3,7},{4,0},{5,1},{6,2},{7,3},{8,12},{9,13},{10,... | collective-permute-start | bytes 368648 | tf_op jit(solution)/shard_map/ppermute | solution.py:243
  37.4 15.1 %collective-permute-start.2 = (f32[4,8,3840]{2,1,0:T(8,128)S(1)}, f32[4,8,3840]{2,1,0:T(8,128)S(1)}, u32[]{:S(2)}, u32[]{:S(2)}) collective-permute-start(f32[4,8,3840]{2,1,0:T(8,128)S(1)} %add_bitcast_fusion), channel_id=1, source_target_pairs={{0,3},{1,2},{2,1},{3,0},{4,7},{5,6},{6,5},{7,4},{8,11},{9,10},{10,... | collective-permute-start | bytes 1474568 | tf_op jit(solution)/shard_map/ppermute | solution.py:243
  43.4 17.9 %collective-permute-start.6 = (f32[8,1920]{1,0:T(8,128)S(1)}, f32[8,1920]{1,0:T(8,128)S(1)}, u32[]{:S(2)}, u32[]{:S(2)}) collective-permute-start(f32[8,1920]{1,0:T(8,128)S(1)} %get-tuple-element.31), channel_id=1, source_target_pairs={{0,12},{1,13},{2,14},{3,15},{4,8},{5,9},{6,10},{7,11},{8,4},{9,5},... | collective-permute-start | bytes 184328 | tf_op jit(solution)/shard_map/ppermute | solution.py:243
  52.6 33.5 %copy-start.2 = (f32[2,4,5120]{2,1,0:T(4,128)S(1)}, f32[2,4,5120]{2,1,0:T(4,128)}, u32[]{:S(2)}) copy-start(f32[2,4,5120]{2,1,0:T(4,128)} %params_ref.1) | copy-start | bytes 491524
  52.7 18.1 %collective-permute-start.4 = (f32[2,8,3840]{2,1,0:T(8,128)S(1)}, f32[2,8,3840]{2,1,0:T(8,128)S(1)}, u32[]{:S(2)}, u32[]{:S(2)}) collective-permute-start(f32[2,8,3840]{2,1,0:T(8,128)S(1)} %slice.83), channel_id=1, source_target_pairs={{0,4},{1,5},{2,6},{3,7},{4,0},{5,1},{6,2},{7,3},{8,12},{9,13},{10,... | collective-permute-start | bytes 737288 | tf_op jit(solution)/shard_map/ppermute | solution.py:243
  71.5 14.7 %all-to-all-start.1 = ((f32[4,8,640]{2,1,0:T(8,128)}), f32[4,8,640]{2,1,0:T(8,128)S(1)}, u32[]{:S(2)}, u32[]{:S(2)}) async-start(f32[4,8,640]{2,1,0:T(8,128)} %broadcast_in_dim.7), calls=%async_computation.1 | async-start | bytes 163840 | tf_op jit(solution)/shard_map/all_to_all | solution.py:247
  80.4 14.3 %collective-permute-start.7 = (f32[8,3840]{1,0:T(8,128)S(1)}, f32[8,3840]{1,0:T(8,128)S(1)}, u32[]{:S(2)}, u32[]{:S(2)}) collective-permute-start(f32[8,3840]{1,0:T(8,128)S(1)} %get-tuple-element.29), channel_id=1, source_target_pairs={{0,12},{1,13},{2,14},{3,15},{4,8},{5,9},{6,10},{7,11},{8,4},{9,5},... | collective-permute-start | bytes 368648 | tf_op jit(solution)/shard_map/ppermute | solution.py:243

commit v5 on v3

--- a/solution.py
+++ b/solution.py
@@ -48,14 +48,7 @@
     return jnp.where(row // SPAN == col // KEEP, tall, 0.0)
 
 
-def row_order():
-    r = lax.broadcasted_iota(jnp.int32, (128, 128), 0)
-    col = lax.broadcasted_iota(jnp.int32, (128, 128), 1)
-    source = ((r // 4) % 2) * 64 + ((r // OWN) % 4) * 16 + (r // (4 * OWN)) * 4 + r % 4
-    return (source == col).astype(jnp.float32).astype(jnp.bfloat16)
-
-
-def slot_order():
+def row_order(by_slot):
     y, z = lax.axis_index("fsdp") % 4, lax.axis_index("fsdp") // 4
     near = 1 + 2 * (lax.axis_index("dp") % 2)
     far = 4 - near
@@ -65,63 +58,20 @@
     def partner(slot):
         return jnp.where(slot == 0, 0, jnp.where(slot == 1, far, jnp.where(slot == 2, near, 2)))
 
-    to_y = y ^ partner(r // (4 * OWN))
-    to_z = z ^ partner((r // OWN) % 4)
+    major, minor = r // (4 * OWN), (r // OWN) % 4
+    to_y = y ^ partner(major) if by_slot else minor
+    to_z = z ^ partner(minor if by_slot else major)
     source = ((r // 4) % 2) * 64 + to_z * 16 + to_y * 4 + r % 4
     return (source == col).astype(jnp.float32).astype(jnp.bfloat16)
 
 
-def coef_kernel(indices_ref, grad_ref, coef_ref, kept_ref, held, sems):
-    indices = pltpu.make_async_copy(indices_ref, kept_ref, sems.at[CHUNKS])
-    indices.start()
-
-    def chunk(c):
-        lanes = pl.ds(c * WIDE, WIDE)
-        return pltpu.make_async_copy(grad_ref.at[:, :, lanes], held.at[:, :, lanes], sems.at[c])
-
-    for c in range(CHUNKS):
-        chunk(c).start()
-    order = row_order()
-    indices.wait()
-    picked = picked_t(kept_ref)
-    high = picked.astype(jnp.bfloat16).astype(jnp.float32)
-    wide_hi = spread(high).astype(jnp.bfloat16)
-    wide_lo = spread(picked - high).astype(jnp.bfloat16)
-    for c in range(CHUNKS):
-        chunk(c).wait()
-        values = held[:, :, c * WIDE:(c + 1) * WIDE].reshape(128, WIDE)
-        exact = jnp.dot(order, values, preferred_element_type=jnp.float32).astype(jnp.bfloat16)
-        coef = jnp.dot(exact, wide_hi, preferred_element_type=jnp.float32)
-        coef = coef + jnp.dot(exact, wide_lo, preferred_element_type=jnp.float32)
-        coef_ref[:, :, :, c * 128:(c + 1) * 128] = coef.reshape(4, 4, OWN, 128)
-
-
-def coef_of(kept, grad):
-    hbm = pl.BlockSpec(memory_space=pltpu.HBM)
-    vmem = pl.BlockSpec(memory_space=pltpu.VMEM)
-    return pl.pallas_call(
-        coef_kernel,
-        out_shape=jax.ShapeDtypeStruct((4, 4, OWN, COEFFS), jnp.float32),
-        in_specs=[hbm, hbm],
-        out_specs=vmem,
-        scratch_shapes=[
-            pltpu.SMEM(kept.shape, kept.dtype),
-            pltpu.VMEM(grad.shape, grad.dtype),
-            pltpu.SemaphoreType.DMA((CHUNKS + 1,)),
-        ],
-        compiler_params=pltpu.CompilerParams(vmem_limit_bytes=32 * 2**20),
-        cost_estimate=pl.CostEstimate(flops=500_000_000, bytes_accessed=2_000_000, transcendentals=0),
-        name="coef",
-    )(kept, grad)
-
-
-def main_kernel(grad_ref, kept_ref, sent_ref):
-    order = slot_order()
+def main_kernel(grad_ref, rest_ref, sent_ref):
+    order = row_order(True)
     for c in range(CHUNKS):
         lanes = slice(c * WIDE, (c + 1) * WIDE)
         values = grad_ref[:, :, lanes].reshape(128, WIDE)
         rows = jnp.dot(order, values, preferred_element_type=jnp.float32)
-        kept_ref[:, :, :, lanes] = rows[:64].reshape(2, 4, OWN, WIDE)
+        rest_ref[:, :, :, lanes] = rows[:64].reshape(2, 4, OWN, WIDE)
         sent_ref[:, :, :, lanes] = rows[64:].reshape(2, 4, OWN, WIDE)
 
 
@@ -137,6 +87,35 @@
         cost_estimate=pl.CostEstimate(flops=200_000_000, bytes_accessed=4_000_000, transcendentals=0),
         name="main",
     )(grad)
+
+
+def coef_kernel(kept_ref, grad_ref, rest_ref, sent_ref):
+    order = row_order(False)
+    picked = picked_t(kept_ref)
+    high = picked.astype(jnp.bfloat16).astype(jnp.float32)
+    wide = jnp.concatenate([spread(high), spread(picked - high)], axis=1).astype(jnp.bfloat16)
+    for c in range(CHUNKS):
+        values = grad_ref[:, :, c * WIDE:(c + 1) * WIDE].reshape(128, WIDE)
+        rows = jnp.dot(order, values, preferred_element_type=jnp.float32).astype(jnp.bfloat16)
+        both = jnp.dot(rows, wide, preferred_element_type=jnp.float32)
+        coef = both[:, :128] + both[:, 128:]
+        lanes = slice(c * 128, (c + 1) * 128)
+        rest_ref[:, :, :, lanes] = coef[:64].reshape(2, 4, OWN, 128)
+        sent_ref[:, :, :, lanes] = coef[64:].reshape(2, 4, OWN, 128)
+
+
+def coef_of(kept, grad):
+    vmem = pl.BlockSpec(memory_space=pltpu.VMEM)
+    half = jax.ShapeDtypeStruct((2, 4, OWN, COEFFS), jnp.float32)
+    return pl.pallas_call(
+        coef_kernel,
+        out_shape=(half, half),
+        in_specs=[pl.BlockSpec(memory_space=pltpu.SMEM), vmem],
+        out_specs=(vmem, vmem),
+        compiler_params=pltpu.CompilerParams(vmem_limit_bytes=32 * 2**20),
+        cost_estimate=pl.CostEstimate(flops=500_000_000, bytes_accessed=2_000_000, transcendentals=0),
+        name="coef",
+    )(kept, grad)
 
 
 def tall(x):
@@ -248,7 +227,6 @@
 
 
 Y_GROUPS = [[z * 4 + y for y in range(4)] for z in range(4)]
-Z_GROUPS = [[z * 4 + y for z in range(4)] for y in range(4)]
 PLANE_GROUPS = [[z * 8 + i for i in range(8)] for z in range(4)]
 COLUMN_GROUPS = [[z * 8 + i for z in range(4)] for i in range(8)]
 
@@ -259,27 +237,31 @@
 
 def shards(grad_partials, momentum, params, kept):
     grad = grad_partials[0, 0]
-    main, main_sent = main_of(grad)
-    main_got = halve(main_sent, 0, "y")
-    coef = coef_of(kept, grad)
+    main, sent = main_of(grad)
+    got = halve(sent, 0, "y")
+    coef, coef_sent = coef_of(kept, grad)
     state_coef, reject, expand = state_of(kept, momentum)
-    coef = sum_over(coef, "fsdp", Y_GROUPS)
-    main_got, coef = after(main_got, coef)
-
-    main_last = halve(main[1] + main_got[1], 1, "y")
-    coef = sum_over(coef, "fsdp", Z_GROUPS) + state_coef
-    main_last, coef = after(main_last, coef)
-
-    main = main[0] + main_got[0] + main_last
-    main_got = halve(main[2:], 0, "z")
+
+    coef_got = halve(coef_sent, 0, "z")
+    coef_next = coef[1] + coef_got[1]
+    got, coef_next = after(got, coef_next)
+    last = halve(main[1] + got[1], 1, "y")
+
+    coef_last = halve(coef_next, 1, "z")
+    coef = coef[0] + coef_got[0] + coef_last
+    last, coef = after(last, coef)
+    main = main[0] + got[0] + last
+    got = halve(main[2:], 0, "z")
+
+    coef = sum_over(coef, "fsdp", Y_GROUPS) + state_coef
+    coef = share(coef, COLUMN_GROUPS)
+    got, coef = after(got, coef)
+    last = halve(main[1] + got[1], 1, "z")
+
     coef = share(coef, PLANE_GROUPS)
-    main_got, coef = after(main_got, coef)
-
-    main_last = halve(main[1] + main_got[1], 1, "z")
-    coef = share(coef, COLUMN_GROUPS)
     new_params = new_params_of(coef, params, expand)
-    main_last, new_params = after(main_last, new_params)
-    new_momentum = new_momentum_of(main[0] + main_got[0], main_last, momentum, reject)
+    last, new_params = after(last, new_params)
+    new_momentum = new_momentum_of(main[0] + got[0], last, momentum, reject)
     return (new_params, new_momentum)
 
 

time: 106 us -> 90.7 us (0.86)
  the two profiles are of different devices: /device:TPU:102 before, /device:TPU:1 now
where the time goes in v5:
time: 90.7 us; the launch traced here: 90.3 us
  starting transfers between devices  47.1 us (52%)
  blocking collectives  24.7 us (27%)
  waiting for transfers between devices  9.97 us (11%)
  Pallas kernels  5.33 us (6%)
  local copies, waits for them, and re-layouts  1.37 us (2%)
  other arithmetic  0.98 us (1%)
    ppermute x6, starting transfers between devices, halve(): return lax.ppermute(x, BOTH, sum_pairs(step, axis))  42.5 us
    all_to_all x2, blocking collectives, sum_over(): lax.all_to_all(x, axis, 0, 0, tiled=True, axis_index_groups=groups)  24.7 us
    ppermute x6, waiting for transfers between devices, halve(): return lax.ppermute(x, BOTH, sum_pairs(step, axis))  6.18 us
    all_to_all x1, starting transfers between devices, sum_over(): lax.all_to_all(x, axis, 0, 0, tiled=True, axis_index_groups=groups)  4.66 us
    all_to_all x1, waiting for transfers between devices, sum_over(): lax.all_to_all(x, axis, 0, 0, tiled=True, axis_index_groups=groups)  3.79 us
  transfers between devices with their start and end apart: 7, of which 3 were waited for; matrix products, arithmetic and copies ran while one was open for 1% of the time, Pallas kernels for 4%

profile of v5, /device:TPU:1, one launch (start us, length us, event | category | flops | bytes accessed | tf_op | source)
XLA Modules:
  0.0 90.3 jit_solution(14342191395911225011)
XLA Ops:
  0.6 1.3 %copy-done = bf16[1,1,2,64,5120]{4,3,2,1,0:T(8,128)(2,1)S(1)} copy-done((bf16[1,1,2,64,5120]{4,3,2,1,0:T(8,128)(2,1)S(1)}, bf16[1,1,2,64,5120]{4,3,2,1,0:T(8,128)(2,1)}, u32[]{:S(2)}) %copy-start) | copy-done | bytes 1310744
  2.0 0.5 main.1
  2.5 5.5 %collective-permute-start = (f32[2,4,8,5120]{3,2,1,0:T(8,128)S(1)}, f32[2,4,8,5120]{3,2,1,0:T(8,128)S(1)}, u32[]{:S(2)}, u32[]{:S(2)}) collective-permute-start(f32[2,4,8,5120]{3,2,1,0:T(8,128)S(1)} %get-tuple-element.18), channel_id=1, source_target_pairs={{0,1},{1,0},{2,3},{3,2},{4,5},{5,4},{6,7},{7,6},{8,9},{9,8},{10,11... | collective-permute-start | bytes 3932168 | tf_op jit(solution)/shard_map/ppermute | solution.py:218
  8.0 1.5 %coef.1 = (f32[2,4,8,640]{3,2,1,0:T(8,128)S(1)}, f32[2,4,8,640]{3,2,1,0:T(8,128)S(1)}) custom-call(s32[8]{0:T(128)S(1)} %copy-done.4, bf16[2,64,5120]{2,1,0:T(8,128)(2,1)S(1)} %bitcast.16), custom_call_target="tpu_custom_call" | custom-call | flops 500000000 | bytes 2000000 | tf_op jit(solution)/shard_map/coef/pallas_call | solution.py:110
  9.5 12.5 %collective-permute-start.1 = (f32[2,4,8,640]{3,2,1,0:T(8,128)S(1)}, f32[2,4,8,640]{3,2,1,0:T(8,128)S(1)}, u32[]{:S(2)}, u32[]{:S(2)}) collective-permute-start(f32[2,4,8,640]{3,2,1,0:T(8,128)S(1)} %get-tuple-element.20), channel_id=1, source_target_pairs={{0,4},{1,5},{2,6},{3,7},{4,0},{5,1},{6,2},{7,3},{8,12},{9,13},{10,... | collective-permute-start | bytes 491528 | tf_op jit(solution)/shard_map/ppermute | solution.py:218
  22.0 4.4 %collective-permute-done.1 = f32[2,4,8,640]{3,2,1,0:T(8,128)S(1)} collective-permute-done((f32[2,4,8,640]{3,2,1,0:T(8,128)S(1)}, f32[2,4,8,640]{3,2,1,0:T(8,128)S(1)}, u32[]{:S(2)}, u32[]{:S(2)}) %collective-permute-start.1) | collective-permute-done | bytes 163872 | tf_op jit(solution)/shard_map/ppermute | solution.py:218
  26.3 0.0 collective-permute-done
  26.3 0.1 add_bitcast_fusion
  26.4 2.0 %collective-permute-start.2 = (f32[4,8,5120]{2,1,0:T(8,128)S(1)}, f32[4,8,5120]{2,1,0:T(8,128)S(1)}, u32[]{:S(2)}, u32[]{:S(2)}) collective-permute-start(f32[4,8,5120]{2,1,0:T(8,128)S(1)} %add_bitcast_fusion), channel_id=1, source_target_pairs={{0,3},{1,2},{2,1},{3,0},{4,7},{5,6},{6,5},{7,4},{8,11},{9,10},{10,... | collective-permute-start | bytes 1966088 | tf_op jit(solution)/shard_map/ppermute | solution.py:218
  28.5 8.7 %collective-permute-start.3 = (f32[4,8,640]{2,1,0:T(8,128)S(1)}, f32[4,8,640]{2,1,0:T(8,128)S(1)}, u32[]{:S(2)}, u32[]{:S(2)}) collective-permute-start(f32[4,8,640]{2,1,0:T(8,128)S(1)} %fusion.4), channel_id=1, source_target_pairs={{0,12},{1,13},{2,14},{3,15},{4,8},{5,9},{6,10},{7,11},{8,4},{9,5},... | collective-permute-start | bytes 245768 | tf_op jit(solution)/shard_map/ppermute | solution.py:218
  37.2 1.8 %collective-permute-done.3 = f32[4,8,640]{2,1,0:T(8,128)S(1)} collective-permute-done((f32[4,8,640]{2,1,0:T(8,128)S(1)}, f32[4,8,640]{2,1,0:T(8,128)S(1)}, u32[]{:S(2)}, u32[]{:S(2)}) %collective-permute-start.3) | collective-permute-done | bytes 81952 | tf_op jit(solution)/shard_map/ppermute | solution.py:218
  39.0 0.6 fusion.3
  39.6 0.0 collective-permute-done.2
  39.6 0.1 bitcast_add_fusion
  39.8 8.4 %collective-permute-start.4 = (f32[2,8,5120]{2,1,0:T(8,128)S(1)}, f32[2,8,5120]{2,1,0:T(8,128)S(1)}, u32[]{:S(2)}, u32[]{:S(2)}) collective-permute-start(f32[2,8,5120]{2,1,0:T(8,128)S(1)} %slice.55), channel_id=1, source_target_pairs={{0,4},{1,5},{2,6},{3,7},{4,0},{5,1},{6,2},{7,3},{8,12},{9,13},{10,... | collective-permute-start | bytes 983048 | tf_op jit(solution)/shard_map/ppermute | solution.py:218
  48.2 4.7 %all-to-all-start = ((f32[4,8,640]{2,1,0:T(8,128)}), f32[4,8,640]{2,1,0:T(8,128)S(1)}, u32[]{:S(2)}, u32[]{:S(2)}) async-start(f32[4,8,640]{2,1,0:T(8,128)} %fusion.3), calls=%async_computation | async-start | bytes 163840 | tf_op jit(solution)/shard_map/all_to_all | solution.py:222
  52.9 1.1 %state.1 = (f32[8,640]{1,0:T(8,128)S(1)}, f32[128,128]{1,0:T(8,128)S(1)}, f32[1024,128]{1,0:T(8,128)S(1)}) custom-call(s32[8]{0:T(128)S(1)} %copy-done.4, f32[1,2,4,5120]{3,2,1,0:T(4,128)S(1)} %copy-done.3), custom_call_target="tpu_custom_call" | custom-call | flops 100000000 | bytes 1000000 | tf_op jit(solution)/shard_map/state/pallas_call | solution.py:143
  53.9 3.8 %all-to-all-done = f32[4,8,640]{2,1,0:T(8,128)S(1)} async-done(((f32[4,8,640]{2,1,0:T(8,128)}), f32[4,8,640]{2,1,0:T(8,128)S(1)}, u32[]{:S(2)}, u32[]{:S(2)}) %all-to-all-start) | async-done | bytes 81952 | tf_op jit(solution)/shard_map/all_to_all | solution.py:222
  57.8 10.1 %all_to_all.15 = f32[4,8,640]{2,1,0:T(8,128)S(1)} all-to-all(f32[4,8,640]{2,1,0:T(8,128)S(1)} %broadcast_in_dim.6), channel_id=1, replica_groups={{0,128,256,384},{16,144,272,400},{32,160,288,416},{48,176,304,432},{64,..., dimensions={0} | all-to-all | bytes 163840 | tf_op jit(solution)/shard_map/all_to_all | solution.py:222
  67.9 5.5 %collective-permute-start.5 = (f32[8,5120]{1,0:T(8,128)S(1)}, f32[8,5120]{1,0:T(8,128)S(1)}, u32[]{:S(2)}, u32[]{:S(2)}) collective-permute-start(f32[8,5120]{1,0:T(8,128)S(1)} %get-tuple-element.33), channel_id=1, source_target_pairs={{0,12},{1,13},{2,14},{3,15},{4,8},{5,9},{6,10},{7,11},{8,4},{9,5},... | collective-permute-start | bytes 491528 | tf_op jit(solution)/shard_map/ppermute | solution.py:218
  73.4 14.6 %all_to_all.16 = f32[8,8,640]{2,1,0:T(8,128)S(1)} all-to-all(f32[8,8,640]{2,1,0:T(8,128)S(1)} %broadcast_in_dim.7), channel_id=1, replica_groups={{0,16,32,48,64,80,96,112},{128,144,160,176,192,208,224,240},{256,272,28..., dimensions={0} | all-to-all | bytes 327680 | tf_op jit(solution)/shard_map/all_to_all | solution.py:222
  88.0 1.3 %params.1 = f32[2,4,5120]{2,1,0:T(4,128)} custom-call(f32[8,640]{1,0:T(8,128)S(1)} %reduce_sum.29.total_ref, f32[2,4,5120]{2,1,0:T(4,128)S(1)} %copy-done.2, f32[1024,128]{1,0:T(8,128)S(1)} %get-tuple-element.28.expand_ref), custom_call_target="tpu_custom_call" | custom-call | flops 60000000 | bytes 700000 | tf_op jit(solution)/shard_map/params/pallas_call | solution.py:196
  89.3 0.0 collective-permute-done.5.got_ref
  89.3 1.0 %momentum.1 = f32[1,2,4,5120]{3,2,1,0:T(4,128)} custom-call(f32[8,5120]{1,0:T(8,128)S(1)} %get-tuple-element.32.own_ref, f32[8,5120]{1,0:T(8,128)S(1)} %collective-permute-done.5.got_ref, f32[1,2,4,5120]{3,2,1,0:T(4,128)S(1)} %copy-done.3, f32[128,128]{1,0:T(8,128)S(1)} %get-tuple-element.31.reject_ref), custom_call_target="tpu_custom_call" | custom-call | flops 60000000 | bytes 700000 | tf_op jit(solution)/shard_map/momentum/pallas_call | solution.py:170
  (19 shorter events, 0.1 us)
Async XLA Ops:
  0.6 7.3 %copy-start.4 = (s32[8]{0:T(128)S(1)}, s32[8]{0:T(128)}, u32[]{:S(2)}) copy-start(s32[8]{0:T(128)} %kept_ref.3) | copy-start | bytes 100
  0.6 1.3 %copy-start = (bf16[1,1,2,64,5120]{4,3,2,1,0:T(8,128)(2,1)S(1)}, bf16[1,1,2,64,5120]{4,3,2,1,0:T(8,128)(2,1)}, u32[]{:S(2)}) copy-start(bf16[1,1,2,64,5120]{4,3,2,1,0:T(8,128)(2,1)} %param.4) | copy-start | bytes 3932164
  2.0 6.0 %copy-start.1 = (bf16[1,1,2,64,5120]{4,3,2,1,0:T(8,128)(2,1)S(1)}, bf16[1,1,2,64,5120]{4,3,2,1,0:T(8,128)(2,1)}, u32[]{:S(2)}) copy-start(bf16[1,1,2,64,5120]{4,3,2,1,0:T(8,128)(2,1)} %param.4) | copy-start | bytes 3932164
  2.5 23.9 %collective-permute-start = (f32[2,4,8,5120]{3,2,1,0:T(8,128)S(1)}, f32[2,4,8,5120]{3,2,1,0:T(8,128)S(1)}, u32[]{:S(2)}, u32[]{:S(2)}) collective-permute-start(f32[2,4,8,5120]{3,2,1,0:T(8,128)S(1)} %get-tuple-element.18), channel_id=1, source_target_pairs={{0,1},{1,0},{2,3},{3,2},{4,5},{5,4},{6,7},{7,6},{8,9},{9,8},{10,11... | collective-permute-start | bytes 3932168 | tf_op jit(solution)/shard_map/ppermute | solution.py:218
  9.5 16.8 %collective-permute-start.1 = (f32[2,4,8,640]{3,2,1,0:T(8,128)S(1)}, f32[2,4,8,640]{3,2,1,0:T(8,128)S(1)}, u32[]{:S(2)}, u32[]{:S(2)}) collective-permute-start(f32[2,4,8,640]{3,2,1,0:T(8,128)S(1)} %get-tuple-element.20), channel_id=1, source_target_pairs={{0,4},{1,5},{2,6},{3,7},{4,0},{5,1},{6,2},{7,3},{8,12},{9,13},{10,... | collective-permute-start | bytes 491528 | tf_op jit(solution)/shard_map/ppermute | solution.py:218
  26.4 13.2 %collective-permute-start.2 = (f32[4,8,5120]{2,1,0:T(8,128)S(1)}, f32[4,8,5120]{2,1,0:T(8,128)S(1)}, u32[]{:S(2)}, u32[]{:S(2)}) collective-permute-start(f32[4,8,5120]{2,1,0:T(8,128)S(1)} %add_bitcast_fusion), channel_id=1, source_target_pairs={{0,3},{1,2},{2,1},{3,0},{4,7},{5,6},{6,5},{7,4},{8,11},{9,10},{10,... | collective-permute-start | bytes 1966088 | tf_op jit(solution)/shard_map/ppermute | solution.py:218
  28.5 10.5 %collective-permute-start.3 = (f32[4,8,640]{2,1,0:T(8,128)S(1)}, f32[4,8,640]{2,1,0:T(8,128)S(1)}, u32[]{:S(2)}, u32[]{:S(2)}) collective-permute-start(f32[4,8,640]{2,1,0:T(8,128)S(1)} %fusion.4), channel_id=1, source_target_pairs={{0,12},{1,13},{2,14},{3,15},{4,8},{5,9},{6,10},{7,11},{8,4},{9,5},... | collective-permute-start | bytes 245768 | tf_op jit(solution)/shard_map/ppermute | solution.py:218
  39.6 13.2 %copy-start.3 = (f32[1,2,4,5120]{3,2,1,0:T(4,128)S(1)}, f32[1,2,4,5120]{3,2,1,0:T(4,128)}, u32[]{:S(2)}) copy-start(f32[1,2,4,5120]{3,2,1,0:T(4,128)} %momentum_ref.3) | copy-start | bytes 491524
  39.8 28.0 %collective-permute-start.4 = (f32[2,8,5120]{2,1,0:T(8,128)S(1)}, f32[2,8,5120]{2,1,0:T(8,128)S(1)}, u32[]{:S(2)}, u32[]{:S(2)}) collective-permute-start(f32[2,8,5120]{2,1,0:T(8,128)S(1)} %slice.55), channel_id=1, source_target_pairs={{0,4},{1,5},{2,6},{3,7},{4,0},{5,1},{6,2},{7,3},{8,12},{9,13},{10,... | collective-permute-start | bytes 983048 | tf_op jit(solution)/shard_map/ppermute | solution.py:218
  48.2 9.5 %all-to-all-start = ((f32[4,8,640]{2,1,0:T(8,128)}), f32[4,8,640]{2,1,0:T(8,128)S(1)}, u32[]{:S(2)}, u32[]{:S(2)}) async-start(f32[4,8,640]{2,1,0:T(8,128)} %fusion.3), calls=%async_computation | async-start | bytes 163840 | tf_op jit(solution)/shard_map/all_to_all | solution.py:222
  52.9 35.2 %copy-start.2 = (f32[2,4,5120]{2,1,0:T(4,128)S(1)}, f32[2,4,5120]{2,1,0:T(4,128)}, u32[]{:S(2)}) copy-start(f32[2,4,5120]{2,1,0:T(4,128)} %params_ref.1) | copy-start | bytes 491524
  67.9 21.4 %collective-permute-start.5 = (f32[8,5120]{1,0:T(8,128)S(1)}, f32[8,5120]{1,0:T(8,128)S(1)}, u32[]{:S(2)}, u32[]{:S(2)}) collective-permute-start(f32[8,5120]{1,0:T(8,128)S(1)} %get-tuple-element.33), channel_id=1, source_target_pairs={{0,12},{1,13},{2,14},{3,15},{4,8},{5,9},{6,10},{7,11},{8,4},{9,5},... | collective-permute-start | bytes 491528 | tf_op jit(solution)/shard_map/ppermute | solution.py:218

commit v6 on v5

--- a/solution.py
+++ b/solution.py
@@ -65,24 +65,26 @@
     return (source == col).astype(jnp.float32).astype(jnp.bfloat16)
 
 
-def main_kernel(grad_ref, rest_ref, sent_ref):
+def main_kernel(grad_ref, rest_ref, near_ref, across_ref):
     order = row_order(True)
     for c in range(CHUNKS):
         lanes = slice(c * WIDE, (c + 1) * WIDE)
         values = grad_ref[:, :, lanes].reshape(128, WIDE)
         rows = jnp.dot(order, values, preferred_element_type=jnp.float32)
         rest_ref[:, :, :, lanes] = rows[:64].reshape(2, 4, OWN, WIDE)
-        sent_ref[:, :, :, lanes] = rows[64:].reshape(2, 4, OWN, WIDE)
+        near_ref[:, :, lanes] = rows[64:96].reshape(4, OWN, WIDE)
+        across_ref[:, :, lanes] = rows[96:].reshape(4, OWN, WIDE)
 
 
 def main_of(grad):
     vmem = pl.BlockSpec(memory_space=pltpu.VMEM)
     half = jax.ShapeDtypeStruct((2, 4, OWN, ROW_VALS), jnp.float32)
+    quarter = jax.ShapeDtypeStruct((4, OWN, ROW_VALS), jnp.float32)
     return pl.pallas_call(
         main_kernel,
-        out_shape=(half, half),
+        out_shape=(half, quarter, quarter),
         in_specs=[vmem],
-        out_specs=(vmem, vmem),
+        out_specs=(vmem, vmem, vmem),
         compiler_params=pltpu.CompilerParams(vmem_limit_bytes=32 * 2**20),
         cost_estimate=pl.CostEstimate(flops=200_000_000, bytes_accessed=4_000_000, transcendentals=0),
         name="main",
@@ -178,8 +180,8 @@
     )(own, got, momentum, reject)
 
 
-def params_kernel(total_ref, params_ref, expand_ref, out_ref):
-    shared = total_ref[...] * (1.0 / N_DP)
+def params_kernel(parts_ref, params_ref, expand_ref, out_ref):
+    shared = jnp.sum(parts_ref[...], axis=0) * (1.0 / N_DP)
     deep = tall(shared)
     update = lax.dot_general(
         deep, expand_ref[...], (((1,), (1,)), ((), ())), precision=HIGHEST, preferred_element_type=jnp.float32
@@ -191,7 +193,7 @@
         out_ref[1, :, lanes] = params_ref[1, :, lanes] - part[4:]
 
 
-def new_params_of(total, params, expand):
+def new_params_of(parts, params, expand):
     vmem = pl.BlockSpec(memory_space=pltpu.VMEM)
     return pl.pallas_call(
         params_kernel,
@@ -201,7 +203,7 @@
         compiler_params=pltpu.CompilerParams(vmem_limit_bytes=32 * 2**20),
         cost_estimate=pl.CostEstimate(flops=60_000_000, bytes_accessed=700_000, transcendentals=0),
         name="params",
-    )(total, params, expand)
+    )(parts, params, expand)
 
 
 def sum_pairs(step, axis):
@@ -218,6 +220,14 @@
     return lax.ppermute(x, BOTH, sum_pairs(step, axis))
 
 
+def deal(x, axis, groups):
+    return lax.all_to_all(x, axis, 0, 0, tiled=True, axis_index_groups=groups)
+
+
+def share_parts(x, groups):
+    return deal(jnp.broadcast_to(x, (len(groups[0]), *x.shape)), "dp", groups)
+
+
 def sum_over(x, axis, groups):
     return jnp.sum(lax.all_to_all(x, axis, 0, 0, tiled=True, axis_index_groups=groups), axis=0)
 
@@ -237,31 +247,30 @@
 
 def shards(grad_partials, momentum, params, kept):
     grad = grad_partials[0, 0]
-    main, sent = main_of(grad)
-    got = halve(sent, 0, "y")
+    main, near, across = main_of(grad)
+    across = halve(across, 0, "y")
+    near = halve(near, 0, "y")
     coef, coef_sent = coef_of(kept, grad)
     state_coef, reject, expand = state_of(kept, momentum)
 
     coef_got = halve(coef_sent, 0, "z")
     coef_next = coef[1] + coef_got[1]
-    got, coef_next = after(got, coef_next)
-    last = halve(main[1] + got[1], 1, "y")
-
+    across, coef_sent, state_coef = lax.optimization_barrier((across, coef_sent, state_coef))
+    last = halve(main[1] + across, 1, "y")
     coef_last = halve(coef_next, 1, "z")
     coef = coef[0] + coef_got[0] + coef_last
     last, coef = after(last, coef)
-    main = main[0] + got[0] + last
-    got = halve(main[2:], 0, "z")
+    main = main[0] + near + last
+    across = halve(main[3], 0, "z")
+    near = halve(main[2], 0, "z")
 
     coef = sum_over(coef, "fsdp", Y_GROUPS) + state_coef
+    across, coef = after(across, coef)
+    last = halve(main[1] + across, 1, "z")
     coef = share(coef, COLUMN_GROUPS)
-    got, coef = after(got, coef)
-    last = halve(main[1] + got[1], 1, "z")
-
-    coef = share(coef, PLANE_GROUPS)
+    coef = share_parts(coef, PLANE_GROUPS)
     new_params = new_params_of(coef, params, expand)
-    last, new_params = after(last, new_params)
-    new_momentum = new_momentum_of(main[0] + got[0], last, momentum, reject)
+    new_momentum = new_momentum_of(main[0] + near, last, momentum, reject)
     return (new_params, new_momentum)
 
 

time: 90.7 us -> 85.4 us (0.942)
  blocking collectives: 24.7 us -> 8.9 us
  starting transfers between devices: 47.1 us -> 52 us
  waiting for transfers between devices: 9.97 us -> 14.8 us
  local copies, waits for them, and re-layouts: 1.37 us -> 2.68 us
    all_to_all x2 -> x1, blocking collectives: 24.7 us -> 8.9 us  [sum_over(): lax.all_to_all(x, axis, 0, 0, tiled=True, axis_index_groups=groups)]
    all_to_all x0 -> x1, starting transfers between devices: none -> 7.47 us  [deal(): return lax.all_to_all(x, axis, 0, 0, tiled=True, axis_index_groups=groups)]
    ppermute x6 -> x8, waiting for transfers between devices: 6.18 us -> 13.2 us  [halve(): return lax.ppermute(x, BOTH, sum_pairs(step, axis))]
    all_to_all x1, waiting for transfers between devices: 3.79 us -> 0.01 us  [sum_over(): lax.all_to_all(x, axis, 0, 0, tiled=True, axis_index_groups=groups)]
    all_to_all x0 -> x1, waiting for transfers between devices: none -> 1.58 us  [deal(): return lax.all_to_all(x, axis, 0, 0, tiled=True, axis_index_groups=groups)]
    all_to_all x1, starting transfers between devices: 4.66 us -> 3.29 us  [sum_over(): lax.all_to_all(x, axis, 0, 0, tiled=True, axis_index_groups=groups)]
    ppermute x6 -> x8, starting transfers between devices: 42.5 us -> 41.2 us  [halve(): return lax.ppermute(x, BOTH, sum_pairs(step, axis))]
  transfers between devices with their start and end apart: 7 -> 10, of which waited for: 3 -> 6; matrix products, arithmetic and copies ran while one was open for 1% -> 2% of each run, Pallas kernels for 4% -> 4%
where the time goes in v6:
time: 85.4 us; the launch traced here: 84.8 us
  starting transfers between devices  52 us (61%)
  waiting for transfers between devices  14.8 us (17%)
  blocking collectives  8.9 us (10%)
  Pallas kernels  5.33 us (6%)
  local copies, waits for them, and re-layouts  2.68 us (3%)
    ppermute x8, starting transfers between devices, halve(): return lax.ppermute(x, BOTH, sum_pairs(step, axis))  41.2 us
    ppermute x8, waiting for transfers between devices, halve(): return lax.ppermute(x, BOTH, sum_pairs(step, axis))  13.2 us
    all_to_all x1, blocking collectives, sum_over(): lax.all_to_all(x, axis, 0, 0, tiled=True, axis_index_groups=groups)  8.9 us
    all_to_all x1, starting transfers between devices, deal(): return lax.all_to_all(x, axis, 0, 0, tiled=True, axis_index_groups=groups)  7.47 us
    all_to_all x1, starting transfers between devices, sum_over(): lax.all_to_all(x, axis, 0, 0, tiled=True, axis_index_groups=groups)  3.29 us
  transfers between devices with their start and end apart: 10, of which 6 were waited for; matrix products, arithmetic and copies ran while one was open for 2% of the time, Pallas kernels for 4%

profile of v6, /device:TPU:1, one launch (start us, length us, event | category | flops | bytes accessed | tf_op | source)
XLA Modules:
  0.0 84.8 jit_solution(9021431485996557880)
XLA Ops:
  0.6 1.3 %copy-done = bf16[1,1,2,64,5120]{4,3,2,1,0:T(8,128)(2,1)S(1)} copy-done((bf16[1,1,2,64,5120]{4,3,2,1,0:T(8,128)(2,1)S(1)}, bf16[1,1,2,64,5120]{4,3,2,1,0:T(8,128)(2,1)}, u32[]{:S(2)}) %copy-start) | copy-done | bytes 1310744
  2.5 5.5 %collective-permute-start.1 = (f32[4,8,5120]{2,1,0:T(8,128)S(1)}, f32[4,8,5120]{2,1,0:T(8,128)S(1)}, u32[]{:S(2)}, u32[]{:S(2)}) collective-permute-start(f32[4,8,5120]{2,1,0:T(8,128)S(1)} %get-tuple-element.18), channel_id=1, source_target_pairs={{0,1},{1,0},{2,3},{3,2},{4,5},{5,4},{6,7},{7,6},{8,9},{9,8},{10,11... | collective-permute-start | bytes 1966088 | tf_op jit(solution)/shard_map/ppermute | solution.py:220
  8.0 1.5 %coef.1 = (f32[2,4,8,640]{3,2,1,0:T(8,128)S(1)}, f32[2,4,8,640]{3,2,1,0:T(8,128)S(1)}) custom-call(s32[8]{0:T(128)S(1)} %copy-done.4, bf16[2,64,5120]{2,1,0:T(8,128)(2,1)S(1)} %bitcast.26), custom_call_target="tpu_custom_call" | custom-call | flops 500000000 | bytes 2000000 | tf_op jit(solution)/shard_map/coef/pallas_call | solution.py:112
  9.5 12.5 %collective-permute-start.3 = (f32[2,4,8,640]{3,2,1,0:T(8,128)S(1)}, f32[2,4,8,640]{3,2,1,0:T(8,128)S(1)}, u32[]{:S(2)}, u32[]{:S(2)}) collective-permute-start(f32[2,4,8,640]{3,2,1,0:T(8,128)S(1)} %get-tuple-element.19), channel_id=1, source_target_pairs={{0,4},{1,5},{2,6},{3,7},{4,0},{5,1},{6,2},{7,3},{8,12},{9,13},{10,... | collective-permute-start | bytes 491528 | tf_op jit(solution)/shard_map/ppermute | solution.py:220
  22.0 1.1 %state.1 = (f32[8,640]{1,0:T(8,128)S(1)}, f32[128,128]{1,0:T(8,128)S(1)}, f32[1024,128]{1,0:T(8,128)S(1)}) custom-call(s32[8]{0:T(128)S(1)} %copy-done.4, f32[1,2,4,5120]{3,2,1,0:T(4,128)S(1)} %copy-done.3), custom_call_target="tpu_custom_call" | custom-call | flops 100000000 | bytes 1000000 | tf_op jit(solution)/shard_map/state/pallas_call | solution.py:145
  23.1 1.9 %collective-permute-start.2 = (f32[4,8,5120]{2,1,0:T(8,128)S(1)}, f32[4,8,5120]{2,1,0:T(8,128)S(1)}, u32[]{:S(2)}, u32[]{:S(2)}) collective-permute-start(f32[4,8,5120]{2,1,0:T(8,128)S(1)} %bitcast_add_fusion), channel_id=1, source_target_pairs={{0,3},{1,2},{2,1},{3,0},{4,7},{5,6},{6,5},{7,4},{8,11},{9,10},{10,... | collective-permute-start | bytes 1966088 | tf_op jit(solution)/shard_map/ppermute | solution.py:220
  25.1 2.5 %collective-permute-start = (f32[4,8,5120]{2,1,0:T(8,128)S(1)}, f32[4,8,5120]{2,1,0:T(8,128)S(1)}, u32[]{:S(2)}, u32[]{:S(2)}) collective-permute-start(f32[4,8,5120]{2,1,0:T(8,128)S(1)} %get-tuple-element.17), channel_id=1, source_target_pairs={{0,1},{1,0},{2,3},{3,2},{4,5},{5,4},{6,7},{7,6},{8,9},{9,8},{10,11... | collective-permute-start | bytes 1966088 | tf_op jit(solution)/shard_map/ppermute | solution.py:220
  27.6 7.5 %collective-permute-start.4 = (f32[4,8,640]{2,1,0:T(8,128)S(1)}, f32[4,8,640]{2,1,0:T(8,128)S(1)}, u32[]{:S(2)}, u32[]{:S(2)}) collective-permute-start(f32[4,8,640]{2,1,0:T(8,128)S(1)} %fusion.3), channel_id=1, source_target_pairs={{0,12},{1,13},{2,14},{3,15},{4,8},{5,9},{6,10},{7,11},{8,4},{9,5},... | collective-permute-start | bytes 245768 | tf_op jit(solution)/shard_map/ppermute | solution.py:220
  35.1 1.8 %collective-permute-done.4 = f32[4,8,640]{2,1,0:T(8,128)S(1)} collective-permute-done((f32[4,8,640]{2,1,0:T(8,128)S(1)}, f32[4,8,640]{2,1,0:T(8,128)S(1)}, u32[]{:S(2)}, u32[]{:S(2)}) %collective-permute-start.4) | collective-permute-done | bytes 81952 | tf_op jit(solution)/shard_map/ppermute | solution.py:220
  37.0 3.6 %collective-permute-done.2 = f32[4,8,5120]{2,1,0:T(8,128)S(1)} collective-permute-done((f32[4,8,5120]{2,1,0:T(8,128)S(1)}, f32[4,8,5120]{2,1,0:T(8,128)S(1)}, u32[]{:S(2)}, u32[]{:S(2)}) %collective-permute-start.2) | collective-permute-done | bytes 655392 | tf_op jit(solution)/shard_map/ppermute | solution.py:220
  40.6 1.4 %collective-permute-done = f32[4,8,5120]{2,1,0:T(8,128)S(1)} collective-permute-done((f32[4,8,5120]{2,1,0:T(8,128)S(1)}, f32[4,8,5120]{2,1,0:T(8,128)S(1)}, u32[]{:S(2)}, u32[]{:S(2)}) %collective-permute-start) | collective-permute-done | bytes 655392 | tf_op jit(solution)/shard_map/ppermute | solution.py:220
  42.1 7.1 %collective-permute-start.5 = (f32[8,5120]{1,0:T(8,128)S(1)}, f32[8,5120]{1,0:T(8,128)S(1)}, u32[]{:S(2)}, u32[]{:S(2)}) collective-permute-start(f32[8,5120]{1,0:T(8,128)S(1)} %get-tuple-element.33), channel_id=1, source_target_pairs={{0,4},{1,5},{2,6},{3,7},{4,0},{5,1},{6,2},{7,3},{8,12},{9,13},{10,... | collective-permute-start | bytes 491528 | tf_op jit(solution)/shard_map/ppermute | solution.py:220
  49.2 2.1 %collective-permute-start.6 = (f32[8,5120]{1,0:T(8,128)S(1)}, f32[8,5120]{1,0:T(8,128)S(1)}, u32[]{:S(2)}, u32[]{:S(2)}) collective-permute-start(f32[8,5120]{1,0:T(8,128)S(1)} %get-tuple-element.32), channel_id=1, source_target_pairs={{0,4},{1,5},{2,6},{3,7},{4,0},{5,1},{6,2},{7,3},{8,12},{9,13},{10,... | collective-permute-start | bytes 491528 | tf_op jit(solution)/shard_map/ppermute | solution.py:220
  51.3 8.9 %all_to_all.15 = f32[4,8,640]{2,1,0:T(8,128)S(1)} all-to-all(f32[4,8,640]{2,1,0:T(8,128)S(1)} %fusion.5), channel_id=1, replica_groups={{0,1,2,3},{4,5,6,7},{8,9,10,11},{12,13,14,15},{16,17,18,19},{20,21,22,2..., dimensions={0} | all-to-all | bytes 163840 | tf_op jit(solution)/shard_map/all_to_all | solution.py:232
  60.3 0.6 broadcast_in_dim.6
  60.9 3.3 %all-to-all-start.1 = ((f32[4,8,640]{2,1,0:T(8,128)}), f32[4,8,640]{2,1,0:T(8,128)S(1)}, u32[]{:S(2)}, u32[]{:S(2)}) async-start(f32[4,8,640]{2,1,0:T(8,128)} %broadcast_in_dim.6), calls=%async_computation.1 | async-start | bytes 163840 | tf_op jit(solution)/shard_map/all_to_all | solution.py:232
  64.2 3.3 %collective-permute-done.6 = f32[8,5120]{1,0:T(8,128)S(1)} collective-permute-done((f32[8,5120]{1,0:T(8,128)S(1)}, f32[8,5120]{1,0:T(8,128)S(1)}, u32[]{:S(2)}, u32[]{:S(2)}) %collective-permute-start.6) | collective-permute-done | bytes 163872 | tf_op jit(solution)/shard_map/ppermute | solution.py:220
  67.6 2.2 %collective-permute-start.7 = (f32[8,5120]{1,0:T(8,128)S(1)}, f32[8,5120]{1,0:T(8,128)S(1)}, u32[]{:S(2)}, u32[]{:S(2)}) collective-permute-start(f32[8,5120]{1,0:T(8,128)S(1)} %get-tuple-element.30), channel_id=1, source_target_pairs={{0,12},{1,13},{2,14},{3,15},{4,8},{5,9},{6,10},{7,11},{8,4},{9,5},... | collective-permute-start | bytes 491528 | tf_op jit(solution)/shard_map/ppermute | solution.py:220
  69.8 0.7 broadcast_in_dim.7
  70.5 7.5 %all-to-all-start.2 = ((f32[8,8,640]{2,1,0:T(8,128)}), f32[8,8,640]{2,1,0:T(8,128)S(1)}, u32[]{:S(2)}, u32[]{:S(2)}) async-start(f32[8,8,640]{2,1,0:T(8,128)} %broadcast_in_dim.7), calls=%async_computation.2 | async-start | bytes 327680 | tf_op jit(solution)/shard_map/all_to_all | solution.py:224
  77.9 3.0 %collective-permute-done.7.got_ref = f32[8,5120]{1,0:T(8,128)S(1)} collective-permute-done((f32[8,5120]{1,0:T(8,128)S(1)}, f32[8,5120]{1,0:T(8,128)S(1)}, u32[]{:S(2)}, u32[]{:S(2)}) %collective-permute-start.7) | collective-permute-done | bytes 163872 | tf_op jit(solution)/shard_map/ppermute | solution.py:220
  81.0 1.0 %momentum.1 = f32[1,2,4,5120]{3,2,1,0:T(4,128)} custom-call(f32[8,5120]{1,0:T(8,128)S(1)} %get-tuple-element.31.own_ref, f32[8,5120]{1,0:T(8,128)S(1)} %collective-permute-done.7.got_ref, f32[1,2,4,5120]{3,2,1,0:T(4,128)S(1)} %copy-done.3, f32[128,128]{1,0:T(8,128)S(1)} %get-tuple-element.29.reject_ref), custom_call_target="tpu_custom_call" | custom-call | flops 60000000 | bytes 700000 | tf_op jit(solution)/shard_map/momentum/pallas_call | solution.py:172
  82.0 1.6 %all-to-all-done.2.parts_ref = f32[8,8,640]{2,1,0:T(8,128)S(1)} async-done(((f32[8,8,640]{2,1,0:T(8,128)}), f32[8,8,640]{2,1,0:T(8,128)S(1)}, u32[]{:S(2)}, u32[]{:S(2)}) %all-to-all-start.2) | async-done | bytes 163872 | tf_op jit(solution)/shard_map/all_to_all | solution.py:224
  83.5 1.3 %params.1 = f32[2,4,5120]{2,1,0:T(4,128)} custom-call(f32[8,8,640]{2,1,0:T(8,128)S(1)} %all-to-all-done.2.parts_ref, f32[2,4,5120]{2,1,0:T(4,128)S(1)} %copy-done.2, f32[1024,128]{1,0:T(8,128)S(1)} %get-tuple-element.27.expand_ref), custom_call_target="tpu_custom_call" | custom-call | flops 60000000 | bytes 700000 | tf_op jit(solution)/shard_map/params/pallas_call | solution.py:198
  (23 shorter events, 0.9 us)
Async XLA Ops:
  0.6 7.3 %copy-start.4 = (s32[8]{0:T(128)S(1)}, s32[8]{0:T(128)}, u32[]{:S(2)}) copy-start(s32[8]{0:T(128)} %kept_ref.3) | copy-start | bytes 100
  0.6 1.3 %copy-start = (bf16[1,1,2,64,5120]{4,3,2,1,0:T(8,128)(2,1)S(1)}, bf16[1,1,2,64,5120]{4,3,2,1,0:T(8,128)(2,1)}, u32[]{:S(2)}) copy-start(bf16[1,1,2,64,5120]{4,3,2,1,0:T(8,128)(2,1)} %param.4) | copy-start | bytes 3932164
  2.0 6.0 %copy-start.1 = (bf16[1,1,2,64,5120]{4,3,2,1,0:T(8,128)(2,1)S(1)}, bf16[1,1,2,64,5120]{4,3,2,1,0:T(8,128)(2,1)}, u32[]{:S(2)}) copy-start(bf16[1,1,2,64,5120]{4,3,2,1,0:T(8,128)(2,1)} %param.4) | copy-start | bytes 3932164
  2.0 20.0 %copy-start.3 = (f32[1,2,4,5120]{3,2,1,0:T(4,128)S(1)}, f32[1,2,4,5120]{3,2,1,0:T(4,128)}, u32[]{:S(2)}) copy-start(f32[1,2,4,5120]{3,2,1,0:T(4,128)} %momentum_ref.3) | copy-start | bytes 491524
  2.5 20.6 %collective-permute-start.1 = (f32[4,8,5120]{2,1,0:T(8,128)S(1)}, f32[4,8,5120]{2,1,0:T(8,128)S(1)}, u32[]{:S(2)}, u32[]{:S(2)}) collective-permute-start(f32[4,8,5120]{2,1,0:T(8,128)S(1)} %get-tuple-element.18), channel_id=1, source_target_pairs={{0,1},{1,0},{2,3},{3,2},{4,5},{5,4},{6,7},{7,6},{8,9},{9,8},{10,11... | collective-permute-start | bytes 1966088 | tf_op jit(solution)/shard_map/ppermute | solution.py:220
  9.5 18.1 %collective-permute-start.3 = (f32[2,4,8,640]{3,2,1,0:T(8,128)S(1)}, f32[2,4,8,640]{3,2,1,0:T(8,128)S(1)}, u32[]{:S(2)}, u32[]{:S(2)}) collective-permute-start(f32[2,4,8,640]{3,2,1,0:T(8,128)S(1)} %get-tuple-element.19), channel_id=1, source_target_pairs={{0,4},{1,5},{2,6},{3,7},{4,0},{5,1},{6,2},{7,3},{8,12},{9,13},{10,... | collective-permute-start | bytes 491528 | tf_op jit(solution)/shard_map/ppermute | solution.py:220
  23.1 17.5 %collective-permute-start.2 = (f32[4,8,5120]{2,1,0:T(8,128)S(1)}, f32[4,8,5120]{2,1,0:T(8,128)S(1)}, u32[]{:S(2)}, u32[]{:S(2)}) collective-permute-start(f32[4,8,5120]{2,1,0:T(8,128)S(1)} %bitcast_add_fusion), channel_id=1, source_target_pairs={{0,3},{1,2},{2,1},{3,0},{4,7},{5,6},{6,5},{7,4},{8,11},{9,10},{10,... | collective-permute-start | bytes 1966088 | tf_op jit(solution)/shard_map/ppermute | solution.py:220
  25.1 16.9 %collective-permute-start = (f32[4,8,5120]{2,1,0:T(8,128)S(1)}, f32[4,8,5120]{2,1,0:T(8,128)S(1)}, u32[]{:S(2)}, u32[]{:S(2)}) collective-permute-start(f32[4,8,5120]{2,1,0:T(8,128)S(1)} %get-tuple-element.17), channel_id=1, source_target_pairs={{0,1},{1,0},{2,3},{3,2},{4,5},{5,4},{6,7},{7,6},{8,9},{9,8},{10,11... | collective-permute-start | bytes 1966088 | tf_op jit(solution)/shard_map/ppermute | solution.py:220
  27.6 9.3 %collective-permute-start.4 = (f32[4,8,640]{2,1,0:T(8,128)S(1)}, f32[4,8,640]{2,1,0:T(8,128)S(1)}, u32[]{:S(2)}, u32[]{:S(2)}) collective-permute-start(f32[4,8,640]{2,1,0:T(8,128)S(1)} %fusion.3), channel_id=1, source_target_pairs={{0,12},{1,13},{2,14},{3,15},{4,8},{5,9},{6,10},{7,11},{8,4},{9,5},... | collective-permute-start | bytes 245768 | tf_op jit(solution)/shard_map/ppermute | solution.py:220
  42.1 18.1 %collective-permute-start.5 = (f32[8,5120]{1,0:T(8,128)S(1)}, f32[8,5120]{1,0:T(8,128)S(1)}, u32[]{:S(2)}, u32[]{:S(2)}) collective-permute-start(f32[8,5120]{1,0:T(8,128)S(1)} %get-tuple-element.33), channel_id=1, source_target_pairs={{0,4},{1,5},{2,6},{3,7},{4,0},{5,1},{6,2},{7,3},{8,12},{9,13},{10,... | collective-permute-start | bytes 491528 | tf_op jit(solution)/shard_map/ppermute | solution.py:220
  49.2 18.3 %collective-permute-start.6 = (f32[8,5120]{1,0:T(8,128)S(1)}, f32[8,5120]{1,0:T(8,128)S(1)}, u32[]{:S(2)}, u32[]{:S(2)}) collective-permute-start(f32[8,5120]{1,0:T(8,128)S(1)} %get-tuple-element.32), channel_id=1, source_target_pairs={{0,4},{1,5},{2,6},{3,7},{4,0},{5,1},{6,2},{7,3},{8,12},{9,13},{10,... | collective-permute-start | bytes 491528 | tf_op jit(solution)/shard_map/ppermute | solution.py:220
  60.3 23.3 %copy-start.2 = (f32[2,4,5120]{2,1,0:T(4,128)S(1)}, f32[2,4,5120]{2,1,0:T(4,128)}, u32[]{:S(2)}) copy-start(f32[2,4,5120]{2,1,0:T(4,128)} %params_ref.1) | copy-start | bytes 491524
  60.9 8.9 %all-to-all-start.1 = ((f32[4,8,640]{2,1,0:T(8,128)}), f32[4,8,640]{2,1,0:T(8,128)S(1)}, u32[]{:S(2)}, u32[]{:S(2)}) async-start(f32[4,8,640]{2,1,0:T(8,128)} %broadcast_in_dim.6), calls=%async_computation.1 | async-start | bytes 163840 | tf_op jit(solution)/shard_map/all_to_all | solution.py:232
  67.6 13.4 %collective-permute-start.7 = (f32[8,5120]{1,0:T(8,128)S(1)}, f32[8,5120]{1,0:T(8,128)S(1)}, u32[]{:S(2)}, u32[]{:S(2)}) collective-permute-start(f32[8,5120]{1,0:T(8,128)S(1)} %get-tuple-element.30), channel_id=1, source_target_pairs={{0,12},{1,13},{2,14},{3,15},{4,8},{5,9},{6,10},{7,11},{8,4},{9,5},... | collective-permute-start | bytes 491528 | tf_op jit(solution)/shard_map/ppermute | solution.py:220
  70.5 13.0 %all-to-all-start.2 = ((f32[8,8,640]{2,1,0:T(8,128)}), f32[8,8,640]{2,1,0:T(8,128)S(1)}, u32[]{:S(2)}, u32[]{:S(2)}) async-start(f32[8,8,640]{2,1,0:T(8,128)} %broadcast_in_dim.7), calls=%async_computation.2 | async-start | bytes 327680 | tf_op jit(solution)/shard_map/all_to_all | solution.py:224

commit v7 on v6

--- a/solution.py
+++ b/solution.py
@@ -96,11 +96,13 @@
     picked = picked_t(kept_ref)
     high = picked.astype(jnp.bfloat16).astype(jnp.float32)
     wide = jnp.concatenate([spread(high), spread(picked - high)], axis=1).astype(jnp.bfloat16)
+    rows = []
     for c in range(CHUNKS):
         values = grad_ref[:, :, c * WIDE:(c + 1) * WIDE].reshape(128, WIDE)
-        rows = jnp.dot(order, values, preferred_element_type=jnp.float32).astype(jnp.bfloat16)
-        both = jnp.dot(rows, wide, preferred_element_type=jnp.float32)
-        coef = both[:, :128] + both[:, 128:]
+        rows.append(jnp.dot(order, values, preferred_element_type=jnp.float32).astype(jnp.bfloat16))
+    both = jnp.dot(jnp.concatenate(rows, axis=0), wide, preferred_element_type=jnp.float32)
+    for c in range(CHUNKS):
+        coef = both[c * 128:(c + 1) * 128, :128] + both[c * 128:(c + 1) * 128, 128:]
         lanes = slice(c * 128, (c + 1) * 128)
         rest_ref[:, :, :, lanes] = coef[:64].reshape(2, 4, OWN, 128)
         sent_ref[:, :, :, lanes] = coef[64:].reshape(2, 4, OWN, 128)
@@ -124,14 +126,17 @@
     return jnp.concatenate([x[:, c * 128:(c + 1) * 128] for c in range(x.shape[1] // 128)], axis=0)
 
 
-def state_kernel(kept_ref, momentum_ref, coef_ref, reject_ref, expand_ref):
+def state_kernel(kept_ref, momentum_ref, coef_ref, reject_ref, expand_ref, rest_ref):
     wide = spread(picked_t(kept_ref))
     pair = wide[:128, :]
     row = lax.broadcasted_iota(jnp.int32, (128, 128), 0)
     col = lax.broadcasted_iota(jnp.int32, (128, 128), 1)
     onto = lax.dot_general(pair, pair, (((1,), (1,)), ((), ())), precision=HIGHEST, preferred_element_type=jnp.float32)
     reject_ref[...] = jnp.where(row == col, 1.0, 0.0) - onto
-    expand_ref[...] = wide
+    across = wide.T
+    high = across.astype(jnp.bfloat16)
+    expand_ref[...] = high
+    rest_ref[...] = (across - high.astype(jnp.float32)).astype(jnp.bfloat16)
     state = 0.9 * jnp.concatenate([momentum_ref[0, 0], momentum_ref[0, 1]], axis=0)
     deep = jnp.concatenate([state[:, c * WIDE:(c + 1) * WIDE] for c in range(CHUNKS)], axis=0)
     coef = jnp.dot(deep, wide, precision=HIGHEST, preferred_element_type=jnp.float32)
@@ -147,10 +152,11 @@
         out_shape=(
             jax.ShapeDtypeStruct((OWN, COEFFS), jnp.float32),
             jax.ShapeDtypeStruct((128, 128), jnp.float32),
-            jax.ShapeDtypeStruct((WIDE, 128), jnp.float32),
+            jax.ShapeDtypeStruct((128, WIDE), jnp.bfloat16),
+            jax.ShapeDtypeStruct((128, WIDE), jnp.bfloat16),
         ),
         in_specs=[smem, vmem],
-        out_specs=(vmem, vmem, vmem),
+        out_specs=(vmem, vmem, vmem, vmem),
         compiler_params=pltpu.CompilerParams(vmem_limit_bytes=32 * 2**20),
         cost_estimate=pl.CostEstimate(flops=100_000_000, bytes_accessed=1_000_000, transcendentals=0),
         name="state",
@@ -180,12 +186,14 @@
     )(own, got, momentum, reject)
 
 
-def params_kernel(parts_ref, params_ref, expand_ref, out_ref):
+def params_kernel(parts_ref, params_ref, expand_ref, rest_ref, out_ref):
     shared = jnp.sum(parts_ref[...], axis=0) * (1.0 / N_DP)
     deep = tall(shared)
-    update = lax.dot_general(
-        deep, expand_ref[...], (((1,), (1,)), ((), ())), precision=HIGHEST, preferred_element_type=jnp.float32
-    )
+    high = deep.astype(jnp.bfloat16)
+    low = (deep - high.astype(jnp.float32)).astype(jnp.bfloat16)
+    update = jnp.dot(jnp.concatenate([high, low], axis=0), expand_ref[...], preferred_element_type=jnp.float32)
+    update = update[:CHUNKS * OWN] + update[CHUNKS * OWN:]
+    update = update + jnp.dot(high, rest_ref[...], preferred_element_type=jnp.float32)
     for c in range(CHUNKS):
         lanes = slice(c * WIDE, (c + 1) * WIDE)
         part = update[c * OWN:(c + 1) * OWN]
@@ -193,17 +201,17 @@
         out_ref[1, :, lanes] = params_ref[1, :, lanes] - part[4:]
 
 
-def new_params_of(parts, params, expand):
+def new_params_of(parts, params, expand, rest):
     vmem = pl.BlockSpec(memory_space=pltpu.VMEM)
     return pl.pallas_call(
         params_kernel,
         out_shape=jax.ShapeDtypeStruct(params.shape, jnp.float32),
-        in_specs=[vmem] * 3,
+        in_specs=[vmem] * 4,
         out_specs=vmem,
         compiler_params=pltpu.CompilerParams(vmem_limit_bytes=32 * 2**20),
         cost_estimate=pl.CostEstimate(flops=60_000_000, bytes_accessed=700_000, transcendentals=0),
         name="params",
-    )(parts, params, expand)
+    )(parts, params, expand, rest)
 
 
 def sum_pairs(step, axis):
@@ -251,26 +259,24 @@
     across = halve(across, 0, "y")
     near = halve(near, 0, "y")
     coef, coef_sent = coef_of(kept, grad)
-    state_coef, reject, expand = state_of(kept, momentum)
+    state_coef, reject, expand, rest = state_of(kept, momentum)
 
     coef_got = halve(coef_sent, 0, "z")
-    coef_next = coef[1] + coef_got[1]
     across, coef_sent, state_coef = lax.optimization_barrier((across, coef_sent, state_coef))
     last = halve(main[1] + across, 1, "y")
+    coef_next = coef[1] + coef_got[1]
     coef_last = halve(coef_next, 1, "z")
     coef = coef[0] + coef_got[0] + coef_last
     last, coef = after(last, coef)
     main = main[0] + near + last
-    across = halve(main[3], 0, "z")
-    near = halve(main[2], 0, "z")
+    got = halve(main[2:], 0, "z")
 
     coef = sum_over(coef, "fsdp", Y_GROUPS) + state_coef
-    across, coef = after(across, coef)
-    last = halve(main[1] + across, 1, "z")
+    last = halve(main[1] + got[1], 1, "z")
     coef = share(coef, COLUMN_GROUPS)
     coef = share_parts(coef, PLANE_GROUPS)
-    new_params = new_params_of(coef, params, expand)
-    new_momentum = new_momentum_of(main[0] + near, last, momentum, reject)
+    new_params = new_params_of(coef, params, expand, rest)
+    new_momentum = new_momentum_of(main[0] + got[0], last, momentum, reject)
     return (new_params, new_momentum)
 
 

time: 85.4 us -> 84.1 us (0.985)
  the two profiles are of different devices: /device:TPU:1 before, /device:TPU:40 now
where the time goes in v7:
time: 84.1 us; the launch traced here: 83.6 us
  starting transfers between devices  50.4 us (60%)
  blocking collectives  19.9 us (24%)
  waiting for transfers between devices  5.34 us (6%)
  Pallas kernels  4.79 us (6%)
  local copies, waits for them, and re-layouts  2.01 us (2%)
    ppermute x7, starting transfers between devices, halve(): return lax.ppermute(x, BOTH, sum_pairs(step, axis))  43.5 us
    all_to_all x1, blocking collectives, deal(): return lax.all_to_all(x, axis, 0, 0, tiled=True, axis_index_groups=groups)  11.4 us
    all_to_all x1, blocking collectives, sum_over(): lax.all_to_all(x, axis, 0, 0, tiled=True, axis_index_groups=groups)  8.48 us
    all_to_all x1, starting transfers between devices, sum_over(): lax.all_to_all(x, axis, 0, 0, tiled=True, axis_index_groups=groups)  6.86 us
    ppermute x7, waiting for transfers between devices, halve(): return lax.ppermute(x, BOTH, sum_pairs(step, axis))  5.34 us
  transfers between devices with their start and end apart: 8, of which 3 were waited for; matrix products, arithmetic and copies ran while one was open for 1% of the time, Pallas kernels for 4%

profile of v7, /device:TPU:40, one launch (start us, length us, event | category | flops | bytes accessed | tf_op | source)
XLA Modules:
  0.0 83.6 jit_solution(3269294704308361644)
XLA Ops:
  0.6 1.3 %copy-done = bf16[1,1,2,64,5120]{4,3,2,1,0:T(8,128)(2,1)S(1)} copy-done((bf16[1,1,2,64,5120]{4,3,2,1,0:T(8,128)(2,1)S(1)}, bf16[1,1,2,64,5120]{4,3,2,1,0:T(8,128)(2,1)}, u32[]{:S(2)}) %copy-start) | copy-done | bytes 1310744
  2.0 0.5 main.1
  2.5 2.4 %collective-permute-start = (f32[4,8,5120]{2,1,0:T(8,128)S(1)}, f32[4,8,5120]{2,1,0:T(8,128)S(1)}, u32[]{:S(2)}, u32[]{:S(2)}) collective-permute-start(f32[4,8,5120]{2,1,0:T(8,128)S(1)} %get-tuple-element.16), channel_id=1, source_target_pairs={{0,1},{1,0},{2,3},{3,2},{4,5},{5,4},{6,7},{7,6},{8,9},{9,8},{10,11... | collective-permute-start | bytes 1966088 | tf_op jit(solution)/shard_map/ppermute | solution.py:228
  4.8 1.4 %coef.1 = (f32[2,4,8,640]{3,2,1,0:T(8,128)S(1)}, f32[2,4,8,640]{3,2,1,0:T(8,128)S(1)}) custom-call(s32[8]{0:T(128)S(1)} %copy-done.4, bf16[2,64,5120]{2,1,0:T(8,128)(2,1)S(1)} %bitcast.18), custom_call_target="tpu_custom_call" | custom-call | flops 500000000 | bytes 2000000 | tf_op jit(solution)/shard_map/coef/pallas_call | solution.py:114
  6.2 9.1 %collective-permute-start.2 = (f32[2,4,8,640]{3,2,1,0:T(8,128)S(1)}, f32[2,4,8,640]{3,2,1,0:T(8,128)S(1)}, u32[]{:S(2)}, u32[]{:S(2)}) collective-permute-start(f32[2,4,8,640]{3,2,1,0:T(8,128)S(1)} %get-tuple-element.17), channel_id=1, source_target_pairs={{0,4},{1,5},{2,6},{3,7},{4,0},{5,1},{6,2},{7,3},{8,12},{9,13},{10,... | collective-permute-start | bytes 491528 | tf_op jit(solution)/shard_map/ppermute | solution.py:228
  15.4 1.1 %state.1 = (f32[8,640]{1,0:T(8,128)S(1)}, f32[128,128]{1,0:T(8,128)S(1)}, bf16[128,1024]{1,0:T(8,128)(2,1)S(1)}, bf16[128,1024]{1,0:T(8,128)(2,1)S(1)}) custom-call(s32[8]{0:T(128)S(1)} %copy-done.4, f32[1,2,4,5120]{3,2,1,0:T(4,128)S(1)} %copy-done.3), custom_call_target="tpu_custom_call" | custom-call | flops 100000000 | bytes 1000000 | tf_op jit(solution)/shard_map/state/pallas_call | solution.py:150
  16.4 0.0 collective-permute-done
  16.4 0.1 bitcast_add_fusion.1
  16.5 4.3 %collective-permute-start.1 = (f32[4,8,5120]{2,1,0:T(8,128)S(1)}, f32[4,8,5120]{2,1,0:T(8,128)S(1)}, u32[]{:S(2)}, u32[]{:S(2)}) collective-permute-start(f32[4,8,5120]{2,1,0:T(8,128)S(1)} %bitcast_add_fusion.1), channel_id=1, source_target_pairs={{0,3},{1,2},{2,1},{3,0},{4,7},{5,6},{6,5},{7,4},{8,11},{9,10},{10,... | collective-permute-start | bytes 1966088 | tf_op jit(solution)/shard_map/ppermute | solution.py:228
  20.8 3.3 %collective-permute-start.4 = (f32[4,8,5120]{2,1,0:T(8,128)S(1)}, f32[4,8,5120]{2,1,0:T(8,128)S(1)}, u32[]{:S(2)}, u32[]{:S(2)}) collective-permute-start(f32[4,8,5120]{2,1,0:T(8,128)S(1)} %get-tuple-element.25), channel_id=1, source_target_pairs={{0,1},{1,0},{2,3},{3,2},{4,5},{5,4},{6,7},{7,6},{8,9},{9,8},{10,11... | collective-permute-start | bytes 1966088 | tf_op jit(solution)/shard_map/ppermute | solution.py:228
  24.1 10.1 %collective-permute-start.3 = (f32[4,8,640]{2,1,0:T(8,128)S(1)}, f32[4,8,640]{2,1,0:T(8,128)S(1)}, u32[]{:S(2)}, u32[]{:S(2)}) collective-permute-start(f32[4,8,640]{2,1,0:T(8,128)S(1)} %fusion.3), channel_id=1, source_target_pairs={{0,12},{1,13},{2,14},{3,15},{4,8},{5,9},{6,10},{7,11},{8,4},{9,5},... | collective-permute-start | bytes 245768 | tf_op jit(solution)/shard_map/ppermute | solution.py:228
  34.2 3.8 %collective-permute-done.3 = f32[4,8,640]{2,1,0:T(8,128)S(1)} collective-permute-done((f32[4,8,640]{2,1,0:T(8,128)S(1)}, f32[4,8,640]{2,1,0:T(8,128)S(1)}, u32[]{:S(2)}, u32[]{:S(2)}) %collective-permute-start.3) | collective-permute-done | bytes 81952 | tf_op jit(solution)/shard_map/ppermute | solution.py:228
  38.0 0.3 collective-permute-done.4
  38.3 0.1 fusion
  38.5 0.0 copy-start.2
  38.5 5.6 %collective-permute-start.5 = (f32[2,8,5120]{2,1,0:T(8,128)S(1)}, f32[2,8,5120]{2,1,0:T(8,128)S(1)}, u32[]{:S(2)}, u32[]{:S(2)}) collective-permute-start(f32[2,8,5120]{2,1,0:T(8,128)S(1)} %slice.47), channel_id=1, source_target_pairs={{0,4},{1,5},{2,6},{3,7},{4,0},{5,1},{6,2},{7,3},{8,12},{9,13},{10,... | collective-permute-start | bytes 983048 | tf_op jit(solution)/shard_map/ppermute | solution.py:228
  44.1 8.5 %all_to_all.15 = f32[4,8,640]{2,1,0:T(8,128)S(1)} all-to-all(f32[4,8,640]{2,1,0:T(8,128)S(1)} %fusion.5), channel_id=1, replica_groups={{0,1,2,3},{4,5,6,7},{8,9,10,11},{12,13,14,15},{16,17,18,19},{20,21,22,2..., dimensions={0} | all-to-all | bytes 163840 | tf_op jit(solution)/shard_map/all_to_all | solution.py:240
  52.7 0.6 broadcast_in_dim.6
  53.3 6.9 %all-to-all-start.1 = ((f32[4,8,640]{2,1,0:T(8,128)}), f32[4,8,640]{2,1,0:T(8,128)S(1)}, u32[]{:S(2)}, u32[]{:S(2)}) async-start(f32[4,8,640]{2,1,0:T(8,128)} %broadcast_in_dim.6), calls=%async_computation.1 | async-start | bytes 163840 | tf_op jit(solution)/shard_map/all_to_all | solution.py:240
  60.2 1.2 %collective-permute-done.5 = f32[2,8,5120]{2,1,0:T(8,128)S(1)} collective-permute-done((f32[2,8,5120]{2,1,0:T(8,128)S(1)}, f32[2,8,5120]{2,1,0:T(8,128)S(1)}, u32[]{:S(2)}, u32[]{:S(2)}) %collective-permute-start.5) | collective-permute-done | bytes 327712 | tf_op jit(solution)/shard_map/ppermute | solution.py:228
  61.4 8.8 %collective-permute-start.6 = (f32[8,5120]{1,0:T(8,128)S(1)}, f32[8,5120]{1,0:T(8,128)S(1)}, u32[]{:S(2)}, u32[]{:S(2)}) collective-permute-start(f32[8,5120]{1,0:T(8,128)S(1)} %get-tuple-element.28), channel_id=1, source_target_pairs={{0,12},{1,13},{2,14},{3,15},{4,8},{5,9},{6,10},{7,11},{8,4},{9,5},... | collective-permute-start | bytes 491528 | tf_op jit(solution)/shard_map/ppermute | solution.py:228
  70.3 11.4 %all_to_all.16.parts_ref = f32[8,8,640]{2,1,0:T(8,128)S(1)} all-to-all(f32[8,8,640]{2,1,0:T(8,128)S(1)} %broadcast_in_dim.7), channel_id=1, replica_groups={{0,16,32,48,64,80,96,112},{128,144,160,176,192,208,224,240},{256,272,28..., dimensions={0} | all-to-all | bytes 327680 | tf_op jit(solution)/shard_map/all_to_all | solution.py:232
  81.7 0.9 %params.1 = f32[2,4,5120]{2,1,0:T(4,128)} custom-call(f32[8,8,640]{2,1,0:T(8,128)S(1)} %all_to_all.16.parts_ref, f32[2,4,5120]{2,1,0:T(4,128)S(1)} %copy-done.2, bf16[128,1024]{1,0:T(8,128)(2,1)S(1)} %get-tuple-element.23.expand_ref, bf16[128,1024]{1,0:T(8,128)(2,1)S(1)} %get-tuple-element.24.rest_ref), custom_call_target="tpu_custom_call" | custom-call | flops 60000000 | bytes 700000 | tf_op jit(solution)/shard_map/params/pallas_call | solution.py:206
  82.6 1.0 %momentum.1 = f32[1,2,4,5120]{3,2,1,0:T(4,128)} custom-call(f32[8,5120]{1,0:T(8,128)S(1)} %get-tuple-element.29.own_ref, f32[8,5120]{1,0:T(8,128)S(1)} %collective-permute-done.6.got_ref, f32[1,2,4,5120]{3,2,1,0:T(4,128)S(1)} %copy-done.3, f32[128,128]{1,0:T(8,128)S(1)} %get-tuple-element.27.reject_ref), custom_call_target="tpu_custom_call" | custom-call | flops 60000000 | bytes 700000 | tf_op jit(solution)/shard_map/momentum/pallas_call | solution.py:178
  (20 shorter events, 0.2 us)
Async XLA Ops:
  0.6 4.2 %copy-start.4 = (s32[8]{0:T(128)S(1)}, s32[8]{0:T(128)}, u32[]{:S(2)}) copy-start(s32[8]{0:T(128)} %kept_ref.3) | copy-start | bytes 100
  0.6 1.3 %copy-start = (bf16[1,1,2,64,5120]{4,3,2,1,0:T(8,128)(2,1)S(1)}, bf16[1,1,2,64,5120]{4,3,2,1,0:T(8,128)(2,1)}, u32[]{:S(2)}) copy-start(bf16[1,1,2,64,5120]{4,3,2,1,0:T(8,128)(2,1)} %param.4) | copy-start | bytes 3932164
  2.0 2.9 %copy-start.1 = (bf16[1,1,2,64,5120]{4,3,2,1,0:T(8,128)(2,1)S(1)}, bf16[1,1,2,64,5120]{4,3,2,1,0:T(8,128)(2,1)}, u32[]{:S(2)}) copy-start(bf16[1,1,2,64,5120]{4,3,2,1,0:T(8,128)(2,1)} %param.4) | copy-start | bytes 3932164
  2.0 13.4 %copy-start.3 = (f32[1,2,4,5120]{3,2,1,0:T(4,128)S(1)}, f32[1,2,4,5120]{3,2,1,0:T(4,128)}, u32[]{:S(2)}) copy-start(f32[1,2,4,5120]{3,2,1,0:T(4,128)} %momentum_ref.3) | copy-start | bytes 491524
  2.5 14.0 %collective-permute-start = (f32[4,8,5120]{2,1,0:T(8,128)S(1)}, f32[4,8,5120]{2,1,0:T(8,128)S(1)}, u32[]{:S(2)}, u32[]{:S(2)}) collective-permute-start(f32[4,8,5120]{2,1,0:T(8,128)S(1)} %get-tuple-element.16), channel_id=1, source_target_pairs={{0,1},{1,0},{2,3},{3,2},{4,5},{5,4},{6,7},{7,6},{8,9},{9,8},{10,11... | collective-permute-start | bytes 1966088 | tf_op jit(solution)/shard_map/ppermute | solution.py:228
  6.2 17.9 %collective-permute-start.2 = (f32[2,4,8,640]{3,2,1,0:T(8,128)S(1)}, f32[2,4,8,640]{3,2,1,0:T(8,128)S(1)}, u32[]{:S(2)}, u32[]{:S(2)}) collective-permute-start(f32[2,4,8,640]{3,2,1,0:T(8,128)S(1)} %get-tuple-element.17), channel_id=1, source_target_pairs={{0,4},{1,5},{2,6},{3,7},{4,0},{5,1},{6,2},{7,3},{8,12},{9,13},{10,... | collective-permute-start | bytes 491528 | tf_op jit(solution)/shard_map/ppermute | solution.py:228
  16.5 21.5 %collective-permute-start.1 = (f32[4,8,5120]{2,1,0:T(8,128)S(1)}, f32[4,8,5120]{2,1,0:T(8,128)S(1)}, u32[]{:S(2)}, u32[]{:S(2)}) collective-permute-start(f32[4,8,5120]{2,1,0:T(8,128)S(1)} %bitcast_add_fusion.1), channel_id=1, source_target_pairs={{0,3},{1,2},{2,1},{3,0},{4,7},{5,6},{6,5},{7,4},{8,11},{9,10},{10,... | collective-permute-start | bytes 1966088 | tf_op jit(solution)/shard_map/ppermute | solution.py:228
  20.8 17.5 %collective-permute-start.4 = (f32[4,8,5120]{2,1,0:T(8,128)S(1)}, f32[4,8,5120]{2,1,0:T(8,128)S(1)}, u32[]{:S(2)}, u32[]{:S(2)}) collective-permute-start(f32[4,8,5120]{2,1,0:T(8,128)S(1)} %get-tuple-element.25), channel_id=1, source_target_pairs={{0,1},{1,0},{2,3},{3,2},{4,5},{5,4},{6,7},{7,6},{8,9},{9,8},{10,11... | collective-permute-start | bytes 1966088 | tf_op jit(solution)/shard_map/ppermute | solution.py:228
  24.1 13.8 %collective-permute-start.3 = (f32[4,8,640]{2,1,0:T(8,128)S(1)}, f32[4,8,640]{2,1,0:T(8,128)S(1)}, u32[]{:S(2)}, u32[]{:S(2)}) collective-permute-start(f32[4,8,640]{2,1,0:T(8,128)S(1)} %fusion.3), channel_id=1, source_target_pairs={{0,12},{1,13},{2,14},{3,15},{4,8},{5,9},{6,10},{7,11},{8,4},{9,5},... | collective-permute-start | bytes 245768 | tf_op jit(solution)/shard_map/ppermute | solution.py:228
  38.5 43.3 %copy-start.2 = (f32[2,4,5120]{2,1,0:T(4,128)S(1)}, f32[2,4,5120]{2,1,0:T(4,128)}, u32[]{:S(2)}) copy-start(f32[2,4,5120]{2,1,0:T(4,128)} %params_ref.1) | copy-start | bytes 491524
  38.5 22.8 %collective-permute-start.5 = (f32[2,8,5120]{2,1,0:T(8,128)S(1)}, f32[2,8,5120]{2,1,0:T(8,128)S(1)}, u32[]{:S(2)}, u32[]{:S(2)}) collective-permute-start(f32[2,8,5120]{2,1,0:T(8,128)S(1)} %slice.47), channel_id=1, source_target_pairs={{0,4},{1,5},{2,6},{3,7},{4,0},{5,1},{6,2},{7,3},{8,12},{9,13},{10,... | collective-permute-start | bytes 983048 | tf_op jit(solution)/shard_map/ppermute | solution.py:228
  53.3 17.0 %all-to-all-start.1 = ((f32[4,8,640]{2,1,0:T(8,128)}), f32[4,8,640]{2,1,0:T(8,128)S(1)}, u32[]{:S(2)}, u32[]{:S(2)}) async-start(f32[4,8,640]{2,1,0:T(8,128)} %broadcast_in_dim.6), calls=%async_computation.1 | async-start | bytes 163840 | tf_op jit(solution)/shard_map/all_to_all | solution.py:240
  61.4 21.2 %collective-permute-start.6 = (f32[8,5120]{1,0:T(8,128)S(1)}, f32[8,5120]{1,0:T(8,128)S(1)}, u32[]{:S(2)}, u32[]{:S(2)}) collective-permute-start(f32[8,5120]{1,0:T(8,128)S(1)} %get-tuple-element.28), channel_id=1, source_target_pairs={{0,12},{1,13},{2,14},{3,15},{4,8},{5,9},{6,10},{7,11},{8,4},{9,5},... | collective-permute-start | bytes 491528 | tf_op jit(solution)/shard_map/ppermute | solution.py:228

commit v8 on v7

--- a/solution.py
+++ b/solution.py
@@ -245,8 +245,8 @@
 
 
 Y_GROUPS = [[z * 4 + y for y in range(4)] for z in range(4)]
-PLANE_GROUPS = [[z * 8 + i for i in range(8)] for z in range(4)]
-COLUMN_GROUPS = [[z * 8 + i for z in range(4)] for i in range(8)]
+PLANE_GROUPS = [[z * 8 + x * 2 + c for x in range(4)] for z in range(4) for c in range(2)]
+COLUMN_GROUPS = [[z * 8 + x * 2 + c for z in range(4) for c in range(2)] for x in range(4)]
 
 
 def after(x, earlier):

time: 84.1 us -> 83.1 us (0.988)
  the two profiles are of different devices: /device:TPU:40 before, /device:TPU:6 now
where the time goes in v8:
time: 83.1 us; the launch traced here: 81.5 us
  starting transfers between devices  48.4 us (58%)
  waiting for transfers between devices  16.4 us (20%)
  blocking collectives  8.08 us (10%)
  Pallas kernels  4.81 us (6%)
  local copies, waits for them, and re-layouts  2.68 us (3%)
    ppermute x7, starting transfers between devices, halve(): return lax.ppermute(x, BOTH, sum_pairs(step, axis))  38.3 us
    ppermute x7, waiting for transfers between devices, halve(): return lax.ppermute(x, BOTH, sum_pairs(step, axis))  15.5 us
    all_to_all x1, blocking collectives, sum_over(): lax.all_to_all(x, axis, 0, 0, tiled=True, axis_index_groups=groups)  8.08 us
    all_to_all x1, starting transfers between devices, sum_over(): lax.all_to_all(x, axis, 0, 0, tiled=True, axis_index_groups=groups)  5.41 us
    all_to_all x1, starting transfers between devices, deal(): return lax.all_to_all(x, axis, 0, 0, tiled=True, axis_index_groups=groups)  4.73 us
  transfers between devices with their start and end apart: 9, of which 6 were waited for; matrix products, arithmetic and copies ran while one was open for 2% of the time, Pallas kernels for 4%

profile of v8, /device:TPU:6, one launch (start us, length us, event | category | flops | bytes accessed | tf_op | source)
XLA Modules:
  0.0 81.5 jit_solution(6676933636980643263)
XLA Ops:
  0.6 1.3 %copy-done = bf16[1,1,2,64,5120]{4,3,2,1,0:T(8,128)(2,1)S(1)} copy-done((bf16[1,1,2,64,5120]{4,3,2,1,0:T(8,128)(2,1)S(1)}, bf16[1,1,2,64,5120]{4,3,2,1,0:T(8,128)(2,1)}, u32[]{:S(2)}) %copy-start) | copy-done | bytes 1310744
  2.0 0.5 main.1
  2.5 3.5 %collective-permute-start = (f32[4,8,5120]{2,1,0:T(8,128)S(1)}, f32[4,8,5120]{2,1,0:T(8,128)S(1)}, u32[]{:S(2)}, u32[]{:S(2)}) collective-permute-start(f32[4,8,5120]{2,1,0:T(8,128)S(1)} %get-tuple-element.16), channel_id=1, source_target_pairs={{0,1},{1,0},{2,3},{3,2},{4,5},{5,4},{6,7},{7,6},{8,9},{9,8},{10,11... | collective-permute-start | bytes 1966088 | tf_op jit(solution)/shard_map/ppermute | solution.py:228
  6.0 1.4 %coef.1 = (f32[2,4,8,640]{3,2,1,0:T(8,128)S(1)}, f32[2,4,8,640]{3,2,1,0:T(8,128)S(1)}) custom-call(s32[8]{0:T(128)S(1)} %copy-done.4, bf16[2,64,5120]{2,1,0:T(8,128)(2,1)S(1)} %bitcast.18), custom_call_target="tpu_custom_call" | custom-call | flops 500000000 | bytes 2000000 | tf_op jit(solution)/shard_map/coef/pallas_call | solution.py:114
  7.4 9.1 %collective-permute-start.2 = (f32[2,4,8,640]{3,2,1,0:T(8,128)S(1)}, f32[2,4,8,640]{3,2,1,0:T(8,128)S(1)}, u32[]{:S(2)}, u32[]{:S(2)}) collective-permute-start(f32[2,4,8,640]{3,2,1,0:T(8,128)S(1)} %get-tuple-element.17), channel_id=1, source_target_pairs={{0,4},{1,5},{2,6},{3,7},{4,0},{5,1},{6,2},{7,3},{8,12},{9,13},{10,... | collective-permute-start | bytes 491528 | tf_op jit(solution)/shard_map/ppermute | solution.py:228
  16.5 1.1 %state.1 = (f32[8,640]{1,0:T(8,128)S(1)}, f32[128,128]{1,0:T(8,128)S(1)}, bf16[128,1024]{1,0:T(8,128)(2,1)S(1)}, bf16[128,1024]{1,0:T(8,128)(2,1)S(1)}) custom-call(s32[8]{0:T(128)S(1)} %copy-done.4, f32[1,2,4,5120]{3,2,1,0:T(4,128)S(1)} %copy-done.3), custom_call_target="tpu_custom_call" | custom-call | flops 100000000 | bytes 1000000 | tf_op jit(solution)/shard_map/state/pallas_call | solution.py:150
  17.7 4.1 %collective-permute-start.1 = (f32[4,8,5120]{2,1,0:T(8,128)S(1)}, f32[4,8,5120]{2,1,0:T(8,128)S(1)}, u32[]{:S(2)}, u32[]{:S(2)}) collective-permute-start(f32[4,8,5120]{2,1,0:T(8,128)S(1)} %bitcast_add_fusion.1), channel_id=1, source_target_pairs={{0,3},{1,2},{2,1},{3,0},{4,7},{5,6},{6,5},{7,4},{8,11},{9,10},{10,... | collective-permute-start | bytes 1966088 | tf_op jit(solution)/shard_map/ppermute | solution.py:228
  21.7 2.6 %collective-permute-start.4 = (f32[4,8,5120]{2,1,0:T(8,128)S(1)}, f32[4,8,5120]{2,1,0:T(8,128)S(1)}, u32[]{:S(2)}, u32[]{:S(2)}) collective-permute-start(f32[4,8,5120]{2,1,0:T(8,128)S(1)} %get-tuple-element.25), channel_id=1, source_target_pairs={{0,1},{1,0},{2,3},{3,2},{4,5},{5,4},{6,7},{7,6},{8,9},{9,8},{10,11... | collective-permute-start | bytes 1966088 | tf_op jit(solution)/shard_map/ppermute | solution.py:228
  24.4 0.8 collective-permute-done.2
  25.2 9.6 %collective-permute-start.3 = (f32[4,8,640]{2,1,0:T(8,128)S(1)}, f32[4,8,640]{2,1,0:T(8,128)S(1)}, u32[]{:S(2)}, u32[]{:S(2)}) collective-permute-start(f32[4,8,640]{2,1,0:T(8,128)S(1)} %fusion.3), channel_id=1, source_target_pairs={{0,12},{1,13},{2,14},{3,15},{4,8},{5,9},{6,10},{7,11},{8,4},{9,5},... | collective-permute-start | bytes 245768 | tf_op jit(solution)/shard_map/ppermute | solution.py:228
  34.8 2.7 %collective-permute-done.3 = f32[4,8,640]{2,1,0:T(8,128)S(1)} collective-permute-done((f32[4,8,640]{2,1,0:T(8,128)S(1)}, f32[4,8,640]{2,1,0:T(8,128)S(1)}, u32[]{:S(2)}, u32[]{:S(2)}) %collective-permute-start.3) | collective-permute-done | bytes 81952 | tf_op jit(solution)/shard_map/ppermute | solution.py:228
  37.5 3.0 %collective-permute-done.4 = f32[4,8,5120]{2,1,0:T(8,128)S(1)} collective-permute-done((f32[4,8,5120]{2,1,0:T(8,128)S(1)}, f32[4,8,5120]{2,1,0:T(8,128)S(1)}, u32[]{:S(2)}, u32[]{:S(2)}) %collective-permute-start.4) | collective-permute-done | bytes 655392 | tf_op jit(solution)/shard_map/ppermute | solution.py:228
  40.7 6.1 %collective-permute-start.5 = (f32[2,8,5120]{2,1,0:T(8,128)S(1)}, f32[2,8,5120]{2,1,0:T(8,128)S(1)}, u32[]{:S(2)}, u32[]{:S(2)}) collective-permute-start(f32[2,8,5120]{2,1,0:T(8,128)S(1)} %slice.47), channel_id=1, source_target_pairs={{0,4},{1,5},{2,6},{3,7},{4,0},{5,1},{6,2},{7,3},{8,12},{9,13},{10,... | collective-permute-start | bytes 983048 | tf_op jit(solution)/shard_map/ppermute | solution.py:228
  46.8 8.1 %all_to_all.15 = f32[4,8,640]{2,1,0:T(8,128)S(1)} all-to-all(f32[4,8,640]{2,1,0:T(8,128)S(1)} %fusion.5), channel_id=1, replica_groups={{0,1,2,3},{4,5,6,7},{8,9,10,11},{12,13,14,15},{16,17,18,19},{20,21,22,2..., dimensions={0} | all-to-all | bytes 163840 | tf_op jit(solution)/shard_map/all_to_all | solution.py:240
  54.9 0.7 broadcast_in_dim.6
  55.6 5.4 %all-to-all-start.1 = ((f32[8,8,640]{2,1,0:T(8,128)}), f32[8,8,640]{2,1,0:T(8,128)S(1)}, u32[]{:S(2)}, u32[]{:S(2)}) async-start(f32[8,8,640]{2,1,0:T(8,128)} %broadcast_in_dim.6), calls=%async_computation.1 | async-start | bytes 327680 | tf_op jit(solution)/shard_map/all_to_all | solution.py:240
  61.0 3.0 %collective-permute-done.5 = f32[2,8,5120]{2,1,0:T(8,128)S(1)} collective-permute-done((f32[2,8,5120]{2,1,0:T(8,128)S(1)}, f32[2,8,5120]{2,1,0:T(8,128)S(1)}, u32[]{:S(2)}, u32[]{:S(2)}) %collective-permute-start.5) | collective-permute-done | bytes 327712 | tf_op jit(solution)/shard_map/ppermute | solution.py:228
  64.0 3.3 %collective-permute-start.6 = (f32[8,5120]{1,0:T(8,128)S(1)}, f32[8,5120]{1,0:T(8,128)S(1)}, u32[]{:S(2)}, u32[]{:S(2)}) collective-permute-start(f32[8,5120]{1,0:T(8,128)S(1)} %get-tuple-element.28), channel_id=1, source_target_pairs={{0,12},{1,13},{2,14},{3,15},{4,8},{5,9},{6,10},{7,11},{8,4},{9,5},... | collective-permute-start | bytes 491528 | tf_op jit(solution)/shard_map/ppermute | solution.py:228
  67.3 0.9 %all-to-all-done.1 = f32[8,8,640]{2,1,0:T(8,128)S(1)} async-done(((f32[8,8,640]{2,1,0:T(8,128)}), f32[8,8,640]{2,1,0:T(8,128)S(1)}, u32[]{:S(2)}, u32[]{:S(2)}) %all-to-all-start.1) | async-done | bytes 163872 | tf_op jit(solution)/shard_map/all_to_all | solution.py:240
  68.3 0.6 broadcast_in_dim.7
  68.9 4.7 %all-to-all-start.2 = ((f32[4,8,640]{2,1,0:T(8,128)}), f32[4,8,640]{2,1,0:T(8,128)S(1)}, u32[]{:S(2)}, u32[]{:S(2)}) async-start(f32[4,8,640]{2,1,0:T(8,128)} %broadcast_in_dim.7), calls=%async_computation.2 | async-start | bytes 163840 | tf_op jit(solution)/shard_map/all_to_all | solution.py:232
  73.6 6.0 %collective-permute-done.6.got_ref = f32[8,5120]{1,0:T(8,128)S(1)} collective-permute-done((f32[8,5120]{1,0:T(8,128)S(1)}, f32[8,5120]{1,0:T(8,128)S(1)}, u32[]{:S(2)}, u32[]{:S(2)}) %collective-permute-start.6) | collective-permute-done | bytes 163872 | tf_op jit(solution)/shard_map/ppermute | solution.py:228
  79.7 1.0 %momentum.1 = f32[1,2,4,5120]{3,2,1,0:T(4,128)} custom-call(f32[8,5120]{1,0:T(8,128)S(1)} %get-tuple-element.29.own_ref, f32[8,5120]{1,0:T(8,128)S(1)} %collective-permute-done.6.got_ref, f32[1,2,4,5120]{3,2,1,0:T(4,128)S(1)} %copy-done.3, f32[128,128]{1,0:T(8,128)S(1)} %get-tuple-element.27.reject_ref), custom_call_target="tpu_custom_call" | custom-call | flops 60000000 | bytes 700000 | tf_op jit(solution)/shard_map/momentum/pallas_call | solution.py:178
  80.6 0.9 %params.1 = f32[2,4,5120]{2,1,0:T(4,128)} custom-call(f32[4,8,640]{2,1,0:T(8,128)S(1)} %all-to-all-done.2.parts_ref, f32[2,4,5120]{2,1,0:T(4,128)S(1)} %copy-done.2, bf16[128,1024]{1,0:T(8,128)(2,1)S(1)} %get-tuple-element.23.expand_ref, bf16[128,1024]{1,0:T(8,128)(2,1)S(1)} %get-tuple-element.24.rest_ref), custom_call_target="tpu_custom_call" | custom-call | flops 60000000 | bytes 700000 | tf_op jit(solution)/shard_map/params/pallas_call | solution.py:206
  (21 shorter events, 0.4 us)
Async XLA Ops:
  0.6 5.3 %copy-start.4 = (s32[8]{0:T(128)S(1)}, s32[8]{0:T(128)}, u32[]{:S(2)}) copy-start(s32[8]{0:T(128)} %kept_ref.3) | copy-start | bytes 100
  0.6 1.3 %copy-start = (bf16[1,1,2,64,5120]{4,3,2,1,0:T(8,128)(2,1)S(1)}, bf16[1,1,2,64,5120]{4,3,2,1,0:T(8,128)(2,1)}, u32[]{:S(2)}) copy-start(bf16[1,1,2,64,5120]{4,3,2,1,0:T(8,128)(2,1)} %param.4) | copy-start | bytes 3932164
  2.0 4.0 %copy-start.1 = (bf16[1,1,2,64,5120]{4,3,2,1,0:T(8,128)(2,1)S(1)}, bf16[1,1,2,64,5120]{4,3,2,1,0:T(8,128)(2,1)}, u32[]{:S(2)}) copy-start(bf16[1,1,2,64,5120]{4,3,2,1,0:T(8,128)(2,1)} %param.4) | copy-start | bytes 3932164
  2.0 14.5 %copy-start.3 = (f32[1,2,4,5120]{3,2,1,0:T(4,128)S(1)}, f32[1,2,4,5120]{3,2,1,0:T(4,128)}, u32[]{:S(2)}) copy-start(f32[1,2,4,5120]{3,2,1,0:T(4,128)} %momentum_ref.3) | copy-start | bytes 491524
  2.5 15.1 %collective-permute-start = (f32[4,8,5120]{2,1,0:T(8,128)S(1)}, f32[4,8,5120]{2,1,0:T(8,128)S(1)}, u32[]{:S(2)}, u32[]{:S(2)}) collective-permute-start(f32[4,8,5120]{2,1,0:T(8,128)S(1)} %get-tuple-element.16), channel_id=1, source_target_pairs={{0,1},{1,0},{2,3},{3,2},{4,5},{5,4},{6,7},{7,6},{8,9},{9,8},{10,11... | collective-permute-start | bytes 1966088 | tf_op jit(solution)/shard_map/ppermute | solution.py:228
  7.4 17.8 %collective-permute-start.2 = (f32[2,4,8,640]{3,2,1,0:T(8,128)S(1)}, f32[2,4,8,640]{3,2,1,0:T(8,128)S(1)}, u32[]{:S(2)}, u32[]{:S(2)}) collective-permute-start(f32[2,4,8,640]{3,2,1,0:T(8,128)S(1)} %get-tuple-element.17), channel_id=1, source_target_pairs={{0,4},{1,5},{2,6},{3,7},{4,0},{5,1},{6,2},{7,3},{8,12},{9,13},{10,... | collective-permute-start | bytes 491528 | tf_op jit(solution)/shard_map/ppermute | solution.py:228
  17.7 19.8 %collective-permute-start.1 = (f32[4,8,5120]{2,1,0:T(8,128)S(1)}, f32[4,8,5120]{2,1,0:T(8,128)S(1)}, u32[]{:S(2)}, u32[]{:S(2)}) collective-permute-start(f32[4,8,5120]{2,1,0:T(8,128)S(1)} %bitcast_add_fusion.1), channel_id=1, source_target_pairs={{0,3},{1,2},{2,1},{3,0},{4,7},{5,6},{6,5},{7,4},{8,11},{9,10},{10,... | collective-permute-start | bytes 1966088 | tf_op jit(solution)/shard_map/ppermute | solution.py:228
  21.7 18.8 %collective-permute-start.4 = (f32[4,8,5120]{2,1,0:T(8,128)S(1)}, f32[4,8,5120]{2,1,0:T(8,128)S(1)}, u32[]{:S(2)}, u32[]{:S(2)}) collective-permute-start(f32[4,8,5120]{2,1,0:T(8,128)S(1)} %get-tuple-element.25), channel_id=1, source_target_pairs={{0,1},{1,0},{2,3},{3,2},{4,5},{5,4},{6,7},{7,6},{8,9},{9,8},{10,11... | collective-permute-start | bytes 1966088 | tf_op jit(solution)/shard_map/ppermute | solution.py:228
  25.2 12.3 %collective-permute-start.3 = (f32[4,8,640]{2,1,0:T(8,128)S(1)}, f32[4,8,640]{2,1,0:T(8,128)S(1)}, u32[]{:S(2)}, u32[]{:S(2)}) collective-permute-start(f32[4,8,640]{2,1,0:T(8,128)S(1)} %fusion.3), channel_id=1, source_target_pairs={{0,12},{1,13},{2,14},{3,15},{4,8},{5,9},{6,10},{7,11},{8,4},{9,5},... | collective-permute-start | bytes 245768 | tf_op jit(solution)/shard_map/ppermute | solution.py:228
  40.7 23.3 %collective-permute-start.5 = (f32[2,8,5120]{2,1,0:T(8,128)S(1)}, f32[2,8,5120]{2,1,0:T(8,128)S(1)}, u32[]{:S(2)}, u32[]{:S(2)}) collective-permute-start(f32[2,8,5120]{2,1,0:T(8,128)S(1)} %slice.47), channel_id=1, source_target_pairs={{0,4},{1,5},{2,6},{3,7},{4,0},{5,1},{6,2},{7,3},{8,12},{9,13},{10,... | collective-permute-start | bytes 983048 | tf_op jit(solution)/shard_map/ppermute | solution.py:228
  54.9 25.7 %copy-start.2 = (f32[2,4,5120]{2,1,0:T(4,128)S(1)}, f32[2,4,5120]{2,1,0:T(4,128)}, u32[]{:S(2)}) copy-start(f32[2,4,5120]{2,1,0:T(4,128)} %params_ref.1) | copy-start | bytes 491524
  55.6 12.6 %all-to-all-start.1 = ((f32[8,8,640]{2,1,0:T(8,128)}), f32[8,8,640]{2,1,0:T(8,128)S(1)}, u32[]{:S(2)}, u32[]{:S(2)}) async-start(f32[8,8,640]{2,1,0:T(8,128)} %broadcast_in_dim.6), calls=%async_computation.1 | async-start | bytes 327680 | tf_op jit(solution)/shard_map/all_to_all | solution.py:240
  64.0 15.6 %collective-permute-start.6 = (f32[8,5120]{1,0:T(8,128)S(1)}, f32[8,5120]{1,0:T(8,128)S(1)}, u32[]{:S(2)}, u32[]{:S(2)}) collective-permute-start(f32[8,5120]{1,0:T(8,128)S(1)} %get-tuple-element.28), channel_id=1, source_target_pairs={{0,12},{1,13},{2,14},{3,15},{4,8},{5,9},{6,10},{7,11},{8,4},{9,5},... | collective-permute-start | bytes 491528 | tf_op jit(solution)/shard_map/ppermute | solution.py:228
  68.9 11.7 %all-to-all-start.2 = ((f32[4,8,640]{2,1,0:T(8,128)}), f32[4,8,640]{2,1,0:T(8,128)S(1)}, u32[]{:S(2)}, u32[]{:S(2)}) async-start(f32[4,8,640]{2,1,0:T(8,128)} %broadcast_in_dim.7), calls=%async_computation.2 | async-start | bytes 163840 | tf_op jit(solution)/shard_map/all_to_all | solution.py:232

commit v9 on v8

--- a/solution.py
+++ b/solution.py
@@ -140,8 +140,11 @@
     state = 0.9 * jnp.concatenate([momentum_ref[0, 0], momentum_ref[0, 1]], axis=0)
     deep = jnp.concatenate([state[:, c * WIDE:(c + 1) * WIDE] for c in range(CHUNKS)], axis=0)
     coef = jnp.dot(deep, wide, precision=HIGHEST, preferred_element_type=jnp.float32)
-    for c in range(CHUNKS):
-        coef_ref[:, c * 128:(c + 1) * 128] = coef[c * OWN:(c + 1) * OWN]
+    y = lax.axis_index("fsdp") % 4
+    for c in range(CHUNKS):
+        part = coef[c * OWN:(c + 1) * OWN]
+        for slot in range(4):
+            coef_ref[slot, :, c * 128:(c + 1) * 128] = jnp.where(slot == y, part, 0.0)
 
 
 def state_of(kept, momentum):
@@ -150,7 +153,7 @@
     return pl.pallas_call(
         state_kernel,
         out_shape=(
-            jax.ShapeDtypeStruct((OWN, COEFFS), jnp.float32),
+            jax.ShapeDtypeStruct((4, OWN, COEFFS), jnp.float32),
             jax.ShapeDtypeStruct((128, 128), jnp.float32),
             jax.ShapeDtypeStruct((128, WIDE), jnp.bfloat16),
             jax.ShapeDtypeStruct((128, WIDE), jnp.bfloat16),
@@ -246,7 +249,11 @@
 
 Y_GROUPS = [[z * 4 + y for y in range(4)] for z in range(4)]
 PLANE_GROUPS = [[z * 8 + x * 2 + c for x in range(4)] for z in range(4) for c in range(2)]
-COLUMN_GROUPS = [[z * 8 + x * 2 + c for z in range(4) for c in range(2)] for x in range(4)]
+COLUMN_GROUPS = [[z * 8 + i for z in range(4)] for i in range(8)]
+PAIR_GROUPS = [
+    [(lo * 8 + x * 2 + c) * N_FSDP + hi * 4 + y for c in range(2) for y in range(4)]
+    for lo in range(4) for x in range(4) for hi in range(4)
+]
 
 
 def after(x, earlier):
@@ -271,7 +278,8 @@
     main = main[0] + near + last
     got = halve(main[2:], 0, "z")
 
-    coef = sum_over(coef, "fsdp", Y_GROUPS) + state_coef
+    coef = coef + state_coef
+    coef = sum_over(jnp.broadcast_to(coef, (2, *coef.shape)).reshape(8, OWN, COEFFS), BOTH, PAIR_GROUPS)
     last = halve(main[1] + got[1], 1, "z")
     coef = share(coef, COLUMN_GROUPS)
     coef = share_parts(coef, PLANE_GROUPS)

time: 83.1 us -> 81.8 us (0.984)
  blocking collectives: 8.08 us -> 19.2 us
  starting transfers between devices: 48.4 us -> 41.6 us
  waiting for transfers between devices: 16.4 us -> 12.1 us
    all_to_all x0 -> x1, blocking collectives: none -> 8.21 us  [deal(): return lax.all_to_all(x, axis, 0, 0, tiled=True, axis_index_groups=groups)]
    all_to_all x1 -> x0, starting transfers between devices: 4.73 us -> none  [deal(): return lax.all_to_all(x, axis, 0, 0, tiled=True, axis_index_groups=groups)]
    ppermute x7, waiting for transfers between devices: 15.5 us -> 11.8 us  [halve(): return lax.ppermute(x, BOTH, sum_pairs(step, axis))]
    all_to_all x1, blocking collectives: 8.08 us -> 11 us  [sum_over(): lax.all_to_all(x, axis, 0, 0, tiled=True, axis_index_groups=groups)]
    all_to_all x1, starting transfers between devices: 5.41 us -> 3.29 us  [sum_over(): lax.all_to_all(x, axis, 0, 0, tiled=True, axis_index_groups=groups)]
  transfers between devices with their start and end apart: 9 -> 8, of which waited for: 6 -> 6; matrix products, arithmetic and copies ran while one was open for 2% -> 1% of each run, Pallas kernels for 4% -> 4%
where the time goes in v9:
time: 81.8 us; the launch traced here: 80.9 us
  starting transfers between devices  41.6 us (51%)
  blocking collectives  19.2 us (23%)
  waiting for transfers between devices  12.1 us (15%)
  Pallas kernels  4.81 us (6%)
  local copies, waits for them, and re-layouts  2.02 us (2%)
  between operations  0.83 us (1%)
    ppermute x7, starting transfers between devices, halve(): return lax.ppermute(x, BOTH, sum_pairs(step, axis))  38.4 us
    ppermute x7, waiting for transfers between devices, halve(): return lax.ppermute(x, BOTH, sum_pairs(step, axis))  11.8 us
    all_to_all x1, blocking collectives, sum_over(): lax.all_to_all(x, axis, 0, 0, tiled=True, axis_index_groups=groups)  11 us
    all_to_all x1, blocking collectives, deal(): return lax.all_to_all(x, axis, 0, 0, tiled=True, axis_index_groups=groups)  8.21 us
    all_to_all x1, starting transfers between devices, sum_over(): lax.all_to_all(x, axis, 0, 0, tiled=True, axis_index_groups=groups)  3.29 us
  transfers between devices with their start and end apart: 8, of which 6 were waited for; matrix products, arithmetic and copies ran while one was open for 1% of the time, Pallas kernels for 4%

profile of v9, /device:TPU:6, one launch (start us, length us, event | category | flops | bytes accessed | tf_op | source)
XLA Modules:
  0.0 80.9 jit_solution(3496379252482035394)
XLA Ops:
  0.6 1.3 %copy-done = bf16[1,1,2,64,5120]{4,3,2,1,0:T(8,128)(2,1)S(1)} copy-done((bf16[1,1,2,64,5120]{4,3,2,1,0:T(8,128)(2,1)S(1)}, bf16[1,1,2,64,5120]{4,3,2,1,0:T(8,128)(2,1)}, u32[]{:S(2)}) %copy-start) | copy-done | bytes 1310744
  2.0 0.5 main.1
  2.5 3.5 %collective-permute-start = (f32[4,8,5120]{2,1,0:T(8,128)S(1)}, f32[4,8,5120]{2,1,0:T(8,128)S(1)}, u32[]{:S(2)}, u32[]{:S(2)}) collective-permute-start(f32[4,8,5120]{2,1,0:T(8,128)S(1)} %get-tuple-element.16), channel_id=1, source_target_pairs={{0,1},{1,0},{2,3},{3,2},{4,5},{5,4},{6,7},{7,6},{8,9},{9,8},{10,11... | collective-permute-start | bytes 1966088 | tf_op jit(solution)/shard_map/ppermute | solution.py:231
  6.0 1.4 %coef.1 = (f32[2,4,8,640]{3,2,1,0:T(8,128)S(1)}, f32[2,4,8,640]{3,2,1,0:T(8,128)S(1)}) custom-call(s32[8]{0:T(128)S(1)} %copy-done.4, bf16[2,64,5120]{2,1,0:T(8,128)(2,1)S(1)} %bitcast.19), custom_call_target="tpu_custom_call" | custom-call | flops 500000000 | bytes 2000000 | tf_op jit(solution)/shard_map/coef/pallas_call | solution.py:114
  7.4 9.1 %collective-permute-start.2 = (f32[2,4,8,640]{3,2,1,0:T(8,128)S(1)}, f32[2,4,8,640]{3,2,1,0:T(8,128)S(1)}, u32[]{:S(2)}, u32[]{:S(2)}) collective-permute-start(f32[2,4,8,640]{3,2,1,0:T(8,128)S(1)} %get-tuple-element.17), channel_id=1, source_target_pairs={{0,4},{1,5},{2,6},{3,7},{4,0},{5,1},{6,2},{7,3},{8,12},{9,13},{10,... | collective-permute-start | bytes 491528 | tf_op jit(solution)/shard_map/ppermute | solution.py:231
  16.5 1.1 %state.1 = (f32[4,8,640]{2,1,0:T(8,128)S(1)}, f32[128,128]{1,0:T(8,128)S(1)}, bf16[128,1024]{1,0:T(8,128)(2,1)S(1)}, bf16[128,1024]{1,0:T(8,128)(2,1)S(1)}) custom-call(s32[8]{0:T(128)S(1)} %copy-done.4, f32[1,2,4,5120]{3,2,1,0:T(4,128)S(1)} %copy-done.3), custom_call_target="tpu_custom_call" | custom-call | flops 100000000 | bytes 1000000 | tf_op jit(solution)/shard_map/state/pallas_call | solution.py:153
  17.7 4.1 %collective-permute-start.1 = (f32[4,8,5120]{2,1,0:T(8,128)S(1)}, f32[4,8,5120]{2,1,0:T(8,128)S(1)}, u32[]{:S(2)}, u32[]{:S(2)}) collective-permute-start(f32[4,8,5120]{2,1,0:T(8,128)S(1)} %bitcast_add_fusion.1), channel_id=1, source_target_pairs={{0,3},{1,2},{2,1},{3,0},{4,7},{5,6},{6,5},{7,4},{8,11},{9,10},{10,... | collective-permute-start | bytes 1966088 | tf_op jit(solution)/shard_map/ppermute | solution.py:231
  21.8 2.6 %collective-permute-start.4 = (f32[4,8,5120]{2,1,0:T(8,128)S(1)}, f32[4,8,5120]{2,1,0:T(8,128)S(1)}, u32[]{:S(2)}, u32[]{:S(2)}) collective-permute-start(f32[4,8,5120]{2,1,0:T(8,128)S(1)} %get-tuple-element.25), channel_id=1, source_target_pairs={{0,1},{1,0},{2,3},{3,2},{4,5},{5,4},{6,7},{7,6},{8,9},{9,8},{10,11... | collective-permute-start | bytes 1966088 | tf_op jit(solution)/shard_map/ppermute | solution.py:231
  24.4 0.8 collective-permute-done.2
  25.2 9.7 %collective-permute-start.3 = (f32[4,8,640]{2,1,0:T(8,128)S(1)}, f32[4,8,640]{2,1,0:T(8,128)S(1)}, u32[]{:S(2)}, u32[]{:S(2)}) collective-permute-start(f32[4,8,640]{2,1,0:T(8,128)S(1)} %fusion.3), channel_id=1, source_target_pairs={{0,12},{1,13},{2,14},{3,15},{4,8},{5,9},{6,10},{7,11},{8,4},{9,5},... | collective-permute-start | bytes 245768 | tf_op jit(solution)/shard_map/ppermute | solution.py:231
  34.8 2.7 %collective-permute-done.3 = f32[4,8,640]{2,1,0:T(8,128)S(1)} collective-permute-done((f32[4,8,640]{2,1,0:T(8,128)S(1)}, f32[4,8,640]{2,1,0:T(8,128)S(1)}, u32[]{:S(2)}, u32[]{:S(2)}) %collective-permute-start.3) | collective-permute-done | bytes 81952 | tf_op jit(solution)/shard_map/ppermute | solution.py:231
  37.5 3.1 %collective-permute-done.4 = f32[4,8,5120]{2,1,0:T(8,128)S(1)} collective-permute-done((f32[4,8,5120]{2,1,0:T(8,128)S(1)}, f32[4,8,5120]{2,1,0:T(8,128)S(1)}, u32[]{:S(2)}, u32[]{:S(2)}) %collective-permute-start.4) | collective-permute-done | bytes 655392 | tf_op jit(solution)/shard_map/ppermute | solution.py:231
  40.6 0.1 fusion
  40.8 6.2 %collective-permute-start.5 = (f32[2,8,5120]{2,1,0:T(8,128)S(1)}, f32[2,8,5120]{2,1,0:T(8,128)S(1)}, u32[]{:S(2)}, u32[]{:S(2)}) collective-permute-start(f32[2,8,5120]{2,1,0:T(8,128)S(1)} %slice.47), channel_id=1, source_target_pairs={{0,4},{1,5},{2,6},{3,7},{4,0},{5,1},{6,2},{7,3},{8,12},{9,13},{10,... | collective-permute-start | bytes 983048 | tf_op jit(solution)/shard_map/ppermute | solution.py:231
  47.0 11.0 %all_to_all.15 = f32[8,8,640]{2,1,0:T(8,128)S(1)} all-to-all(f32[8,8,640]{2,1,0:T(8,128)S(1)} %bitcast.20), channel_id=1, replica_groups={{0,1,2,3,16,17,18,19},{4,5,6,7,20,21,22,23},{8,9,10,11,24,25,26,27},{12..., dimensions={0} | all-to-all | bytes 327680 | tf_op jit(solution)/shard_map/all_to_all | solution.py:243
  58.0 0.6 broadcast_in_dim.10
  58.6 3.3 %all-to-all-start.1 = ((f32[4,8,640]{2,1,0:T(8,128)}), f32[4,8,640]{2,1,0:T(8,128)S(1)}, u32[]{:S(2)}, u32[]{:S(2)}) async-start(f32[4,8,640]{2,1,0:T(8,128)} %broadcast_in_dim.10), calls=%async_computation.1 | async-start | bytes 163840 | tf_op jit(solution)/shard_map/all_to_all | solution.py:243
  61.9 2.3 %collective-permute-done.5 = f32[2,8,5120]{2,1,0:T(8,128)S(1)} collective-permute-done((f32[2,8,5120]{2,1,0:T(8,128)S(1)}, f32[2,8,5120]{2,1,0:T(8,128)S(1)}, u32[]{:S(2)}, u32[]{:S(2)}) %collective-permute-start.5) | collective-permute-done | bytes 327712 | tf_op jit(solution)/shard_map/ppermute | solution.py:231
  64.3 3.2 %collective-permute-start.6 = (f32[8,5120]{1,0:T(8,128)S(1)}, f32[8,5120]{1,0:T(8,128)S(1)}, u32[]{:S(2)}, u32[]{:S(2)}) collective-permute-start(f32[8,5120]{1,0:T(8,128)S(1)} %get-tuple-element.28), channel_id=1, source_target_pairs={{0,12},{1,13},{2,14},{3,15},{4,8},{5,9},{6,10},{7,11},{8,4},{9,5},... | collective-permute-start | bytes 491528 | tf_op jit(solution)/shard_map/ppermute | solution.py:231
  67.5 0.3 all-to-all-done.1
  67.8 8.2 %all_to_all.16.parts_ref = f32[4,8,640]{2,1,0:T(8,128)S(1)} all-to-all(f32[4,8,640]{2,1,0:T(8,128)S(1)} %broadcast_in_dim.11), channel_id=1, replica_groups={{0,32,64,96},{16,48,80,112},{128,160,192,224},{144,176,208,240},{256,28..., dimensions={0} | all-to-all | bytes 163840 | tf_op jit(solution)/shard_map/all_to_all | solution.py:235
  76.1 0.9 %params.1 = f32[2,4,5120]{2,1,0:T(4,128)} custom-call(f32[4,8,640]{2,1,0:T(8,128)S(1)} %all_to_all.16.parts_ref, f32[2,4,5120]{2,1,0:T(4,128)S(1)} %copy-done.2, bf16[128,1024]{1,0:T(8,128)(2,1)S(1)} %get-tuple-element.23.expand_ref, bf16[128,1024]{1,0:T(8,128)(2,1)S(1)} %get-tuple-element.24.rest_ref), custom_call_target="tpu_custom_call" | custom-call | flops 60000000 | bytes 700000 | tf_op jit(solution)/shard_map/params/pallas_call | solution.py:209
  77.0 3.0 %collective-permute-done.6.got_ref = f32[8,5120]{1,0:T(8,128)S(1)} collective-permute-done((f32[8,5120]{1,0:T(8,128)S(1)}, f32[8,5120]{1,0:T(8,128)S(1)}, u32[]{:S(2)}, u32[]{:S(2)}) %collective-permute-start.6) | collective-permute-done | bytes 163872 | tf_op jit(solution)/shard_map/ppermute | solution.py:231
  80.0 1.0 %momentum.1 = f32[1,2,4,5120]{3,2,1,0:T(4,128)} custom-call(f32[8,5120]{1,0:T(8,128)S(1)} %get-tuple-element.29.own_ref, f32[8,5120]{1,0:T(8,128)S(1)} %collective-permute-done.6.got_ref, f32[1,2,4,5120]{3,2,1,0:T(4,128)S(1)} %copy-done.3, f32[128,128]{1,0:T(8,128)S(1)} %get-tuple-element.27.reject_ref), custom_call_target="tpu_custom_call" | custom-call | flops 60000000 | bytes 700000 | tf_op jit(solution)/shard_map/momentum/pallas_call | solution.py:181
  (21 shorter events, 0.3 us)
Async XLA Ops:
  0.6 5.3 %copy-start.4 = (s32[8]{0:T(128)S(1)}, s32[8]{0:T(128)}, u32[]{:S(2)}) copy-start(s32[8]{0:T(128)} %kept_ref.3) | copy-start | bytes 100
  0.6 1.3 %copy-start = (bf16[1,1,2,64,5120]{4,3,2,1,0:T(8,128)(2,1)S(1)}, bf16[1,1,2,64,5120]{4,3,2,1,0:T(8,128)(2,1)}, u32[]{:S(2)}) copy-start(bf16[1,1,2,64,5120]{4,3,2,1,0:T(8,128)(2,1)} %param.4) | copy-start | bytes 3932164
  2.0 4.0 %copy-start.1 = (bf16[1,1,2,64,5120]{4,3,2,1,0:T(8,128)(2,1)S(1)}, bf16[1,1,2,64,5120]{4,3,2,1,0:T(8,128)(2,1)}, u32[]{:S(2)}) copy-start(bf16[1,1,2,64,5120]{4,3,2,1,0:T(8,128)(2,1)} %param.4) | copy-start | bytes 3932164
  2.0 14.5 %copy-start.3 = (f32[1,2,4,5120]{3,2,1,0:T(4,128)S(1)}, f32[1,2,4,5120]{3,2,1,0:T(4,128)}, u32[]{:S(2)}) copy-start(f32[1,2,4,5120]{3,2,1,0:T(4,128)} %momentum_ref.3) | copy-start | bytes 491524
  2.5 15.1 %collective-permute-start = (f32[4,8,5120]{2,1,0:T(8,128)S(1)}, f32[4,8,5120]{2,1,0:T(8,128)S(1)}, u32[]{:S(2)}, u32[]{:S(2)}) collective-permute-start(f32[4,8,5120]{2,1,0:T(8,128)S(1)} %get-tuple-element.16), channel_id=1, source_target_pairs={{0,1},{1,0},{2,3},{3,2},{4,5},{5,4},{6,7},{7,6},{8,9},{9,8},{10,11... | collective-permute-start | bytes 1966088 | tf_op jit(solution)/shard_map/ppermute | solution.py:231
  7.4 17.8 %collective-permute-start.2 = (f32[2,4,8,640]{3,2,1,0:T(8,128)S(1)}, f32[2,4,8,640]{3,2,1,0:T(8,128)S(1)}, u32[]{:S(2)}, u32[]{:S(2)}) collective-permute-start(f32[2,4,8,640]{3,2,1,0:T(8,128)S(1)} %get-tuple-element.17), channel_id=1, source_target_pairs={{0,4},{1,5},{2,6},{3,7},{4,0},{5,1},{6,2},{7,3},{8,12},{9,13},{10,... | collective-permute-start | bytes 491528 | tf_op jit(solution)/shard_map/ppermute | solution.py:231
  17.7 19.8 %collective-permute-start.1 = (f32[4,8,5120]{2,1,0:T(8,128)S(1)}, f32[4,8,5120]{2,1,0:T(8,128)S(1)}, u32[]{:S(2)}, u32[]{:S(2)}) collective-permute-start(f32[4,8,5120]{2,1,0:T(8,128)S(1)} %bitcast_add_fusion.1), channel_id=1, source_target_pairs={{0,3},{1,2},{2,1},{3,0},{4,7},{5,6},{6,5},{7,4},{8,11},{9,10},{10,... | collective-permute-start | bytes 1966088 | tf_op jit(solution)/shard_map/ppermute | solution.py:231
  21.8 18.8 %collective-permute-start.4 = (f32[4,8,5120]{2,1,0:T(8,128)S(1)}, f32[4,8,5120]{2,1,0:T(8,128)S(1)}, u32[]{:S(2)}, u32[]{:S(2)}) collective-permute-start(f32[4,8,5120]{2,1,0:T(8,128)S(1)} %get-tuple-element.25), channel_id=1, source_target_pairs={{0,1},{1,0},{2,3},{3,2},{4,5},{5,4},{6,7},{7,6},{8,9},{9,8},{10,11... | collective-permute-start | bytes 1966088 | tf_op jit(solution)/shard_map/ppermute | solution.py:231
  25.2 12.3 %collective-permute-start.3 = (f32[4,8,640]{2,1,0:T(8,128)S(1)}, f32[4,8,640]{2,1,0:T(8,128)S(1)}, u32[]{:S(2)}, u32[]{:S(2)}) collective-permute-start(f32[4,8,640]{2,1,0:T(8,128)S(1)} %fusion.3), channel_id=1, source_target_pairs={{0,12},{1,13},{2,14},{3,15},{4,8},{5,9},{6,10},{7,11},{8,4},{9,5},... | collective-permute-start | bytes 245768 | tf_op jit(solution)/shard_map/ppermute | solution.py:231
  40.7 35.3 %copy-start.2 = (f32[2,4,5120]{2,1,0:T(4,128)S(1)}, f32[2,4,5120]{2,1,0:T(4,128)}, u32[]{:S(2)}) copy-start(f32[2,4,5120]{2,1,0:T(4,128)} %params_ref.1) | copy-start | bytes 491524
  40.8 23.5 %collective-permute-start.5 = (f32[2,8,5120]{2,1,0:T(8,128)S(1)}, f32[2,8,5120]{2,1,0:T(8,128)S(1)}, u32[]{:S(2)}, u32[]{:S(2)}) collective-permute-start(f32[2,8,5120]{2,1,0:T(8,128)S(1)} %slice.47), channel_id=1, source_target_pairs={{0,4},{1,5},{2,6},{3,7},{4,0},{5,1},{6,2},{7,3},{8,12},{9,13},{10,... | collective-permute-start | bytes 983048 | tf_op jit(solution)/shard_map/ppermute | solution.py:231
  58.6 9.2 %all-to-all-start.1 = ((f32[4,8,640]{2,1,0:T(8,128)}), f32[4,8,640]{2,1,0:T(8,128)S(1)}, u32[]{:S(2)}, u32[]{:S(2)}) async-start(f32[4,8,640]{2,1,0:T(8,128)} %broadcast_in_dim.10), calls=%async_computation.1 | async-start | bytes 163840 | tf_op jit(solution)/shard_map/all_to_all | solution.py:243
  64.3 15.7 %collective-permute-start.6 = (f32[8,5120]{1,0:T(8,128)S(1)}, f32[8,5120]{1,0:T(8,128)S(1)}, u32[]{:S(2)}, u32[]{:S(2)}) collective-permute-start(f32[8,5120]{1,0:T(8,128)S(1)} %get-tuple-element.28), channel_id=1, source_target_pairs={{0,12},{1,13},{2,14},{3,15},{4,8},{5,9},{6,10},{7,11},{8,4},{9,5},... | collective-permute-start | bytes 491528 | tf_op jit(solution)/shard_map/ppermute | solution.py:231

commit v10 on v9

--- a/solution.py
+++ b/solution.py
@@ -273,12 +273,11 @@
     last = halve(main[1] + across, 1, "y")
     coef_next = coef[1] + coef_got[1]
     coef_last = halve(coef_next, 1, "z")
-    coef = coef[0] + coef_got[0] + coef_last
+    coef = coef[0] + coef_got[0] + coef_last + state_coef
     last, coef = after(last, coef)
     main = main[0] + near + last
     got = halve(main[2:], 0, "z")
 
-    coef = coef + state_coef
     coef = sum_over(jnp.broadcast_to(coef, (2, *coef.shape)).reshape(8, OWN, COEFFS), BOTH, PAIR_GROUPS)
     last = halve(main[1] + got[1], 1, "z")
     coef = share(coef, COLUMN_GROUPS)

time: 81.8 us -> 81.8 us (level)
  no operation moved by 1% of the time
where the time goes in v10:
time: 81.8 us; the launch traced here: 80.9 us
  starting transfers between devices  41.7 us (51%)
  blocking collectives  19.2 us (23%)
  waiting for transfers between devices  12.1 us (15%)
  Pallas kernels  4.81 us (6%)
  local copies, waits for them, and re-layouts  2.02 us (2%)
  between operations  0.82 us (1%)
    ppermute x7, starting transfers between devices, halve(): return lax.ppermute(x, BOTH, sum_pairs(step, axis))  38.4 us
    ppermute x7, waiting for transfers between devices, halve(): return lax.ppermute(x, BOTH, sum_pairs(step, axis))  11.8 us
    all_to_all x1, blocking collectives, sum_over(): lax.all_to_all(x, axis, 0, 0, tiled=True, axis_index_groups=groups)  11 us
    all_to_all x1, blocking collectives, deal(): return lax.all_to_all(x, axis, 0, 0, tiled=True, axis_index_groups=groups)  8.21 us
    all_to_all x1, starting transfers between devices, sum_over(): lax.all_to_all(x, axis, 0, 0, tiled=True, axis_index_groups=groups)  3.29 us
  transfers between devices with their start and end apart: 8, of which 6 were waited for; matrix products, arithmetic and copies ran while one was open for 1% of the time, Pallas kernels for 4%

profile of v10, /device:TPU:6, one launch (start us, length us, event | category | flops | bytes accessed | tf_op | source)
XLA Modules:
  0.0 80.9 jit_solution(5352305491019442805)
XLA Ops:
  0.6 1.3 %copy-done = bf16[1,1,2,64,5120]{4,3,2,1,0:T(8,128)(2,1)S(1)} copy-done((bf16[1,1,2,64,5120]{4,3,2,1,0:T(8,128)(2,1)S(1)}, bf16[1,1,2,64,5120]{4,3,2,1,0:T(8,128)(2,1)}, u32[]{:S(2)}) %copy-start) | copy-done | bytes 1310744
  2.0 0.5 main.1
  2.5 3.5 %collective-permute-start = (f32[4,8,5120]{2,1,0:T(8,128)S(1)}, f32[4,8,5120]{2,1,0:T(8,128)S(1)}, u32[]{:S(2)}, u32[]{:S(2)}) collective-permute-start(f32[4,8,5120]{2,1,0:T(8,128)S(1)} %get-tuple-element.16), channel_id=1, source_target_pairs={{0,1},{1,0},{2,3},{3,2},{4,5},{5,4},{6,7},{7,6},{8,9},{9,8},{10,11... | collective-permute-start | bytes 1966088 | tf_op jit(solution)/shard_map/ppermute | solution.py:231
  6.0 1.4 %coef.1 = (f32[2,4,8,640]{3,2,1,0:T(8,128)S(1)}, f32[2,4,8,640]{3,2,1,0:T(8,128)S(1)}) custom-call(s32[8]{0:T(128)S(1)} %copy-done.4, bf16[2,64,5120]{2,1,0:T(8,128)(2,1)S(1)} %bitcast.21), custom_call_target="tpu_custom_call" | custom-call | flops 500000000 | bytes 2000000 | tf_op jit(solution)/shard_map/coef/pallas_call | solution.py:114
  7.4 9.1 %collective-permute-start.2 = (f32[2,4,8,640]{3,2,1,0:T(8,128)S(1)}, f32[2,4,8,640]{3,2,1,0:T(8,128)S(1)}, u32[]{:S(2)}, u32[]{:S(2)}) collective-permute-start(f32[2,4,8,640]{3,2,1,0:T(8,128)S(1)} %get-tuple-element.17), channel_id=1, source_target_pairs={{0,4},{1,5},{2,6},{3,7},{4,0},{5,1},{6,2},{7,3},{8,12},{9,13},{10,... | collective-permute-start | bytes 491528 | tf_op jit(solution)/shard_map/ppermute | solution.py:231
  16.5 1.1 %state.1 = (f32[4,8,640]{2,1,0:T(8,128)S(1)}, f32[128,128]{1,0:T(8,128)S(1)}, bf16[128,1024]{1,0:T(8,128)(2,1)S(1)}, bf16[128,1024]{1,0:T(8,128)(2,1)S(1)}) custom-call(s32[8]{0:T(128)S(1)} %copy-done.4, f32[1,2,4,5120]{3,2,1,0:T(4,128)S(1)} %copy-done.3), custom_call_target="tpu_custom_call" | custom-call | flops 100000000 | bytes 1000000 | tf_op jit(solution)/shard_map/state/pallas_call | solution.py:153
  17.7 4.1 %collective-permute-start.1 = (f32[4,8,5120]{2,1,0:T(8,128)S(1)}, f32[4,8,5120]{2,1,0:T(8,128)S(1)}, u32[]{:S(2)}, u32[]{:S(2)}) collective-permute-start(f32[4,8,5120]{2,1,0:T(8,128)S(1)} %bitcast_add_fusion.1), channel_id=1, source_target_pairs={{0,3},{1,2},{2,1},{3,0},{4,7},{5,6},{6,5},{7,4},{8,11},{9,10},{10,... | collective-permute-start | bytes 1966088 | tf_op jit(solution)/shard_map/ppermute | solution.py:231
  21.8 2.6 %collective-permute-start.4 = (f32[4,8,5120]{2,1,0:T(8,128)S(1)}, f32[4,8,5120]{2,1,0:T(8,128)S(1)}, u32[]{:S(2)}, u32[]{:S(2)}) collective-permute-start(f32[4,8,5120]{2,1,0:T(8,128)S(1)} %get-tuple-element.25), channel_id=1, source_target_pairs={{0,1},{1,0},{2,3},{3,2},{4,5},{5,4},{6,7},{7,6},{8,9},{9,8},{10,11... | collective-permute-start | bytes 1966088 | tf_op jit(solution)/shard_map/ppermute | solution.py:231
  24.4 0.8 collective-permute-done.2
  25.2 9.7 %collective-permute-start.3 = (f32[4,8,640]{2,1,0:T(8,128)S(1)}, f32[4,8,640]{2,1,0:T(8,128)S(1)}, u32[]{:S(2)}, u32[]{:S(2)}) collective-permute-start(f32[4,8,640]{2,1,0:T(8,128)S(1)} %fusion.3), channel_id=1, source_target_pairs={{0,12},{1,13},{2,14},{3,15},{4,8},{5,9},{6,10},{7,11},{8,4},{9,5},... | collective-permute-start | bytes 245768 | tf_op jit(solution)/shard_map/ppermute | solution.py:231
  34.8 2.7 %collective-permute-done.3 = f32[4,8,640]{2,1,0:T(8,128)S(1)} collective-permute-done((f32[4,8,640]{2,1,0:T(8,128)S(1)}, f32[4,8,640]{2,1,0:T(8,128)S(1)}, u32[]{:S(2)}, u32[]{:S(2)}) %collective-permute-start.3) | collective-permute-done | bytes 81952 | tf_op jit(solution)/shard_map/ppermute | solution.py:231
  37.5 3.0 %collective-permute-done.4 = f32[4,8,5120]{2,1,0:T(8,128)S(1)} collective-permute-done((f32[4,8,5120]{2,1,0:T(8,128)S(1)}, f32[4,8,5120]{2,1,0:T(8,128)S(1)}, u32[]{:S(2)}, u32[]{:S(2)}) %collective-permute-start.4) | collective-permute-done | bytes 655392 | tf_op jit(solution)/shard_map/ppermute | solution.py:231
  40.6 0.1 fusion
  40.8 6.2 %collective-permute-start.5 = (f32[2,8,5120]{2,1,0:T(8,128)S(1)}, f32[2,8,5120]{2,1,0:T(8,128)S(1)}, u32[]{:S(2)}, u32[]{:S(2)}) collective-permute-start(f32[2,8,5120]{2,1,0:T(8,128)S(1)} %slice.47), channel_id=1, source_target_pairs={{0,4},{1,5},{2,6},{3,7},{4,0},{5,1},{6,2},{7,3},{8,12},{9,13},{10,... | collective-permute-start | bytes 983048 | tf_op jit(solution)/shard_map/ppermute | solution.py:231
  47.0 11.0 %all_to_all.15 = f32[8,8,640]{2,1,0:T(8,128)S(1)} all-to-all(f32[8,8,640]{2,1,0:T(8,128)S(1)} %bitcast.22), channel_id=1, replica_groups={{0,1,2,3,16,17,18,19},{4,5,6,7,20,21,22,23},{8,9,10,11,24,25,26,27},{12..., dimensions={0} | all-to-all | bytes 327680 | tf_op jit(solution)/shard_map/all_to_all | solution.py:243
  58.0 0.6 broadcast_in_dim.10
  58.6 3.3 %all-to-all-start.1 = ((f32[4,8,640]{2,1,0:T(8,128)}), f32[4,8,640]{2,1,0:T(8,128)S(1)}, u32[]{:S(2)}, u32[]{:S(2)}) async-start(f32[4,8,640]{2,1,0:T(8,128)} %broadcast_in_dim.10), calls=%async_computation.1 | async-start | bytes 163840 | tf_op jit(solution)/shard_map/all_to_all | solution.py:243
  61.9 2.3 %collective-permute-done.5 = f32[2,8,5120]{2,1,0:T(8,128)S(1)} collective-permute-done((f32[2,8,5120]{2,1,0:T(8,128)S(1)}, f32[2,8,5120]{2,1,0:T(8,128)S(1)}, u32[]{:S(2)}, u32[]{:S(2)}) %collective-permute-start.5) | collective-permute-done | bytes 327712 | tf_op jit(solution)/shard_map/ppermute | solution.py:231
  64.3 3.2 %collective-permute-start.6 = (f32[8,5120]{1,0:T(8,128)S(1)}, f32[8,5120]{1,0:T(8,128)S(1)}, u32[]{:S(2)}, u32[]{:S(2)}) collective-permute-start(f32[8,5120]{1,0:T(8,128)S(1)} %get-tuple-element.28), channel_id=1, source_target_pairs={{0,12},{1,13},{2,14},{3,15},{4,8},{5,9},{6,10},{7,11},{8,4},{9,5},... | collective-permute-start | bytes 491528 | tf_op jit(solution)/shard_map/ppermute | solution.py:231
  67.5 0.3 all-to-all-done.1
  67.8 8.2 %all_to_all.16.parts_ref = f32[4,8,640]{2,1,0:T(8,128)S(1)} all-to-all(f32[4,8,640]{2,1,0:T(8,128)S(1)} %broadcast_in_dim.11), channel_id=1, replica_groups={{0,32,64,96},{16,48,80,112},{128,160,192,224},{144,176,208,240},{256,28..., dimensions={0} | all-to-all | bytes 163840 | tf_op jit(solution)/shard_map/all_to_all | solution.py:235
  76.0 0.9 %params.1 = f32[2,4,5120]{2,1,0:T(4,128)} custom-call(f32[4,8,640]{2,1,0:T(8,128)S(1)} %all_to_all.16.parts_ref, f32[2,4,5120]{2,1,0:T(4,128)S(1)} %copy-done.2, bf16[128,1024]{1,0:T(8,128)(2,1)S(1)} %get-tuple-element.23.expand_ref, bf16[128,1024]{1,0:T(8,128)(2,1)S(1)} %get-tuple-element.24.rest_ref), custom_call_target="tpu_custom_call" | custom-call | flops 60000000 | bytes 700000 | tf_op jit(solution)/shard_map/params/pallas_call | solution.py:209
  76.9 3.0 %collective-permute-done.6.got_ref = f32[8,5120]{1,0:T(8,128)S(1)} collective-permute-done((f32[8,5120]{1,0:T(8,128)S(1)}, f32[8,5120]{1,0:T(8,128)S(1)}, u32[]{:S(2)}, u32[]{:S(2)}) %collective-permute-start.6) | collective-permute-done | bytes 163872 | tf_op jit(solution)/shard_map/ppermute | solution.py:231
  79.9 1.0 %momentum.1 = f32[1,2,4,5120]{3,2,1,0:T(4,128)} custom-call(f32[8,5120]{1,0:T(8,128)S(1)} %get-tuple-element.29.own_ref, f32[8,5120]{1,0:T(8,128)S(1)} %collective-permute-done.6.got_ref, f32[1,2,4,5120]{3,2,1,0:T(4,128)S(1)} %copy-done.3, f32[128,128]{1,0:T(8,128)S(1)} %get-tuple-element.27.reject_ref), custom_call_target="tpu_custom_call" | custom-call | flops 60000000 | bytes 700000 | tf_op jit(solution)/shard_map/momentum/pallas_call | solution.py:181
  (20 shorter events, 0.3 us)
Async XLA Ops:
  0.6 5.3 %copy-start.4 = (s32[8]{0:T(128)S(1)}, s32[8]{0:T(128)}, u32[]{:S(2)}) copy-start(s32[8]{0:T(128)} %kept_ref.3) | copy-start | bytes 100
  0.6 1.3 %copy-start = (bf16[1,1,2,64,5120]{4,3,2,1,0:T(8,128)(2,1)S(1)}, bf16[1,1,2,64,5120]{4,3,2,1,0:T(8,128)(2,1)}, u32[]{:S(2)}) copy-start(bf16[1,1,2,64,5120]{4,3,2,1,0:T(8,128)(2,1)} %param.4) | copy-start | bytes 3932164
  2.0 4.0 %copy-start.1 = (bf16[1,1,2,64,5120]{4,3,2,1,0:T(8,128)(2,1)S(1)}, bf16[1,1,2,64,5120]{4,3,2,1,0:T(8,128)(2,1)}, u32[]{:S(2)}) copy-start(bf16[1,1,2,64,5120]{4,3,2,1,0:T(8,128)(2,1)} %param.4) | copy-start | bytes 3932164
  2.0 14.5 %copy-start.3 = (f32[1,2,4,5120]{3,2,1,0:T(4,128)S(1)}, f32[1,2,4,5120]{3,2,1,0:T(4,128)}, u32[]{:S(2)}) copy-start(f32[1,2,4,5120]{3,2,1,0:T(4,128)} %momentum_ref.3) | copy-start | bytes 491524
  2.5 15.1 %collective-permute-start = (f32[4,8,5120]{2,1,0:T(8,128)S(1)}, f32[4,8,5120]{2,1,0:T(8,128)S(1)}, u32[]{:S(2)}, u32[]{:S(2)}) collective-permute-start(f32[4,8,5120]{2,1,0:T(8,128)S(1)} %get-tuple-element.16), channel_id=1, source_target_pairs={{0,1},{1,0},{2,3},{3,2},{4,5},{5,4},{6,7},{7,6},{8,9},{9,8},{10,11... | collective-permute-start | bytes 1966088 | tf_op jit(solution)/shard_map/ppermute | solution.py:231
  7.4 17.8 %collective-permute-start.2 = (f32[2,4,8,640]{3,2,1,0:T(8,128)S(1)}, f32[2,4,8,640]{3,2,1,0:T(8,128)S(1)}, u32[]{:S(2)}, u32[]{:S(2)}) collective-permute-start(f32[2,4,8,640]{3,2,1,0:T(8,128)S(1)} %get-tuple-element.17), channel_id=1, source_target_pairs={{0,4},{1,5},{2,6},{3,7},{4,0},{5,1},{6,2},{7,3},{8,12},{9,13},{10,... | collective-permute-start | bytes 491528 | tf_op jit(solution)/shard_map/ppermute | solution.py:231
  17.7 19.8 %collective-permute-start.1 = (f32[4,8,5120]{2,1,0:T(8,128)S(1)}, f32[4,8,5120]{2,1,0:T(8,128)S(1)}, u32[]{:S(2)}, u32[]{:S(2)}) collective-permute-start(f32[4,8,5120]{2,1,0:T(8,128)S(1)} %bitcast_add_fusion.1), channel_id=1, source_target_pairs={{0,3},{1,2},{2,1},{3,0},{4,7},{5,6},{6,5},{7,4},{8,11},{9,10},{10,... | collective-permute-start | bytes 1966088 | tf_op jit(solution)/shard_map/ppermute | solution.py:231
  21.8 18.8 %collective-permute-start.4 = (f32[4,8,5120]{2,1,0:T(8,128)S(1)}, f32[4,8,5120]{2,1,0:T(8,128)S(1)}, u32[]{:S(2)}, u32[]{:S(2)}) collective-permute-start(f32[4,8,5120]{2,1,0:T(8,128)S(1)} %get-tuple-element.25), channel_id=1, source_target_pairs={{0,1},{1,0},{2,3},{3,2},{4,5},{5,4},{6,7},{7,6},{8,9},{9,8},{10,11... | collective-permute-start | bytes 1966088 | tf_op jit(solution)/shard_map/ppermute | solution.py:231
  25.2 12.3 %collective-permute-start.3 = (f32[4,8,640]{2,1,0:T(8,128)S(1)}, f32[4,8,640]{2,1,0:T(8,128)S(1)}, u32[]{:S(2)}, u32[]{:S(2)}) collective-permute-start(f32[4,8,640]{2,1,0:T(8,128)S(1)} %fusion.3), channel_id=1, source_target_pairs={{0,12},{1,13},{2,14},{3,15},{4,8},{5,9},{6,10},{7,11},{8,4},{9,5},... | collective-permute-start | bytes 245768 | tf_op jit(solution)/shard_map/ppermute | solution.py:231
  40.7 35.3 %copy-start.2 = (f32[2,4,5120]{2,1,0:T(4,128)S(1)}, f32[2,4,5120]{2,1,0:T(4,128)}, u32[]{:S(2)}) copy-start(f32[2,4,5120]{2,1,0:T(4,128)} %params_ref.1) | copy-start | bytes 491524
  40.8 23.5 %collective-permute-start.5 = (f32[2,8,5120]{2,1,0:T(8,128)S(1)}, f32[2,8,5120]{2,1,0:T(8,128)S(1)}, u32[]{:S(2)}, u32[]{:S(2)}) collective-permute-start(f32[2,8,5120]{2,1,0:T(8,128)S(1)} %slice.47), channel_id=1, source_target_pairs={{0,4},{1,5},{2,6},{3,7},{4,0},{5,1},{6,2},{7,3},{8,12},{9,13},{10,... | collective-permute-start | bytes 983048 | tf_op jit(solution)/shard_map/ppermute | solution.py:231
  58.6 9.2 %all-to-all-start.1 = ((f32[4,8,640]{2,1,0:T(8,128)}), f32[4,8,640]{2,1,0:T(8,128)S(1)}, u32[]{:S(2)}, u32[]{:S(2)}) async-start(f32[4,8,640]{2,1,0:T(8,128)} %broadcast_in_dim.10), calls=%async_computation.1 | async-start | bytes 163840 | tf_op jit(solution)/shard_map/all_to_all | solution.py:243
  64.3 15.7 %collective-permute-start.6 = (f32[8,5120]{1,0:T(8,128)S(1)}, f32[8,5120]{1,0:T(8,128)S(1)}, u32[]{:S(2)}, u32[]{:S(2)}) collective-permute-start(f32[8,5120]{1,0:T(8,128)S(1)} %get-tuple-element.28), channel_id=1, source_target_pairs={{0,12},{1,13},{2,14},{3,15},{4,8},{5,9},{6,10},{7,11},{8,4},{9,5},... | collective-permute-start | bytes 491528 | tf_op jit(solution)/shard_map/ppermute | solution.py:231
